TPU v7x, 256 devices: a whole 4x4x8 slice. The times are simulated.
256 devices in a mesh: dp: 4 (over x), tensor: 4 (over y), expert: 16 (over z, core).
Axes of the slice: x: 4, y: 4, z: 8, core: 2. Of those that a mesh axis runs over, the one named last changes fastest.
Arguments:
- tokens: bfloat16 [8192, 5120], P(('dp', 'expert')), may hold values from -6 to 6
- expert_ids: int32 [8192, 1], P(('dp', 'expert')), may hold values from 0 to 15; in each aligned block of 128 rows (0 to 127, 128 to 255, ...) at most 10 rows name the same one
- norm_gain: float32 [5120], replicated, may hold values from 0.1 to 1.9
- router_weight: bfloat16 [5120, 16], replicated, may hold values from -0.078125 to 0.078125
- w_gate: bfloat16 [16, 5120, 6144], P(('dp', 'tensor'), None, 'expert'), may hold values from -0.15625 to 0.15625
- w_up: bfloat16 [16, 5120, 6144], P(('dp', 'tensor'), None, 'expert'), may hold values from -0.15625 to 0.15625
- w_down: bfloat16 [16, 6144, 5120], P(('dp', 'tensor'), 'expert'), may hold values from -0.078125 to 0.078125
Outputs:
- mixed: bfloat16 [8192, 5120], P(('dp', 'expert'))
Inputs may be any that keep to these rules, and one draw needn't show every extreme that they name: `expert_ids`: within each aligned block of 128 rows (one group) no expert is named more than 10 times; in every draw some expert is named exactly 10 times in some block.
All inputs are finite; a program needn't handle non-finite values.
Results may differ from a plain program's by a relative error of at most 0.03.
Values may be sent and summed in bfloat16 or wider, within the bound.
No kernel may reach another device: no remote copies, remote signals or barrier semaphores. Data moves between devices by JAX's collectives and lax.ppermute only.
A program may use at most 128 MiB of HBM per device.

v0:
```python
import functools

import jax
import jax.numpy as jnp
from jax import lax
from jax.experimental import pallas as pl
from jax.experimental.pallas import tpu as pltpu
from jax.sharding import PartitionSpec as P

BF16 = jnp.bfloat16
F32 = jnp.float32


def normalize(values, gain):
    widened = values.astype(F32)
    mean_square = jnp.mean(widened * widened, axis=-1, keepdims=True)
    return (widened * lax.rsqrt(mean_square + 1e-05) * gain).astype(BF16)


def add(*terms):
    total = terms[0].astype(F32)
    for term in terms[1:]:
        total = total + term.astype(F32)
    return total.astype(BF16)


def select_rows(row_of, row_count, values):
    picks = row_of[None, :] == jnp.arange(row_count, dtype=jnp.int32)[:, None]
    return jnp.dot(picks.astype(BF16), values, preferred_element_type=F32)


def shift(values, axis, steps):
    size = lax.axis_size(axis)
    return lax.ppermute(values, axis, [(i, (i + steps) % size) for i in range(size)])


def ring_step(values):
    size = lax.axis_size("expert")
    pairs = [(i, (i + (2 if i % 2 == 0 else -2)) % size) for i in range(size)]
    return lax.ppermute(values, "expert", pairs)


def swap(values):
    size = lax.axis_size("expert")
    return lax.ppermute(values, "expert", [(i, i ^ 1) for i in range(size)])


def expert_kernel(groups, step, *refs):
    count = sum(groups)
    pieces, (gate, up, down), outs = refs[:count], refs[count : count + 3], refs[count + 3 : -2]
    acts, hidden = refs[-2:]
    features, units = gate.shape
    acts[...] = jnp.zeros_like(acts)

    @pl.loop(0, features // step)
    def _(i):
        cols = pl.ds(pl.multiple_of(i * step, step), step)
        rows = jnp.concatenate([piece[:, cols].astype(F32) for piece in pieces], axis=0)
        weights = jnp.concatenate([gate[cols, :], up[cols, :]], axis=1)
        acts[...] += jnp.dot(rows.astype(BF16), weights, preferred_element_type=F32)

    gate_act, up_act = acts[:, :units], acts[:, units:]
    hidden[...] = (gate_act / (1.0 + jnp.exp(-gate_act)) * up_act).astype(BF16)

    @pl.loop(0, features // step)
    def _(i):
        cols = pl.ds(pl.multiple_of(i * step, step), step)
        product = jnp.dot(hidden[...], down[:, cols], preferred_element_type=F32)
        first = 0
        for out in outs:
            out[:, cols] = product[first : first + out.shape[0]].astype(BF16)
            first += out.shape[0]


def expert_apply(groups, pieces, gate, up, down):
    rows, features = pieces[0].shape
    total = rows * sum(groups)
    units = gate.shape[1]
    operands = [pltpu.with_memory_space_constraint(x, pltpu.VMEM) for x in (*pieces, gate, up, down)]
    return pl.pallas_call(
        functools.partial(expert_kernel, groups, 1024),
        out_shape=[pltpu.VMEM((rows * n, features), BF16) for n in groups],
        in_specs=[pl.BlockSpec(memory_space=pltpu.VMEM)] * len(operands),
        out_specs=[pl.BlockSpec(memory_space=pltpu.VMEM)] * len(groups),
        scratch_shapes=[pltpu.VMEM((total, 2 * units), F32), pltpu.VMEM((total, units), BF16)],
        compiler_params=pltpu.CompilerParams(vmem_limit_bytes=8 << 20),
        cost_estimate=pl.CostEstimate(
            flops=6 * total * features * units,
            bytes_accessed=6 * features * units + 4 * total * features,
            transcendentals=total * units,
        ),
    )(*operands)


def per_device(tokens, expert_ids, norm_gain, router_weight, w_gate, w_up, w_down):
    dp_size = lax.axis_size("dp")
    tensor_size = lax.axis_size("tensor")
    chips = lax.axis_size("expert") // 2
    half = chips // 2
    token_count = tokens.shape[0]
    expert_count = dp_size * tensor_size
    capacity = 5 * token_count // (4 * expert_count)
    rows = dp_size * capacity
    my_dp = lax.axis_index("dp")
    my_tensor = lax.axis_index("tensor")
    gate, up, down = w_gate[0], w_up[0], w_down[0]

    normed = normalize(tokens, norm_gain)
    expert_of = expert_ids[:, 0]
    one_hot = expert_of[:, None] == jnp.arange(expert_count, dtype=jnp.int32)[None, :]
    logits = jnp.dot(normed, router_weight, preferred_element_type=F32)
    chosen_logit = jnp.sum(jnp.where(one_hot, logits, 0.0), axis=1)
    routed = (normed.astype(F32) * jax.nn.sigmoid(chosen_logit)[:, None]).astype(BF16)
    order = jnp.arange(token_count, dtype=jnp.int32)
    earlier = (expert_of[:, None] == expert_of[None, :]) & (order[:, None] < order[None, :])
    slot_index = jnp.sum(earlier.astype(jnp.int32), axis=0)
    ahead_dp = (expert_of // tensor_size - my_dp) % dp_size
    ahead_tensor = (expert_of % tensor_size - my_tensor) % tensor_size
    row_of = ahead_tensor * rows + ahead_dp * capacity + slot_index

    outgoing = select_rows(row_of, rows, routed).astype(BF16)
    arrived = [outgoing[:capacity]]
    for j in range(1, dp_size):
        arrived.append(shift(outgoing[j * capacity : (j + 1) * capacity], "dp", j))
    mine = jnp.concatenate(arrived, axis=0)

    apply = functools.partial(expert_apply, gate=gate, up=up, down=down)
    other = swap(mine)
    own_part, other_part = apply((1, 1), [mine, other])
    far, near = ring_step(mine), ring_step(other)
    near, own_part = lax.optimization_barrier((near, own_part))
    parts = []
    for k in range(1, half):
        part = apply((2, 1, 1), [far, near, swap(far), swap(near)])
        far = ring_step(far)
        if k < half - 1:
            near = ring_step(near)
            near, part = lax.optimization_barrier((near, part))
        parts.append(part)
    last_kept, last_sent = apply((1, 1), [far, swap(far)])

    near_sum, far_sum = None, None
    for k in range(half - 1, 0, -1):
        sent, near_part, far_part = parts[k - 1]
        theirs = swap(sent)
        if near_sum is None:
            near_sum = ring_step(add(near_part, theirs[:rows]))
            far_sum = ring_step(add(last_kept, swap(last_sent)))
        else:
            near_sum = ring_step(add(near_sum, near_part, theirs[:rows]))
        far_sum = ring_step(add(far_sum, far_part, theirs[rows:]))
    slot_out = add(far_sum, own_part, swap(add(near_sum, other_part)))

    returned = [slot_out[:capacity]]
    for j in range(1, dp_size):
        returned.append(shift(slot_out[j * capacity : (j + 1) * capacity], "dp", -j))
    here = jnp.concatenate(returned, axis=0)
    ahead = shift(here, "tensor", -1)
    behind = shift(here, "tensor", 1)
    cut = rows // 16 * 8
    opposite = jnp.concatenate(
        [shift(ahead[:cut], "tensor", -1), shift(behind[cut:], "tensor", 1)], axis=0
    )
    held = jnp.concatenate([here, ahead, opposite, behind], axis=0)
    picks = row_of[:, None] == jnp.arange(tensor_size * rows, dtype=jnp.int32)[None, :]
    return jnp.dot(picks.astype(BF16), held, preferred_element_type=F32).astype(BF16)


def solution(mesh):
    return jax.shard_map(
        per_device,
        mesh=mesh,
        in_specs=(
            P(("dp", "expert"), None),
            P(("dp", "expert"), None),
            P(),
            P(),
            P(("dp", "tensor"), None, "expert"),
            P(("dp", "tensor"), None, "expert"),
            P(("dp", "tensor"), "expert", None),
        ),
        out_specs=P(("dp", "expert"), None),
        check_vma=False,
    )
```

profile of v0, /device:TPU:6, one launch (start us, length us, event | category | flops | bytes accessed | tf_op | source)
XLA Modules:
  0.0 152.6 jit_solution(16158528076402906525)
XLA Ops:
  0.0 1.8 %fusion = f32[128]{0:T(128)S(1)} fusion(bf16[128,5120]{1,0:T(8,128)(2,1)} %param.7), kind=kLoop, calls=%fused_computation.4 | loop fusion | flops 1965952 | bytes 1311232 | tf_op jit(solution)/shard_map/reduce_sum | solution.py:16
  2.6 1.9 %fusion.4 = f32[128]{0:T(128)S(1)} fusion(bf16[5120,16]{0,1:T(8,128)(2,1)S(1)} %copy-done, bf16[128,5120]{1,0:T(8,128)(2,1)} %param.7, f32[5120]{0:T(1024)} %param.9, f32[128]{0:T(128)S(1)} %add_rsqrt_fusion, s32[128]{0:T(128)} %bitcast.29), kind=kOutput, calls=%fused_computation.10 | convolution fusion | flops 23598976 | bytes 1496576 | tf_op jit(solution)/shard_map/dot_general | solution.py:111
  6.3 2.8 %collective-permute-start.1 = (bf16[10,5120]{1,0:T(8,128)(2,1)S(1)}, bf16[10,5120]{1,0:T(8,128)(2,1)S(1)}, u32[]{:S(2)}, u32[]{:S(2)}) collective-permute-start(bf16[10,5120]{1,0:T(8,128)(2,1)S(1)} %get-tuple-element.63), channel_id=1, source_target_pairs={{0,128},{64,192},{128,0},{192,64},{1,129},{65,193},{129,1},{193,65... | collective-permute-start | bytes 307208 | tf_op jit(solution)/shard_map/ppermute | solution.py:34
  9.5 6.6 %collective-permute-done.2 = bf16[10,5120]{1,0:T(8,128)(2,1)S(1)} collective-permute-done((bf16[10,5120]{1,0:T(8,128)(2,1)S(1)}, bf16[10,5120]{1,0:T(8,128)(2,1)S(1)}, u32[]{:S(2)}, u32[]{:S(2)}) %collective-permute-start.2) | collective-permute-done | bytes 102432 | tf_op jit(solution)/shard_map/ppermute | solution.py:34
  16.9 2.0 %collective-permute-start.3 = (bf16[40,5120]{1,0:T(8,128)(2,1)S(1)}, bf16[40,5120]{1,0:T(8,128)(2,1)S(1)}, u32[]{:S(2)}, u32[]{:S(2)}) collective-permute-start(bf16[40,5120]{1,0:T(8,128)(2,1)S(1)} %pad_maximum_fusion.refs_0_), channel_id=1, source_target_pairs={{0,2},{1,15},{2,4},{3,1},{4,6},{5,3},{6,8},{7,5},{8,10},{9,7},{10,... | collective-permute-start | bytes 1228808 | tf_op jit(solution)/shard_map/ppermute | solution.py:40
  18.9 2.6 %collective-permute-start.10 = (bf16[40,5120]{1,0:T(8,128)(2,1)S(1)}, bf16[40,5120]{1,0:T(8,128)(2,1)S(1)}, u32[]{:S(2)}, u32[]{:S(2)}) collective-permute-start(bf16[40,5120]{1,0:T(8,128)(2,1)S(1)} %pad_maximum_fusion.refs_0_), channel_id=1, source_target_pairs={{0,1},{1,0},{2,3},{3,2},{4,5},{5,4},{6,7},{7,6},{8,9},{9,8},{10,11... | collective-permute-start | bytes 1228808 | tf_op jit(solution)/shard_map/ppermute | solution.py:45
  21.5 7.2 %collective-permute-done.3.refs_0_ = bf16[40,5120]{1,0:T(8,128)(2,1)S(1)} collective-permute-done((bf16[40,5120]{1,0:T(8,128)(2,1)S(1)}, bf16[40,5120]{1,0:T(8,128)(2,1)S(1)}, u32[]{:S(2)}, u32[]{:S(2)}) %collective-permute-start.3) | collective-permute-done | bytes 409632 | tf_op jit(solution)/shard_map/ppermute | solution.py:40
  29.6 2.1 %copy-done.2 = bf16[1,5120,384]{2,1,0:T(8,128)(2,1)S(1)} copy-done((bf16[1,5120,384]{2,1,0:T(8,128)(2,1)S(1)}, bf16[1,5120,384]{2,1,0:T(8,128)(2,1)}, u32[]{:S(2)}) %copy-start.2) | copy-done | bytes 3932184
  31.7 2.1 %copy-done.3 = bf16[1,384,5120]{2,1,0:T(8,128)(2,1)S(1)} copy-done((bf16[1,384,5120]{2,1,0:T(8,128)(2,1)S(1)}, bf16[1,384,5120]{2,1,0:T(8,128)(2,1)}, u32[]{:S(2)}) %copy-start.3) | copy-done | bytes 3932184
  33.8 3.4 %shard_map.74 = (bf16[40,5120]{1,0:T(8,128)(2,1)S(1)}, bf16[40,5120]{1,0:T(8,128)(2,1)S(1)}) custom-call(bf16[40,5120]{1,0:T(8,128)(2,1)S(1)} %pad_maximum_fusion.refs_0_, bf16[40,5120]{1,0:T(8,128)(2,1)S(1)} %collective-permute-done.10.refs_1_, bf16[5120,384]{1,0:T(8,128)(2,1)S(1)} %bitcast.13, bf16[5120,384]{1,0:T(8,128)(2,1)S(1)} %bitcast.18, ...), custom_call_target="tpu_custom_call" | custom-call | flops 943718400 | bytes 13434880 | tf_op jit(solution)/shard_map/pallas_call | solution.py:80
  39.1 3.2 %collective-permute-done.11.refs_1_ = bf16[40,5120]{1,0:T(8,128)(2,1)S(1)} collective-permute-done((bf16[40,5120]{1,0:T(8,128)(2,1)S(1)}, bf16[40,5120]{1,0:T(8,128)(2,1)S(1)}, u32[]{:S(2)}, u32[]{:S(2)}) %collective-permute-start.11) | collective-permute-done | bytes 409632 | tf_op jit(solution)/shard_map/ppermute | solution.py:40
  43.4 3.7 %collective-permute-done.5.refs_0_ = bf16[40,5120]{1,0:T(8,128)(2,1)S(1)} collective-permute-done((bf16[40,5120]{1,0:T(8,128)(2,1)S(1)}, bf16[40,5120]{1,0:T(8,128)(2,1)S(1)}, u32[]{:S(2)}, u32[]{:S(2)}) %collective-permute-start.5) | collective-permute-done | bytes 409632 | tf_op jit(solution)/shard_map/ppermute | solution.py:40
  48.3 4.0 %shard_map.75 = (bf16[80,5120]{1,0:T(8,128)(2,1)S(1)}, bf16[40,5120]{1,0:T(8,128)(2,1)S(1)}, bf16[40,5120]{1,0:T(8,128)(2,1)S(1)}) custom-call(bf16[40,5120]{1,0:T(8,128)(2,1)S(1)} %collective-permute-done.3.refs_0_, bf16[40,5120]{1,0:T(8,128)(2,1)S(1)} %collective-permute-done.11.refs_1_, bf16[40,5120]{1,0:T(8,128)(2,1)S(1)} %collective-permute-done.13.refs_2_, ...), custom_call_target="tpu_custom_call" | custom-call | flops 1887436800 | bytes 15073280 | tf_op jit(solution)/shard_map/pallas_call | solution.py:80
  52.3 2.7 %collective-permute-start.15 = (bf16[40,5120]{1,0:T(8,128)(2,1)S(1)}, bf16[40,5120]{1,0:T(8,128)(2,1)S(1)}, u32[]{:S(2)}, u32[]{:S(2)}) collective-permute-start(bf16[40,5120]{1,0:T(8,128)(2,1)S(1)} %collective-permute-done.12.refs_1_), channel_id=1, source_target_pairs={{0,2},{1,15},{2,4},{3,1},{4,6},{5,3},{6,8},{7,5},{8,10},{9,7},{10,... | collective-permute-start | bytes 1228808 | tf_op jit(solution)/shard_map/ppermute | solution.py:40
  56.8 4.0 %shard_map.76 = (bf16[80,5120]{1,0:T(8,128)(2,1)S(1)}, bf16[40,5120]{1,0:T(8,128)(2,1)S(1)}, bf16[40,5120]{1,0:T(8,128)(2,1)S(1)}) custom-call(bf16[40,5120]{1,0:T(8,128)(2,1)S(1)} %collective-permute-done.4.refs_0_, bf16[40,5120]{1,0:T(8,128)(2,1)S(1)} %collective-permute-done.12.refs_1_, bf16[40,5120]{1,0:T(8,128)(2,1)S(1)} %collective-permute-done.16.refs_2_, ...), custom_call_target="tpu_custom_call" | custom-call | flops 1887436800 | bytes 15073280 | tf_op jit(solution)/shard_map/pallas_call | solution.py:80
  61.8 3.4 %shard_map.73 = (bf16[40,5120]{1,0:T(8,128)(2,1)S(1)}, bf16[40,5120]{1,0:T(8,128)(2,1)S(1)}) custom-call(bf16[40,5120]{1,0:T(8,128)(2,1)S(1)} %collective-permute-done.6.refs_0_, bf16[40,5120]{1,0:T(8,128)(2,1)S(1)} %collective-permute-done.7.refs_1_, bf16[5120,384]{1,0:T(8,128)(2,1)S(1)} %bitcast.16, bf16[5120,384]{1,0:T(8,128)(2,1)S(1)} %bitcast.21, ...), custom_call_target="tpu_custom_call" | custom-call | flops 943718400 | bytes 13434880 | tf_op jit(solution)/shard_map/pallas_call | solution.py:80
  65.8 4.0 %shard_map.77 = (bf16[80,5120]{1,0:T(8,128)(2,1)S(1)}, bf16[40,5120]{1,0:T(8,128)(2,1)S(1)}, bf16[40,5120]{1,0:T(8,128)(2,1)S(1)}) custom-call(bf16[40,5120]{1,0:T(8,128)(2,1)S(1)} %collective-permute-done.5.refs_0_, bf16[40,5120]{1,0:T(8,128)(2,1)S(1)} %collective-permute-done.15.refs_1_, bf16[40,5120]{1,0:T(8,128)(2,1)S(1)} %collective-permute-done.18.refs_2_, ...), custom_call_target="tpu_custom_call" | custom-call | flops 1887436800 | bytes 15073280 | tf_op jit(solution)/shard_map/pallas_call | solution.py:80
  71.3 7.9 %collective-permute-done.9 = bf16[40,5120]{1,0:T(8,128)(2,1)S(1)} collective-permute-done((bf16[40,5120]{1,0:T(8,128)(2,1)S(1)}, bf16[40,5120]{1,0:T(8,128)(2,1)S(1)}, u32[]{:S(2)}, u32[]{:S(2)}) %collective-permute-start.9) | collective-permute-done | bytes 409632 | tf_op jit(solution)/shard_map/ppermute | solution.py:40
  80.7 8.0 %collective-permute-done.21 = bf16[40,5120]{1,0:T(8,128)(2,1)S(1)} collective-permute-done((bf16[40,5120]{1,0:T(8,128)(2,1)S(1)}, bf16[40,5120]{1,0:T(8,128)(2,1)S(1)}, u32[]{:S(2)}, u32[]{:S(2)}) %collective-permute-start.21) | collective-permute-done | bytes 409632 | tf_op jit(solution)/shard_map/ppermute | solution.py:40
  88.7 4.4 %collective-permute-done.26 = bf16[40,5120]{1,0:T(8,128)(2,1)S(1)} collective-permute-done((bf16[40,5120]{1,0:T(8,128)(2,1)S(1)}, bf16[40,5120]{1,0:T(8,128)(2,1)S(1)}, u32[]{:S(2)}, u32[]{:S(2)}) %collective-permute-start.26) | collective-permute-done | bytes 409632 | tf_op jit(solution)/shard_map/ppermute | solution.py:40
  93.6 9.0 %collective-permute-done.23 = bf16[40,5120]{1,0:T(8,128)(2,1)S(1)} collective-permute-done((bf16[40,5120]{1,0:T(8,128)(2,1)S(1)}, bf16[40,5120]{1,0:T(8,128)(2,1)S(1)}, u32[]{:S(2)}, u32[]{:S(2)}) %collective-permute-start.23) | collective-permute-done | bytes 409632 | tf_op jit(solution)/shard_map/ppermute | solution.py:40
  102.6 4.4 %collective-permute-done.27 = bf16[40,5120]{1,0:T(8,128)(2,1)S(1)} collective-permute-done((bf16[40,5120]{1,0:T(8,128)(2,1)S(1)}, bf16[40,5120]{1,0:T(8,128)(2,1)S(1)}, u32[]{:S(2)}, u32[]{:S(2)}) %collective-permute-start.27) | collective-permute-done | bytes 409632 | tf_op jit(solution)/shard_map/ppermute | solution.py:40
  107.5 9.1 %collective-permute-done.28 = bf16[40,5120]{1,0:T(8,128)(2,1)S(1)} collective-permute-done((bf16[40,5120]{1,0:T(8,128)(2,1)S(1)}, bf16[40,5120]{1,0:T(8,128)(2,1)S(1)}, u32[]{:S(2)}, u32[]{:S(2)}) %collective-permute-start.28) | collective-permute-done | bytes 409632 | tf_op jit(solution)/shard_map/ppermute | solution.py:40
  117.0 4.0 %collective-permute-done.25 = bf16[40,5120]{1,0:T(8,128)(2,1)S(1)} collective-permute-done((bf16[40,5120]{1,0:T(8,128)(2,1)S(1)}, bf16[40,5120]{1,0:T(8,128)(2,1)S(1)}, u32[]{:S(2)}, u32[]{:S(2)}) %collective-permute-start.25) | collective-permute-done | bytes 409632 | tf_op jit(solution)/shard_map/ppermute | solution.py:40
  122.1 3.3 %collective-permute-start.31 = (bf16[10,5120]{1,0:T(8,128)(2,1)S(1)}, bf16[10,5120]{1,0:T(8,128)(2,1)S(1)}, u32[]{:S(2)}, u32[]{:S(2)}) collective-permute-start(bf16[10,5120]{1,0:T(8,128)(2,1)S(1)} %get-tuple-element.58), channel_id=1, source_target_pairs={{0,128},{64,192},{128,0},{192,64},{1,129},{65,193},{129,1},{193,65... | collective-permute-start | bytes 307208 | tf_op jit(solution)/shard_map/ppermute | solution.py:34
  125.4 3.7 %collective-permute-done.30 = bf16[10,5120]{1,0:T(8,128)(2,1)S(1)} collective-permute-done((bf16[10,5120]{1,0:T(8,128)(2,1)S(1)}, bf16[10,5120]{1,0:T(8,128)(2,1)S(1)}, u32[]{:S(2)}, u32[]{:S(2)}) %collective-permute-start.30) | collective-permute-done | bytes 102432 | tf_op jit(solution)/shard_map/ppermute | solution.py:34
  129.1 1.8 %collective-permute-done.31 = bf16[10,5120]{1,0:T(8,128)(2,1)S(1)} collective-permute-done((bf16[10,5120]{1,0:T(8,128)(2,1)S(1)}, bf16[10,5120]{1,0:T(8,128)(2,1)S(1)}, u32[]{:S(2)}, u32[]{:S(2)}) %collective-permute-start.31) | collective-permute-done | bytes 102432 | tf_op jit(solution)/shard_map/ppermute | solution.py:34
  132.7 1.7 %collective-permute-start.33 = (bf16[40,5120]{1,0:T(8,128)(2,1)S(1)}, bf16[40,5120]{1,0:T(8,128)(2,1)S(1)}, u32[]{:S(2)}, u32[]{:S(2)}) collective-permute-start(bf16[40,5120]{1,0:T(8,128)(2,1)S(1)} %pad_maximum_fusion.1), channel_id=1, source_target_pairs={{0,48},{16,0},{32,16},{48,32},{1,49},{17,1},{33,17},{49,33},{2,50}... | collective-permute-start | bytes 1228808 | tf_op jit(solution)/shard_map/ppermute | solution.py:34
  134.4 6.3 %collective-permute-done.35 = bf16[40,5120]{1,0:T(8,128)(2,1)S(1)} collective-permute-done((bf16[40,5120]{1,0:T(8,128)(2,1)S(1)}, bf16[40,5120]{1,0:T(8,128)(2,1)S(1)}, u32[]{:S(2)}, u32[]{:S(2)}) %collective-permute-start.35) | collective-permute-done | bytes 409632 | tf_op jit(solution)/shard_map/ppermute | solution.py:34
  142.3 1.8 %collective-permute-start.34 = (bf16[16,5120]{1,0:T(8,128)(2,1)S(1)}, bf16[16,5120]{1,0:T(8,128)(2,1)S(1)}, u32[]{:S(2)}, u32[]{:S(2)}) collective-permute-start(bf16[16,5120]{1,0:T(8,128)(2,1)S(1)} %slice.78), channel_id=1, source_target_pairs={{0,48},{16,0},{32,16},{48,32},{1,49},{17,1},{33,17},{49,33},{2,50}... | collective-permute-start | bytes 491528 | tf_op jit(solution)/shard_map/ppermute | solution.py:34
  144.1 3.6 %collective-permute-done.34 = bf16[16,5120]{1,0:T(8,128)(2,1)S(1)} collective-permute-done((bf16[16,5120]{1,0:T(8,128)(2,1)S(1)}, bf16[16,5120]{1,0:T(8,128)(2,1)S(1)}, u32[]{:S(2)}, u32[]{:S(2)}) %collective-permute-start.34) | collective-permute-done | bytes 163872 | tf_op jit(solution)/shard_map/ppermute | solution.py:34
  148.4 2.6 %concatenate.12 = bf16[160,5120]{1,0:T(8,128)(2,1)S(1)} concatenate(bf16[10,5120]{1,0:T(8,128)(2,1)S(1)} %get-tuple-element.60, bf16[10,5120]{1,0:T(8,128)(2,1)S(1)} %collective-permute-done.30, bf16[10,5120]{1,0:T(8,128)(2,1)S(1)} %collective-permute-done.31, bf16[10,5120]{1,0:T(8,128)(2,1)S(1)} %collective-permute-done.32, bf16[40,5120]{1,0:T(8,128)(2,1)S(1)} %collective-permute-done.33, ...), dimensions={0} | concatenate | bytes 3276800 | tf_op jit(solution)/shard_map/concatenate | solution.py:164
  (85 shorter events, 23.2 us)
Async XLA Ops:
  5.4 10.7 %collective-permute-start.2 = (bf16[10,5120]{1,0:T(8,128)(2,1)S(1)}, bf16[10,5120]{1,0:T(8,128)(2,1)S(1)}, u32[]{:S(2)}, u32[]{:S(2)}) collective-permute-start(bf16[10,5120]{1,0:T(8,128)(2,1)S(1)} %get-tuple-element.62), channel_id=1, source_target_pairs={{0,192},{64,0},{128,64},{192,128},{1,193},{65,1},{129,65},{193,129... | collective-permute-start | bytes 307208 | tf_op jit(solution)/shard_map/ppermute | solution.py:34
  6.3 9.8 %collective-permute-start.1 = (bf16[10,5120]{1,0:T(8,128)(2,1)S(1)}, bf16[10,5120]{1,0:T(8,128)(2,1)S(1)}, u32[]{:S(2)}, u32[]{:S(2)}) collective-permute-start(bf16[10,5120]{1,0:T(8,128)(2,1)S(1)} %get-tuple-element.63), channel_id=1, source_target_pairs={{0,128},{64,192},{128,0},{192,64},{1,129},{65,193},{129,1},{193,65... | collective-permute-start | bytes 307208 | tf_op jit(solution)/shard_map/ppermute | solution.py:34
  9.1 7.6 %collective-permute-start = (bf16[10,5120]{1,0:T(8,128)(2,1)S(1)}, bf16[10,5120]{1,0:T(8,128)(2,1)S(1)}, u32[]{:S(2)}, u32[]{:S(2)}) collective-permute-start(bf16[10,5120]{1,0:T(8,128)(2,1)S(1)} %get-tuple-element.64), channel_id=1, source_target_pairs={{0,64},{64,128},{128,192},{192,0},{1,65},{65,129},{129,193},{193,1... | collective-permute-start | bytes 307208 | tf_op jit(solution)/shard_map/ppermute | solution.py:34
  16.9 11.9 %collective-permute-start.3 = (bf16[40,5120]{1,0:T(8,128)(2,1)S(1)}, bf16[40,5120]{1,0:T(8,128)(2,1)S(1)}, u32[]{:S(2)}, u32[]{:S(2)}) collective-permute-start(bf16[40,5120]{1,0:T(8,128)(2,1)S(1)} %pad_maximum_fusion.refs_0_), channel_id=1, source_target_pairs={{0,2},{1,15},{2,4},{3,1},{4,6},{5,3},{6,8},{7,5},{8,10},{9,7},{10,... | collective-permute-start | bytes 1228808 | tf_op jit(solution)/shard_map/ppermute | solution.py:40
  18.9 9.9 %collective-permute-start.10 = (bf16[40,5120]{1,0:T(8,128)(2,1)S(1)}, bf16[40,5120]{1,0:T(8,128)(2,1)S(1)}, u32[]{:S(2)}, u32[]{:S(2)}) collective-permute-start(bf16[40,5120]{1,0:T(8,128)(2,1)S(1)} %pad_maximum_fusion.refs_0_), channel_id=1, source_target_pairs={{0,1},{1,0},{2,3},{3,2},{4,5},{5,4},{6,7},{7,6},{8,9},{9,8},{10,11... | collective-permute-start | bytes 1228808 | tf_op jit(solution)/shard_map/ppermute | solution.py:45
  28.8 9.2 %collective-permute-start.4 = (bf16[40,5120]{1,0:T(8,128)(2,1)S(1)}, bf16[40,5120]{1,0:T(8,128)(2,1)S(1)}, u32[]{:S(2)}, u32[]{:S(2)}) collective-permute-start(bf16[40,5120]{1,0:T(8,128)(2,1)S(1)} %collective-permute-done.3.refs_0_), channel_id=1, source_target_pairs={{0,2},{1,15},{2,4},{3,1},{4,6},{5,3},{6,8},{7,5},{8,10},{9,7},{10,... | collective-permute-start | bytes 1228808 | tf_op jit(solution)/shard_map/ppermute | solution.py:40
  28.8 13.5 %collective-permute-start.11 = (bf16[40,5120]{1,0:T(8,128)(2,1)S(1)}, bf16[40,5120]{1,0:T(8,128)(2,1)S(1)}, u32[]{:S(2)}, u32[]{:S(2)}) collective-permute-start(bf16[40,5120]{1,0:T(8,128)(2,1)S(1)} %collective-permute-done.10.refs_1_), channel_id=1, source_target_pairs={{0,2},{1,15},{2,4},{3,1},{4,6},{5,3},{6,8},{7,5},{8,10},{9,7},{10,... | collective-permute-start | bytes 1228808 | tf_op jit(solution)/shard_map/ppermute | solution.py:40
  28.8 19.5 %collective-permute-start.13 = (bf16[40,5120]{1,0:T(8,128)(2,1)S(1)}, bf16[40,5120]{1,0:T(8,128)(2,1)S(1)}, u32[]{:S(2)}, u32[]{:S(2)}) collective-permute-start(bf16[40,5120]{1,0:T(8,128)(2,1)S(1)} %collective-permute-done.3.refs_0_), channel_id=1, source_target_pairs={{0,1},{1,0},{2,3},{3,2},{4,5},{5,4},{6,7},{7,6},{8,9},{9,8},{10,11... | collective-permute-start | bytes 1228808 | tf_op jit(solution)/shard_map/ppermute | solution.py:45
  37.9 9.2 %collective-permute-start.5 = (bf16[40,5120]{1,0:T(8,128)(2,1)S(1)}, bf16[40,5120]{1,0:T(8,128)(2,1)S(1)}, u32[]{:S(2)}, u32[]{:S(2)}) collective-permute-start(bf16[40,5120]{1,0:T(8,128)(2,1)S(1)} %collective-permute-done.4.refs_0_), channel_id=1, source_target_pairs={{0,2},{1,15},{2,4},{3,1},{4,6},{5,3},{6,8},{7,5},{8,10},{9,7},{10,... | collective-permute-start | bytes 1228808 | tf_op jit(solution)/shard_map/ppermute | solution.py:40
  42.3 5.9 %collective-permute-start.14 = (bf16[40,5120]{1,0:T(8,128)(2,1)S(1)}, bf16[40,5120]{1,0:T(8,128)(2,1)S(1)}, u32[]{:S(2)}, u32[]{:S(2)}) collective-permute-start(bf16[40,5120]{1,0:T(8,128)(2,1)S(1)} %collective-permute-done.11.refs_1_), channel_id=1, source_target_pairs={{0,1},{1,0},{2,3},{3,2},{4,5},{5,4},{6,7},{7,6},{8,9},{9,8},{10,11... | collective-permute-start | bytes 1228808 | tf_op jit(solution)/shard_map/ppermute | solution.py:45
  42.3 9.9 %collective-permute-start.12 = (bf16[40,5120]{1,0:T(8,128)(2,1)S(1)}, bf16[40,5120]{1,0:T(8,128)(2,1)S(1)}, u32[]{:S(2)}, u32[]{:S(2)}) collective-permute-start(bf16[40,5120]{1,0:T(8,128)(2,1)S(1)} %collective-permute-done.11.refs_1_), channel_id=1, source_target_pairs={{0,2},{1,15},{2,4},{3,1},{4,6},{5,3},{6,8},{7,5},{8,10},{9,7},{10,... | collective-permute-start | bytes 1228808 | tf_op jit(solution)/shard_map/ppermute | solution.py:40
  42.8 14.0 %collective-permute-start.16 = (bf16[40,5120]{1,0:T(8,128)(2,1)S(1)}, bf16[40,5120]{1,0:T(8,128)(2,1)S(1)}, u32[]{:S(2)}, u32[]{:S(2)}) collective-permute-start(bf16[40,5120]{1,0:T(8,128)(2,1)S(1)} %collective-permute-done.4.refs_0_), channel_id=1, source_target_pairs={{0,1},{1,0},{2,3},{3,2},{4,5},{5,4},{6,7},{7,6},{8,9},{9,8},{10,11... | collective-permute-start | bytes 1228808 | tf_op jit(solution)/shard_map/ppermute | solution.py:45
  47.1 9.2 %collective-permute-start.6 = (bf16[40,5120]{1,0:T(8,128)(2,1)S(1)}, bf16[40,5120]{1,0:T(8,128)(2,1)S(1)}, u32[]{:S(2)}, u32[]{:S(2)}) collective-permute-start(bf16[40,5120]{1,0:T(8,128)(2,1)S(1)} %collective-permute-done.5.refs_0_), channel_id=1, source_target_pairs={{0,2},{1,15},{2,4},{3,1},{4,6},{5,3},{6,8},{7,5},{8,10},{9,7},{10,... | collective-permute-start | bytes 1228808 | tf_op jit(solution)/shard_map/ppermute | solution.py:40
  52.3 9.4 %collective-permute-start.15 = (bf16[40,5120]{1,0:T(8,128)(2,1)S(1)}, bf16[40,5120]{1,0:T(8,128)(2,1)S(1)}, u32[]{:S(2)}, u32[]{:S(2)}) collective-permute-start(bf16[40,5120]{1,0:T(8,128)(2,1)S(1)} %collective-permute-done.12.refs_1_), channel_id=1, source_target_pairs={{0,2},{1,15},{2,4},{3,1},{4,6},{5,3},{6,8},{7,5},{8,10},{9,7},{10,... | collective-permute-start | bytes 1228808 | tf_op jit(solution)/shard_map/ppermute | solution.py:40
  56.3 5.5 %collective-permute-start.7 = (bf16[40,5120]{1,0:T(8,128)(2,1)S(1)}, bf16[40,5120]{1,0:T(8,128)(2,1)S(1)}, u32[]{:S(2)}, u32[]{:S(2)}) collective-permute-start(bf16[40,5120]{1,0:T(8,128)(2,1)S(1)} %collective-permute-done.6.refs_0_), channel_id=1, source_target_pairs={{0,1},{1,0},{2,3},{3,2},{4,5},{5,4},{6,7},{7,6},{8,9},{9,8},{10,11... | collective-permute-start | bytes 1228808 | tf_op jit(solution)/shard_map/ppermute | solution.py:45
  56.3 9.5 %collective-permute-start.18 = (bf16[40,5120]{1,0:T(8,128)(2,1)S(1)}, bf16[40,5120]{1,0:T(8,128)(2,1)S(1)}, u32[]{:S(2)}, u32[]{:S(2)}) collective-permute-start(bf16[40,5120]{1,0:T(8,128)(2,1)S(1)} %collective-permute-done.5.refs_0_), channel_id=1, source_target_pairs={{0,1},{1,0},{2,3},{3,2},{4,5},{5,4},{6,7},{7,6},{8,9},{9,8},{10,11... | collective-permute-start | bytes 1228808 | tf_op jit(solution)/shard_map/ppermute | solution.py:45
  69.8 9.5 %collective-permute-start.20 = (bf16[80,5120]{1,0:T(8,128)(2,1)S(1)}, bf16[80,5120]{1,0:T(8,128)(2,1)S(1)}, u32[]{:S(2)}, u32[]{:S(2)}) collective-permute-start(bf16[80,5120]{1,0:T(8,128)(2,1)S(1)} %get-tuple-element.41), channel_id=1, source_target_pairs={{0,1},{1,0},{2,3},{3,2},{4,5},{5,4},{6,7},{7,6},{8,9},{9,8},{10,11... | collective-permute-start | bytes 2457608 | tf_op jit(solution)/shard_map/ppermute | solution.py:45
  70.0 9.2 %collective-permute-start.9 = (bf16[40,5120]{1,0:T(8,128)(2,1)S(1)}, bf16[40,5120]{1,0:T(8,128)(2,1)S(1)}, u32[]{:S(2)}, u32[]{:S(2)}) collective-permute-start(bf16[40,5120]{1,0:T(8,128)(2,1)S(1)} %add_convert_fusion.8), channel_id=1, source_target_pairs={{0,2},{1,15},{2,4},{3,1},{4,6},{5,3},{6,8},{7,5},{8,10},{9,7},{10,... | collective-permute-start | bytes 1228808 | tf_op jit(solution)/shard_map/ppermute | solution.py:40
  71.3 9.4 %collective-permute-start.22 = (bf16[80,5120]{1,0:T(8,128)(2,1)S(1)}, bf16[80,5120]{1,0:T(8,128)(2,1)S(1)}, u32[]{:S(2)}, u32[]{:S(2)}) collective-permute-start(bf16[80,5120]{1,0:T(8,128)(2,1)S(1)} %get-tuple-element.43), channel_id=1, source_target_pairs={{0,1},{1,0},{2,3},{3,2},{4,5},{5,4},{6,7},{7,6},{8,9},{9,8},{10,11... | collective-permute-start | bytes 2457608 | tf_op jit(solution)/shard_map/ppermute | solution.py:45
  79.5 9.2 %collective-permute-start.21 = (bf16[40,5120]{1,0:T(8,128)(2,1)S(1)}, bf16[40,5120]{1,0:T(8,128)(2,1)S(1)}, u32[]{:S(2)}, u32[]{:S(2)}) collective-permute-start(bf16[40,5120]{1,0:T(8,128)(2,1)S(1)} %get-tuple-element.55), channel_id=1, source_target_pairs={{0,2},{1,15},{2,4},{3,1},{4,6},{5,3},{6,8},{7,5},{8,10},{9,7},{10,... | collective-permute-start | bytes 1228808 | tf_op jit(solution)/shard_map/ppermute | solution.py:40
  79.6 13.5 %collective-permute-start.26 = (bf16[40,5120]{1,0:T(8,128)(2,1)S(1)}, bf16[40,5120]{1,0:T(8,128)(2,1)S(1)}, u32[]{:S(2)}, u32[]{:S(2)}) collective-permute-start(bf16[40,5120]{1,0:T(8,128)(2,1)S(1)} %get-tuple-element.56), channel_id=1, source_target_pairs={{0,2},{1,15},{2,4},{3,1},{4,6},{5,3},{6,8},{7,5},{8,10},{9,7},{10,... | collective-permute-start | bytes 1228808 | tf_op jit(solution)/shard_map/ppermute | solution.py:40
  80.7 12.9 %collective-permute-start.24 = (bf16[80,5120]{1,0:T(8,128)(2,1)S(1)}, bf16[80,5120]{1,0:T(8,128)(2,1)S(1)}, u32[]{:S(2)}, u32[]{:S(2)}) collective-permute-start(bf16[80,5120]{1,0:T(8,128)(2,1)S(1)} %get-tuple-element.45), channel_id=1, source_target_pairs={{0,1},{1,0},{2,3},{3,2},{4,5},{5,4},{6,7},{7,6},{8,9},{9,8},{10,11... | collective-permute-start | bytes 2457608 | tf_op jit(solution)/shard_map/ppermute | solution.py:45
  93.4 9.2 %collective-permute-start.23 = (bf16[40,5120]{1,0:T(8,128)(2,1)S(1)}, bf16[40,5120]{1,0:T(8,128)(2,1)S(1)}, u32[]{:S(2)}, u32[]{:S(2)}) collective-permute-start(bf16[40,5120]{1,0:T(8,128)(2,1)S(1)} %get-tuple-element.53), channel_id=1, source_target_pairs={{0,2},{1,15},{2,4},{3,1},{4,6},{5,3},{6,8},{7,5},{8,10},{9,7},{10,... | collective-permute-start | bytes 1228808 | tf_op jit(solution)/shard_map/ppermute | solution.py:40
  93.5 13.5 %collective-permute-start.27 = (bf16[40,5120]{1,0:T(8,128)(2,1)S(1)}, bf16[40,5120]{1,0:T(8,128)(2,1)S(1)}, u32[]{:S(2)}, u32[]{:S(2)}) collective-permute-start(bf16[40,5120]{1,0:T(8,128)(2,1)S(1)} %get-tuple-element.54), channel_id=1, source_target_pairs={{0,2},{1,15},{2,4},{3,1},{4,6},{5,3},{6,8},{7,5},{8,10},{9,7},{10,... | collective-permute-start | bytes 1228808 | tf_op jit(solution)/shard_map/ppermute | solution.py:40
  107.3 9.2 %collective-permute-start.28 = (bf16[40,5120]{1,0:T(8,128)(2,1)S(1)}, bf16[40,5120]{1,0:T(8,128)(2,1)S(1)}, u32[]{:S(2)}, u32[]{:S(2)}) collective-permute-start(bf16[40,5120]{1,0:T(8,128)(2,1)S(1)} %get-tuple-element.52), channel_id=1, source_target_pairs={{0,2},{1,15},{2,4},{3,1},{4,6},{5,3},{6,8},{7,5},{8,10},{9,7},{10,... | collective-permute-start | bytes 1228808 | tf_op jit(solution)/shard_map/ppermute | solution.py:40
  107.4 13.5 %collective-permute-start.25 = (bf16[40,5120]{1,0:T(8,128)(2,1)S(1)}, bf16[40,5120]{1,0:T(8,128)(2,1)S(1)}, u32[]{:S(2)}, u32[]{:S(2)}) collective-permute-start(bf16[40,5120]{1,0:T(8,128)(2,1)S(1)} %get-tuple-element.51), channel_id=1, source_target_pairs={{0,2},{1,15},{2,4},{3,1},{4,6},{5,3},{6,8},{7,5},{8,10},{9,7},{10,... | collective-permute-start | bytes 1228808 | tf_op jit(solution)/shard_map/ppermute | solution.py:40
  121.2 7.9 %collective-permute-start.30 = (bf16[10,5120]{1,0:T(8,128)(2,1)S(1)}, bf16[10,5120]{1,0:T(8,128)(2,1)S(1)}, u32[]{:S(2)}, u32[]{:S(2)}) collective-permute-start(bf16[10,5120]{1,0:T(8,128)(2,1)S(1)} %get-tuple-element.59), channel_id=1, source_target_pairs={{0,192},{64,0},{128,64},{192,128},{1,193},{65,1},{129,65},{193,129... | collective-permute-start | bytes 307208 | tf_op jit(solution)/shard_map/ppermute | solution.py:34
  122.1 8.8 %collective-permute-start.31 = (bf16[10,5120]{1,0:T(8,128)(2,1)S(1)}, bf16[10,5120]{1,0:T(8,128)(2,1)S(1)}, u32[]{:S(2)}, u32[]{:S(2)}) collective-permute-start(bf16[10,5120]{1,0:T(8,128)(2,1)S(1)} %get-tuple-element.58), channel_id=1, source_target_pairs={{0,128},{64,192},{128,0},{192,64},{1,129},{65,193},{129,1},{193,65... | collective-permute-start | bytes 307208 | tf_op jit(solution)/shard_map/ppermute | solution.py:34
  125.4 5.5 %collective-permute-start.32 = (bf16[10,5120]{1,0:T(8,128)(2,1)S(1)}, bf16[10,5120]{1,0:T(8,128)(2,1)S(1)}, u32[]{:S(2)}, u32[]{:S(2)}) collective-permute-start(bf16[10,5120]{1,0:T(8,128)(2,1)S(1)} %get-tuple-element.57), channel_id=1, source_target_pairs={{0,64},{64,128},{128,192},{192,0},{1,65},{65,129},{129,193},{193,1... | collective-permute-start | bytes 307208 | tf_op jit(solution)/shard_map/ppermute | solution.py:34
  131.1 9.6 %collective-permute-start.35 = (bf16[40,5120]{1,0:T(8,128)(2,1)S(1)}, bf16[40,5120]{1,0:T(8,128)(2,1)S(1)}, u32[]{:S(2)}, u32[]{:S(2)}) collective-permute-start(bf16[40,5120]{1,0:T(8,128)(2,1)S(1)} %pad_maximum_fusion.1), channel_id=1, source_target_pairs={{0,16},{16,32},{32,48},{48,0},{1,17},{17,33},{33,49},{49,1},{2,18}... | collective-permute-start | bytes 1228808 | tf_op jit(solution)/shard_map/ppermute | solution.py:34
  132.7 9.6 %collective-permute-start.33 = (bf16[40,5120]{1,0:T(8,128)(2,1)S(1)}, bf16[40,5120]{1,0:T(8,128)(2,1)S(1)}, u32[]{:S(2)}, u32[]{:S(2)}) collective-permute-start(bf16[40,5120]{1,0:T(8,128)(2,1)S(1)} %pad_maximum_fusion.1), channel_id=1, source_target_pairs={{0,48},{16,0},{32,16},{48,32},{1,49},{17,1},{33,17},{49,33},{2,50}... | collective-permute-start | bytes 1228808 | tf_op jit(solution)/shard_map/ppermute | solution.py:34
  140.7 7.7 %collective-permute-start.36 = (bf16[24,5120]{1,0:T(8,128)(2,1)S(1)}, bf16[24,5120]{1,0:T(8,128)(2,1)S(1)}, u32[]{:S(2)}, u32[]{:S(2)}) collective-permute-start(bf16[24,5120]{1,0:T(8,128)(2,1)S(1)} %slice.79), channel_id=1, source_target_pairs={{0,16},{16,32},{32,48},{48,0},{1,17},{17,33},{33,49},{49,1},{2,18}... | collective-permute-start | bytes 737288 | tf_op jit(solution)/shard_map/ppermute | solution.py:34
  (13 other events, 69.1 us)
where the time goes:
time: 155 us; the launch traced here: 153 us
  waiting for transfers between devices  86.5 us (56%)
  starting transfers between devices  31 us (20%)
  Pallas kernels  18.7 us (12%)
  local copies, waits for them, and re-layouts  7.72 us (5%)
  other arithmetic  4.21 us (3%)
  matrix products  4.12 us (3%)
    ppermute x14, waiting for transfers between devices, ring_step(): return lax.ppermute(values, 'expert', pairs)  63.9 us
    ppermute x10, waiting for transfers between devices, shift(): lax.ppermute(values, axis, [(i, (i + steps) % size) for i in range(size)])  22.6 us
    pallas_call x5, Pallas kernels, expert_apply(): pl.pallas_call(functools.partial(expert_kernel, groups, 1024), out_shape=...  18.7 us
    ppermute x10, starting transfers between devices, shift(): lax.ppermute(values, axis, [(i, (i + steps) % size) for i in range(size)])  15 us
    ppermute x14, starting transfers between devices, ring_step(): return lax.ppermute(values, 'expert', pairs)  10.4 us
    ppermute x13, starting transfers between devices, swap(): return lax.ppermute(values, 'expert', [(i, i ^ 1) for i in range(size)])  5.6 us
    unnamed x16, local copies, waits for them, and re-layouts  4.92 us
  transfers between devices with their start and end apart: 37, of which 19 were waited for; matrix products, arithmetic and copies ran while one was open for 1% of the time, Pallas kernels for 12%

commit v1 on v0

v1 whole, which is shorter than its diff:
```python
import functools

import jax
import jax.numpy as jnp
from jax import lax
from jax.experimental import pallas as pl
from jax.experimental.pallas import tpu as pltpu
from jax.sharding import PartitionSpec as P

BF16 = jnp.bfloat16
F32 = jnp.float32
I32 = jnp.int32
LANES = 128
VMEM_LIMIT = 8 << 20


def in_vmem(values):
    return pltpu.with_memory_space_constraint(values, pltpu.VMEM)


def vmem_specs(count):
    return [pl.BlockSpec(memory_space=pltpu.VMEM)] * count


def step_of(size, most):
    return max(s for s in range(LANES, most + 1, LANES) if size % s == 0)


def add(*terms):
    total = terms[0].astype(F32)
    for term in terms[1:]:
        total = total + term.astype(F32)
    return total.astype(BF16)


def shift(values, axis, steps):
    size = lax.axis_size(axis)
    return lax.ppermute(values, axis, [(i, (i + steps) % size) for i in range(size)])


def ring_step(values):
    size = lax.axis_size("expert")
    pairs = [(i, (i + (2 if i % 2 == 0 else -2)) % size) for i in range(size)]
    return lax.ppermute(values, "expert", pairs)


def swap(values):
    size = lax.axis_size("expert")
    return lax.ppermute(values, "expert", [(i, i ^ 1) for i in range(size)])


def route_kernel(sizes, place, tokens, ids_col, ids_row, gain, router, row_of, *outs):
    dp_size, tensor_size, capacity = sizes
    blocks, normed = outs[:-1], outs[-1]
    count, features = tokens.shape
    step = step_of(features, 512)
    spans = [pl.ds(i, step) for i in range(0, features, step)]

    total = jnp.zeros((count, LANES), F32)
    for i in range(0, features, LANES):
        part = tokens[:, i : i + LANES].astype(F32)
        total = total + part * part
    scale = lax.rsqrt(jnp.sum(total, axis=1, keepdims=True) * (1.0 / features) + 1e-05)

    logits = jnp.zeros((count, router.shape[0]), F32)
    for cols in spans:
        part = (tokens[:, cols].astype(F32) * scale * gain[:, cols]).astype(BF16)
        normed[:, cols] = part
        logits = logits + lax.dot_general(
            part, router[:, cols], (((1,), (1,)), ((), ())), preferred_element_type=F32
        )
    expert = lax.broadcasted_iota(I32, logits.shape, 1)
    chosen = jnp.sum(jnp.where(ids_col[...] == expert, logits, 0.0), axis=1, keepdims=True)
    gate = 1.0 / (1.0 + jnp.exp(-chosen))

    down = lax.broadcasted_iota(I32, (count, count), 0)
    across = lax.broadcasted_iota(I32, (count, count), 1)
    same = ids_col[...] == ids_row[...]
    slot_col = jnp.sum(jnp.where(same & (across < down), 1, 0), axis=1, keepdims=True)
    slot_row = jnp.sum(jnp.where(same & (down < across), 1, 0), axis=0, keepdims=True)

    def ahead(ids):
        dp_of = jnp.zeros_like(ids)
        for d in range(1, dp_size):
            dp_of = dp_of + jnp.where(ids >= d * tensor_size, 1, 0)
        on_dp = dp_of - place[0]
        on_tensor = ids - dp_of * tensor_size - place[1]
        on_dp = jnp.where(on_dp < 0, on_dp + dp_size, on_dp)
        return on_dp, jnp.where(on_tensor < 0, on_tensor + tensor_size, on_tensor)

    on_dp, on_tensor = ahead(ids_col[...])
    row_of[...] = (on_tensor * dp_size + on_dp) * capacity + slot_col
    on_dp, on_tensor = ahead(ids_row[...])
    padded = -(-capacity // 16) * 16
    target = jnp.where(on_tensor == 0, on_dp * padded + slot_row, -1)
    row = lax.broadcasted_iota(I32, (dp_size * padded, count), 0)
    picks = jnp.where(row == target, 1.0, 0.0).astype(BF16)
    for cols in spans:
        routed = (normed[:, cols].astype(F32) * gate).astype(BF16)
        product = jnp.dot(picks, routed, preferred_element_type=F32)
        for j, block in enumerate(blocks):
            block[:, cols] = product[j * padded : j * padded + capacity].astype(BF16)


def route(sizes, place, tokens, expert_ids, norm_gain, router_weight):
    count, features = tokens.shape
    dp_size, _, capacity = sizes
    operands = (
        tokens,
        expert_ids,
        expert_ids.reshape(1, count),
        norm_gain.reshape(1, features),
        router_weight.T,
    )
    return pl.pallas_call(
        functools.partial(route_kernel, sizes),
        out_shape=[pltpu.VMEM((count, 1), I32)]
        + [pltpu.VMEM((capacity, features), BF16)] * dp_size,
        in_specs=[pl.BlockSpec(memory_space=pltpu.SMEM)] + vmem_specs(len(operands)),
        out_specs=vmem_specs(1 + dp_size),
        scratch_shapes=[pltpu.VMEM((count, features), BF16)],
        compiler_params=pltpu.CompilerParams(vmem_limit_bytes=VMEM_LIMIT),
    )(place, *map(in_vmem, operands))


def load_kernel(*refs):
    count = len(refs) // 2
    sems = refs[-1]
    copies = [
        pltpu.make_async_copy(refs[i], refs[count + i], sems.at[i]) for i in range(count)
    ]
    for copy in copies:
        copy.start()
    for copy in copies:
        copy.wait()


def load(*arrays):
    return pl.pallas_call(
        load_kernel,
        out_shape=[pltpu.VMEM(x.shape, x.dtype) for x in arrays],
        in_specs=[pl.BlockSpec(memory_space=pl.ANY)] * len(arrays),
        out_specs=vmem_specs(len(arrays)),
        scratch_shapes=[pltpu.SemaphoreType.DMA((len(arrays),))],
        cost_estimate=pl.CostEstimate(
            flops=0, bytes_accessed=2 * sum(x.size * 2 for x in arrays), transcendentals=0
        ),
        compiler_params=pltpu.CompilerParams(vmem_limit_bytes=VMEM_LIMIT),
    )(*arrays)


def expert_kernel(groups, *refs):
    count = sum(groups)
    pieces, (gate, up, down), outs = refs[:count], refs[count : count + 3], refs[count + 3 : -2]
    acts, hidden = refs[-2:]
    features, units = gate.shape
    step = step_of(features, 1024)
    acts[...] = jnp.zeros_like(acts)

    @pl.loop(0, features // step)
    def _(i):
        cols = pl.ds(pl.multiple_of(i * step, step), step)
        rows = jnp.concatenate([piece[:, cols].astype(F32) for piece in pieces], axis=0)
        weights = jnp.concatenate([gate[cols, :], up[cols, :]], axis=1)
        acts[...] += jnp.dot(rows.astype(BF16), weights, preferred_element_type=F32)

    gate_act, up_act = acts[:, :units], acts[:, units:]
    hidden[...] = (gate_act / (1.0 + jnp.exp(-gate_act)) * up_act).astype(BF16)

    @pl.loop(0, features // step)
    def _(i):
        cols = pl.ds(pl.multiple_of(i * step, step), step)
        product = jnp.dot(hidden[...], down[:, cols], preferred_element_type=F32)
        first = 0
        for out in outs:
            out[:, cols] = product[first : first + out.shape[0]].astype(BF16)
            first += out.shape[0]


def expert_apply(groups, pieces, gate, up, down):
    rows, features = pieces[0].shape
    total = rows * sum(groups)
    units = gate.shape[1]
    operands = [in_vmem(x) for x in (*pieces, gate, up, down)]
    return pl.pallas_call(
        functools.partial(expert_kernel, groups),
        out_shape=[pltpu.VMEM((rows * n, features), BF16) for n in groups],
        in_specs=vmem_specs(len(operands)),
        out_specs=vmem_specs(len(groups)),
        scratch_shapes=[pltpu.VMEM((total, 2 * units), F32), pltpu.VMEM((total, units), BF16)],
        compiler_params=pltpu.CompilerParams(vmem_limit_bytes=VMEM_LIMIT),
        cost_estimate=pl.CostEstimate(
            flops=6 * total * features * units,
            bytes_accessed=6 * features * units + 4 * total * features,
            transcendentals=total * units,
        ),
    )(*operands)


def collect_kernel(row_of, *refs):
    pieces, (out, held, sems) = refs[:-3], refs[-3:]
    count, features = held.shape
    step = step_of(features, 1024)
    total = sum(piece.shape[0] for piece in pieces)
    across = lax.broadcasted_iota(I32, (count, total), 1)
    picks = jnp.where(row_of[...] == across, 1.0, 0.0).astype(BF16)
    copies = []
    for i in range(features // step):
        cols = pl.ds(i * step, step)
        rows = jnp.concatenate([piece[:, cols].astype(F32) for piece in pieces], axis=0)
        held[:, cols] = jnp.dot(picks, rows.astype(BF16), preferred_element_type=F32).astype(BF16)
        copies.append(pltpu.make_async_copy(held.at[:, cols], out.at[:, cols], sems.at[i]))
        copies[-1].start()
    for copy in copies:
        copy.wait()


def collect(row_of, pieces):
    count, features = row_of.shape[0], pieces[0].shape[1]
    return pl.pallas_call(
        collect_kernel,
        out_shape=jax.ShapeDtypeStruct((count, features), BF16),
        in_specs=vmem_specs(1 + len(pieces)),
        out_specs=pl.BlockSpec(memory_space=pl.ANY),
        scratch_shapes=[
            pltpu.VMEM((count, features), BF16),
            pltpu.SemaphoreType.DMA((features // step_of(features, 1024),)),
        ],
        compiler_params=pltpu.CompilerParams(vmem_limit_bytes=VMEM_LIMIT),
    )(*map(in_vmem, (row_of, *pieces)))


def after(values, *earlier):
    return lax.optimization_barrier((values, *earlier))[0]


def per_device(tokens, expert_ids, norm_gain, router_weight, w_gate, w_up, w_down):
    dp_size = lax.axis_size("dp")
    tensor_size = lax.axis_size("tensor")
    chips = lax.axis_size("expert") // 2
    half = chips // 2
    capacity = 5 * tokens.shape[0] // (4 * dp_size * tensor_size)
    rows = dp_size * capacity
    place = jnp.stack([lax.axis_index("dp"), lax.axis_index("tensor")]).astype(I32)

    row_of, *outgoing = route(
        (dp_size, tensor_size, capacity), place, tokens, expert_ids, norm_gain, router_weight
    )
    arrived = [outgoing[0]]
    for j in range(1, dp_size):
        arrived.append(shift(outgoing[j], "dp", j))
    gate, up, down = load(w_gate[0], w_up[0], w_down[0])
    arrived[-1] = after(arrived[-1], gate)
    mine = jnp.concatenate(arrived, axis=0)

    apply = functools.partial(expert_apply, gate=gate, up=up, down=down)
    other = swap(mine)
    own_part, other_part = apply((1, 1), [mine, other])
    far, near = after(ring_step(mine), own_part), ring_step(other)
    parts = []
    for k in range(1, half):
        part = apply((2, 1, 1), [far, near, swap(far), swap(near)])
        far = ring_step(far)
        if k < half - 1:
            near = after(ring_step(near), part[0])
        parts.append(part)
    last_kept, last_sent = apply((1, 1), [after(far, parts[-1][0]), swap(far)])

    near_sum, far_sum = None, None
    for k in range(half - 1, 0, -1):
        sent, near_part, far_part = parts[k - 1]
        theirs = swap(sent)
        if near_sum is None:
            near_term = add(near_part, theirs[:rows])
            far_sum = ring_step(add(last_kept, swap(last_sent)))
        else:
            near_term = add(near_sum, near_part, theirs[:rows])
        near_sum = ring_step(near_term)
        far_sum = ring_step(add(after(far_sum, near_term), far_part, theirs[rows:]))
    near_term = swap(add(near_sum, other_part))
    slot_out = add(after(far_sum, near_term), own_part, near_term)

    returned = [slot_out[:capacity]]
    for j in range(1, dp_size):
        returned.append(shift(slot_out[j * capacity : (j + 1) * capacity], "dp", -j))
    here = jnp.concatenate(returned, axis=0)
    ahead = shift(here, "tensor", -1)
    behind = shift(here, "tensor", 1)
    cut = rows // 16 * 8
    opposite = [shift(ahead[:cut], "tensor", -1), shift(behind[cut:], "tensor", 1)]
    return collect(row_of, [here, ahead, *opposite, behind])


def solution(mesh):
    return jax.shard_map(
        per_device,
        mesh=mesh,
        in_specs=(
            P(("dp", "expert"), None),
            P(("dp", "expert"), None),
            P(),
            P(),
            P(("dp", "tensor"), None, "expert"),
            P(("dp", "tensor"), None, "expert"),
            P(("dp", "tensor"), "expert", None),
        ),
        out_specs=P(("dp", "expert"), None),
        check_vma=False,
    )
```

time: 155 us -> 138 us (0.89); the launches traced: 153 us -> 137 us
  waiting for transfers between devices: 86.5 us -> 74.7 us
  starting transfers between devices: 31 us -> 26.7 us
  Pallas kernels: 18.7 us -> 22.9 us
  matrix products: 4.12 us -> 0 us
  local copies, waits for them, and re-layouts: 7.72 us -> 10.8 us
  other arithmetic: 4.21 us -> 1.63 us
    ppermute x14, waiting for transfers between devices: 63.9 us -> 52 us  [ring_step(): return lax.ppermute(values, 'expert', pairs)]
    unnamed x16 -> x15, local copies, waits for them, and re-layouts: 4.92 us -> 10.7 us
    ppermute x14, starting transfers between devices: 10.4 us -> 4.9 us  [ring_step(): return lax.ppermute(values, 'expert', pairs)]
    pallas_call x5 -> x8, Pallas kernels: 18.7 us -> 22.9 us  [the longest x5 18.6 us: expert_apply(): pl.pallas_call(functools.partial(expert_kernel, groups), out_shape=[pltpu...]
    dot_general x3 -> x0, matrix products: 4.12 us -> none  [the longest x1 1.86 us: per_device(): logits = jnp.dot(normed, router_weight, preferred_element_type=F32)]
    ppermute x13, waiting for transfers between devices: 0.03 us -> 4.11 us  [swap(): return lax.ppermute(values, 'expert', [(i, i ^ 1) for i in range(size)])]
    ppermute x10, waiting for transfers between devices: 22.6 us -> 18.6 us  [shift(): lax.ppermute(values, axis, [(i, (i + steps) % size) for i in range(size)])]
    reduce_sum x2 -> x0, other arithmetic: 2.6 us -> none  [the longest x1 1.76 us: normalize(): mean_square = jnp.mean(widened * widened, axis=-1, keepdims=True)]
  transfers between devices with their start and end apart: 37 -> 37, of which waited for: 19 -> 22; matrix products, arithmetic and copies ran while one was open for 1% -> 1% of each run, Pallas kernels for 12% -> 12%
where the time goes in v1:
time: 138 us; the launch traced here: 137 us
  waiting for transfers between devices  74.7 us (54%)
  starting transfers between devices  26.7 us (19%)
  Pallas kernels  22.9 us (17%)
  local copies, waits for them, and re-layouts  10.8 us (8%)
  other arithmetic  1.63 us (1%)
    ppermute x14, waiting for transfers between devices, ring_step(): return lax.ppermute(values, 'expert', pairs)  52 us
    pallas_call x5, Pallas kernels, expert_apply(): pl.pallas_call(functools.partial(expert_kernel, groups), out_shape=[pltpu...  18.6 us
    ppermute x10, waiting for transfers between devices, shift(): lax.ppermute(values, axis, [(i, (i + steps) % size) for i in range(size)])  18.6 us
    ppermute x10, starting transfers between devices, shift(): lax.ppermute(values, axis, [(i, (i + steps) % size) for i in range(size)])  15.2 us
    unnamed x15, local copies, waits for them, and re-layouts  10.7 us
    ppermute x13, starting transfers between devices, swap(): return lax.ppermute(values, 'expert', [(i, i ^ 1) for i in range(size)])  6.59 us
    ppermute x14, starting transfers between devices, ring_step(): return lax.ppermute(values, 'expert', pairs)  4.9 us
    ppermute x13, waiting for transfers between devices, swap(): return lax.ppermute(values, 'expert', [(i, i ^ 1) for i in range(size)])  4.11 us
  transfers between devices with their start and end apart: 37, of which 22 were waited for; matrix products, arithmetic and copies ran while one was open for 1% of the time, Pallas kernels for 12%

profile of v1, /device:TPU:6, one launch (start us, length us, event | category | flops | bytes accessed | tf_op | source)
XLA Modules:
  0.0 137.3 jit_solution(18409162208636826271)
XLA Ops:
  4.5 2.1 %shard_map.73 = (s32[128,1]{1,0:T(8,128)S(1)}, bf16[10,5120]{1,0:T(8,128)(2,1)S(1)}, bf16[10,5120]{1,0:T(8,128)(2,1)S(1)}, bf16[10,5120]{1,0:T(8,128)(2,1)S(1)}, bf16[10,5120]{1,0:T(8,128)(2,1)S(1)}) custom-call(s32[2]{0:T(128)S(1)} %pad_add_fusion.place, bf16[128,5120]{1,0:T(8,128)(2,1)S(1)} %copy-done.3, s32[128,1]{1,0:T(8,128)S(1)} %copy.8.ids_col, ...), custom_call_target="tpu_custom_call" | custom-call | tf_op jit(solution)/shard_map/pallas_call | solution.py:115
  7.5 2.4 %collective-permute-start = (bf16[10,5120]{1,0:T(8,128)(2,1)S(1)}, bf16[10,5120]{1,0:T(8,128)(2,1)S(1)}, u32[]{:S(2)}, u32[]{:S(2)}) collective-permute-start(bf16[10,5120]{1,0:T(8,128)(2,1)S(1)} %get-tuple-element.37), channel_id=1, source_target_pairs={{0,64},{64,128},{128,192},{192,0},{1,65},{65,129},{129,193},{193,1... | collective-permute-start | bytes 307208 | tf_op jit(solution)/shard_map/ppermute | solution.py:38
  10.3 2.1 %copy-done = bf16[1,5120,384]{2,1,0:T(8,128)(2,1)S(1)} copy-done((bf16[1,5120,384]{2,1,0:T(8,128)(2,1)S(1)}, bf16[1,5120,384]{2,1,0:T(8,128)(2,1)}, u32[]{:S(2)}) %copy-start) | copy-done | bytes 3932184
  12.5 2.1 %copy-done.1 = bf16[1,5120,384]{2,1,0:T(8,128)(2,1)S(1)} copy-done((bf16[1,5120,384]{2,1,0:T(8,128)(2,1)S(1)}, bf16[1,5120,384]{2,1,0:T(8,128)(2,1)}, u32[]{:S(2)}) %copy-start.1) | copy-done | bytes 3932184
  14.6 2.1 %copy-done.2 = bf16[1,384,5120]{2,1,0:T(8,128)(2,1)S(1)} copy-done((bf16[1,384,5120]{2,1,0:T(8,128)(2,1)S(1)}, bf16[1,384,5120]{2,1,0:T(8,128)(2,1)}, u32[]{:S(2)}) %copy-start.2) | copy-done | bytes 3932184
  17.8 1.8 %collective-permute-start.3 = (bf16[40,5120]{1,0:T(8,128)(2,1)S(1)}, bf16[40,5120]{1,0:T(8,128)(2,1)S(1)}, u32[]{:S(2)}, u32[]{:S(2)}) collective-permute-start(bf16[40,5120]{1,0:T(8,128)(2,1)S(1)} %pad_maximum_fusion.refs_0_), channel_id=1, source_target_pairs={{0,2},{1,15},{2,4},{3,1},{4,6},{5,3},{6,8},{7,5},{8,10},{9,7},{10,... | collective-permute-start | bytes 1228808 | tf_op jit(solution)/shard_map/ppermute | solution.py:44
  19.6 1.9 %collective-permute-start.8 = (bf16[40,5120]{1,0:T(8,128)(2,1)S(1)}, bf16[40,5120]{1,0:T(8,128)(2,1)S(1)}, u32[]{:S(2)}, u32[]{:S(2)}) collective-permute-start(bf16[40,5120]{1,0:T(8,128)(2,1)S(1)} %collective-permute-done.4.refs_1_), channel_id=1, source_target_pairs={{0,2},{1,15},{2,4},{3,1},{4,6},{5,3},{6,8},{7,5},{8,10},{9,7},{10,... | collective-permute-start | bytes 1228808 | tf_op jit(solution)/shard_map/ppermute | solution.py:44
  21.5 3.4 %shard_map.75 = (bf16[40,5120]{1,0:T(8,128)(2,1)S(1)}, bf16[40,5120]{1,0:T(8,128)(2,1)S(1)}) custom-call(bf16[40,5120]{1,0:T(8,128)(2,1)S(1)} %pad_maximum_fusion.refs_0_, bf16[40,5120]{1,0:T(8,128)(2,1)S(1)} %collective-permute-done.4.refs_1_, bf16[5120,384]{1,0:T(8,128)(2,1)S(1)} %get-tuple-element.40.refs_2_.refs_4_, ...), custom_call_target="tpu_custom_call" | custom-call | flops 943718400 | bytes 13434880 | tf_op jit(solution)/shard_map/pallas_call | solution.py:185
  24.9 4.6 %collective-permute-done.3.refs_0_ = bf16[40,5120]{1,0:T(8,128)(2,1)S(1)} collective-permute-done((bf16[40,5120]{1,0:T(8,128)(2,1)S(1)}, bf16[40,5120]{1,0:T(8,128)(2,1)S(1)}, u32[]{:S(2)}, u32[]{:S(2)}) %collective-permute-start.3) | collective-permute-done | bytes 409632 | tf_op jit(solution)/shard_map/ppermute | solution.py:44
  29.5 2.2 %collective-permute-start.10 = (bf16[40,5120]{1,0:T(8,128)(2,1)S(1)}, bf16[40,5120]{1,0:T(8,128)(2,1)S(1)}, u32[]{:S(2)}, u32[]{:S(2)}) collective-permute-start(bf16[40,5120]{1,0:T(8,128)(2,1)S(1)} %collective-permute-done.3.refs_0_), channel_id=1, source_target_pairs={{0,1},{1,0},{2,3},{3,2},{4,5},{5,4},{6,7},{7,6},{8,9},{9,8},{10,11... | collective-permute-start | bytes 1228808 | tf_op jit(solution)/shard_map/ppermute | solution.py:49
  31.7 2.2 %collective-permute-done.8.refs_1_ = bf16[40,5120]{1,0:T(8,128)(2,1)S(1)} collective-permute-done((bf16[40,5120]{1,0:T(8,128)(2,1)S(1)}, bf16[40,5120]{1,0:T(8,128)(2,1)S(1)}, u32[]{:S(2)}, u32[]{:S(2)}) %collective-permute-start.8) | collective-permute-done | bytes 409632 | tf_op jit(solution)/shard_map/ppermute | solution.py:44
  33.9 4.8 %collective-permute-done.5.refs_0_ = bf16[40,5120]{1,0:T(8,128)(2,1)S(1)} collective-permute-done((bf16[40,5120]{1,0:T(8,128)(2,1)S(1)}, bf16[40,5120]{1,0:T(8,128)(2,1)S(1)}, u32[]{:S(2)}, u32[]{:S(2)}) %collective-permute-start.5) | collective-permute-done | bytes 409632 | tf_op jit(solution)/shard_map/ppermute | solution.py:44
  38.7 3.9 %shard_map.76 = (bf16[80,5120]{1,0:T(8,128)(2,1)S(1)}, bf16[40,5120]{1,0:T(8,128)(2,1)S(1)}, bf16[40,5120]{1,0:T(8,128)(2,1)S(1)}) custom-call(bf16[40,5120]{1,0:T(8,128)(2,1)S(1)} %collective-permute-done.3.refs_0_, bf16[40,5120]{1,0:T(8,128)(2,1)S(1)} %collective-permute-done.8.refs_1_, bf16[40,5120]{1,0:T(8,128)(2,1)S(1)} %collective-permute-done.10.refs_2_, ...), custom_call_target="tpu_custom_call" | custom-call | flops 1887436800 | bytes 15073280 | tf_op jit(solution)/shard_map/pallas_call | solution.py:185
  45.0 2.9 %collective-permute-done.6.refs_0_ = bf16[40,5120]{1,0:T(8,128)(2,1)S(1)} collective-permute-done((bf16[40,5120]{1,0:T(8,128)(2,1)S(1)}, bf16[40,5120]{1,0:T(8,128)(2,1)S(1)}, u32[]{:S(2)}, u32[]{:S(2)}) %collective-permute-start.6) | collective-permute-done | bytes 409632 | tf_op jit(solution)/shard_map/ppermute | solution.py:44
  49.3 3.9 %shard_map.77 = (bf16[80,5120]{1,0:T(8,128)(2,1)S(1)}, bf16[40,5120]{1,0:T(8,128)(2,1)S(1)}, bf16[40,5120]{1,0:T(8,128)(2,1)S(1)}) custom-call(bf16[40,5120]{1,0:T(8,128)(2,1)S(1)} %collective-permute-done.5.refs_0_, bf16[40,5120]{1,0:T(8,128)(2,1)S(1)} %collective-permute-done.9.refs_1_, bf16[40,5120]{1,0:T(8,128)(2,1)S(1)} %collective-permute-done.13.refs_2_, ...), custom_call_target="tpu_custom_call" | custom-call | flops 1887436800 | bytes 15073280 | tf_op jit(solution)/shard_map/pallas_call | solution.py:185
  53.7 4.4 %collective-permute-done.7.refs_0_ = bf16[40,5120]{1,0:T(8,128)(2,1)S(1)} collective-permute-done((bf16[40,5120]{1,0:T(8,128)(2,1)S(1)}, bf16[40,5120]{1,0:T(8,128)(2,1)S(1)}, u32[]{:S(2)}, u32[]{:S(2)}) %collective-permute-start.7) | collective-permute-done | bytes 409632 | tf_op jit(solution)/shard_map/ppermute | solution.py:44
  58.1 3.9 %shard_map.78 = (bf16[80,5120]{1,0:T(8,128)(2,1)S(1)}, bf16[40,5120]{1,0:T(8,128)(2,1)S(1)}, bf16[40,5120]{1,0:T(8,128)(2,1)S(1)}) custom-call(bf16[40,5120]{1,0:T(8,128)(2,1)S(1)} %collective-permute-done.6.refs_0_, bf16[40,5120]{1,0:T(8,128)(2,1)S(1)} %collective-permute-done.12.refs_1_, bf16[40,5120]{1,0:T(8,128)(2,1)S(1)} %collective-permute-done.15.refs_2_, ...), custom_call_target="tpu_custom_call" | custom-call | flops 1887436800 | bytes 15073280 | tf_op jit(solution)/shard_map/pallas_call | solution.py:185
  62.1 3.4 %shard_map.79 = (bf16[40,5120]{1,0:T(8,128)(2,1)S(1)}, bf16[40,5120]{1,0:T(8,128)(2,1)S(1)}) custom-call(bf16[40,5120]{1,0:T(8,128)(2,1)S(1)} %collective-permute-done.7.refs_0_, bf16[40,5120]{1,0:T(8,128)(2,1)S(1)} %collective-permute-done.17.refs_1_, bf16[5120,384]{1,0:T(8,128)(2,1)S(1)} %get-tuple-element.40.refs_2_.refs_4_, ...), custom_call_target="tpu_custom_call" | custom-call | flops 943718400 | bytes 13434880 | tf_op jit(solution)/shard_map/pallas_call | solution.py:185
  67.6 3.3 %collective-permute-done.20 = bf16[80,5120]{1,0:T(8,128)(2,1)S(1)} collective-permute-done((bf16[80,5120]{1,0:T(8,128)(2,1)S(1)}, bf16[80,5120]{1,0:T(8,128)(2,1)S(1)}, u32[]{:S(2)}, u32[]{:S(2)}) %collective-permute-start.20) | collective-permute-done | bytes 819232 | tf_op jit(solution)/shard_map/ppermute | solution.py:49
  71.2 5.6 %collective-permute-done.19 = bf16[40,5120]{1,0:T(8,128)(2,1)S(1)} collective-permute-done((bf16[40,5120]{1,0:T(8,128)(2,1)S(1)}, bf16[40,5120]{1,0:T(8,128)(2,1)S(1)}, u32[]{:S(2)}, u32[]{:S(2)}) %collective-permute-start.19) | collective-permute-done | bytes 409632 | tf_op jit(solution)/shard_map/ppermute | solution.py:44
  77.0 4.1 %collective-permute-done.22 = bf16[40,5120]{1,0:T(8,128)(2,1)S(1)} collective-permute-done((bf16[40,5120]{1,0:T(8,128)(2,1)S(1)}, bf16[40,5120]{1,0:T(8,128)(2,1)S(1)}, u32[]{:S(2)}, u32[]{:S(2)}) %collective-permute-start.22) | collective-permute-done | bytes 409632 | tf_op jit(solution)/shard_map/ppermute | solution.py:44
  81.4 4.8 %collective-permute-done.21 = bf16[40,5120]{1,0:T(8,128)(2,1)S(1)} collective-permute-done((bf16[40,5120]{1,0:T(8,128)(2,1)S(1)}, bf16[40,5120]{1,0:T(8,128)(2,1)S(1)}, u32[]{:S(2)}, u32[]{:S(2)}) %collective-permute-start.21) | collective-permute-done | bytes 409632 | tf_op jit(solution)/shard_map/ppermute | solution.py:44
  86.4 4.1 %collective-permute-done.25 = bf16[40,5120]{1,0:T(8,128)(2,1)S(1)} collective-permute-done((bf16[40,5120]{1,0:T(8,128)(2,1)S(1)}, bf16[40,5120]{1,0:T(8,128)(2,1)S(1)}, u32[]{:S(2)}, u32[]{:S(2)}) %collective-permute-start.25) | collective-permute-done | bytes 409632 | tf_op jit(solution)/shard_map/ppermute | solution.py:44
  90.8 4.8 %collective-permute-done.24 = bf16[40,5120]{1,0:T(8,128)(2,1)S(1)} collective-permute-done((bf16[40,5120]{1,0:T(8,128)(2,1)S(1)}, bf16[40,5120]{1,0:T(8,128)(2,1)S(1)}, u32[]{:S(2)}, u32[]{:S(2)}) %collective-permute-start.24) | collective-permute-done | bytes 409632 | tf_op jit(solution)/shard_map/ppermute | solution.py:44
  96.0 3.9 %collective-permute-done.28 = bf16[40,5120]{1,0:T(8,128)(2,1)S(1)} collective-permute-done((bf16[40,5120]{1,0:T(8,128)(2,1)S(1)}, bf16[40,5120]{1,0:T(8,128)(2,1)S(1)}, u32[]{:S(2)}, u32[]{:S(2)}) %collective-permute-start.28) | collective-permute-done | bytes 409632 | tf_op jit(solution)/shard_map/ppermute | solution.py:44
  100.2 5.0 %collective-permute-done.27 = bf16[40,5120]{1,0:T(8,128)(2,1)S(1)} collective-permute-done((bf16[40,5120]{1,0:T(8,128)(2,1)S(1)}, bf16[40,5120]{1,0:T(8,128)(2,1)S(1)}, u32[]{:S(2)}, u32[]{:S(2)}) %collective-permute-start.27) | collective-permute-done | bytes 409632 | tf_op jit(solution)/shard_map/ppermute | solution.py:44
  105.5 3.0 %collective-permute-start.32 = (bf16[10,5120]{1,0:T(8,128)(2,1)S(1)}, bf16[10,5120]{1,0:T(8,128)(2,1)S(1)}, u32[]{:S(2)}, u32[]{:S(2)}) collective-permute-start(bf16[10,5120]{1,0:T(8,128)(2,1)S(1)} %get-tuple-element.66), channel_id=1, source_target_pairs={{0,64},{64,128},{128,192},{192,0},{1,65},{65,129},{129,193},{193,1... | collective-permute-start | bytes 307208 | tf_op jit(solution)/shard_map/ppermute | solution.py:38
  110.2 2.9 %collective-permute-done.32 = bf16[10,5120]{1,0:T(8,128)(2,1)S(1)} collective-permute-done((bf16[10,5120]{1,0:T(8,128)(2,1)S(1)}, bf16[10,5120]{1,0:T(8,128)(2,1)S(1)}, u32[]{:S(2)}, u32[]{:S(2)}) %collective-permute-start.32) | collective-permute-done | bytes 102432 | tf_op jit(solution)/shard_map/ppermute | solution.py:38
  113.1 2.3 %collective-permute-done.31 = bf16[10,5120]{1,0:T(8,128)(2,1)S(1)} collective-permute-done((bf16[10,5120]{1,0:T(8,128)(2,1)S(1)}, bf16[10,5120]{1,0:T(8,128)(2,1)S(1)}, u32[]{:S(2)}, u32[]{:S(2)}) %collective-permute-start.31) | collective-permute-done | bytes 102432 | tf_op jit(solution)/shard_map/ppermute | solution.py:38
  120.6 7.6 %collective-permute-done.35.refs_4_ = bf16[40,5120]{1,0:T(8,128)(2,1)S(1)} collective-permute-done((bf16[40,5120]{1,0:T(8,128)(2,1)S(1)}, bf16[40,5120]{1,0:T(8,128)(2,1)S(1)}, u32[]{:S(2)}, u32[]{:S(2)}) %collective-permute-start.35) | collective-permute-done | bytes 409632 | tf_op jit(solution)/shard_map/ppermute | solution.py:38
  129.6 2.0 %collective-permute-start.34 = (bf16[16,5120]{1,0:T(8,128)(2,1)S(1)}, bf16[16,5120]{1,0:T(8,128)(2,1)S(1)}, u32[]{:S(2)}, u32[]{:S(2)}) collective-permute-start(bf16[16,5120]{1,0:T(8,128)(2,1)S(1)} %slice.58), channel_id=1, source_target_pairs={{0,48},{16,0},{32,16},{48,32},{1,49},{17,1},{33,17},{49,33},{2,50}... | collective-permute-start | bytes 491528 | tf_op jit(solution)/shard_map/ppermute | solution.py:38
  131.7 3.4 %collective-permute-done.34.refs_2_ = bf16[16,5120]{1,0:T(8,128)(2,1)S(1)} collective-permute-done((bf16[16,5120]{1,0:T(8,128)(2,1)S(1)}, bf16[16,5120]{1,0:T(8,128)(2,1)S(1)}, u32[]{:S(2)}, u32[]{:S(2)}) %collective-permute-start.34) | collective-permute-done | bytes 163872 | tf_op jit(solution)/shard_map/ppermute | solution.py:38
  (80 shorter events, 25.8 us)
Async XLA Ops:
  6.6 10.9 %collective-permute-start.2 = (bf16[10,5120]{1,0:T(8,128)(2,1)S(1)}, bf16[10,5120]{1,0:T(8,128)(2,1)S(1)}, u32[]{:S(2)}, u32[]{:S(2)}) collective-permute-start(bf16[10,5120]{1,0:T(8,128)(2,1)S(1)} %get-tuple-element.39), channel_id=1, source_target_pairs={{0,192},{64,0},{128,64},{192,128},{1,193},{65,1},{129,65},{193,129... | collective-permute-start | bytes 307208 | tf_op jit(solution)/shard_map/ppermute | solution.py:38
  7.5 10.0 %collective-permute-start = (bf16[10,5120]{1,0:T(8,128)(2,1)S(1)}, bf16[10,5120]{1,0:T(8,128)(2,1)S(1)}, u32[]{:S(2)}, u32[]{:S(2)}) collective-permute-start(bf16[10,5120]{1,0:T(8,128)(2,1)S(1)} %get-tuple-element.37), channel_id=1, source_target_pairs={{0,64},{64,128},{128,192},{192,0},{1,65},{65,129},{129,193},{193,1... | collective-permute-start | bytes 307208 | tf_op jit(solution)/shard_map/ppermute | solution.py:38
  9.9 7.6 %collective-permute-start.1 = (bf16[10,5120]{1,0:T(8,128)(2,1)S(1)}, bf16[10,5120]{1,0:T(8,128)(2,1)S(1)}, u32[]{:S(2)}, u32[]{:S(2)}) collective-permute-start(bf16[10,5120]{1,0:T(8,128)(2,1)S(1)} %get-tuple-element.38), channel_id=1, source_target_pairs={{0,128},{64,192},{128,0},{192,64},{1,129},{65,193},{129,1},{193,65... | collective-permute-start | bytes 307208 | tf_op jit(solution)/shard_map/ppermute | solution.py:38
  17.8 11.6 %collective-permute-start.3 = (bf16[40,5120]{1,0:T(8,128)(2,1)S(1)}, bf16[40,5120]{1,0:T(8,128)(2,1)S(1)}, u32[]{:S(2)}, u32[]{:S(2)}) collective-permute-start(bf16[40,5120]{1,0:T(8,128)(2,1)S(1)} %pad_maximum_fusion.refs_0_), channel_id=1, source_target_pairs={{0,2},{1,15},{2,4},{3,1},{4,6},{5,3},{6,8},{7,5},{8,10},{9,7},{10,... | collective-permute-start | bytes 1228808 | tf_op jit(solution)/shard_map/ppermute | solution.py:44
  19.6 14.3 %collective-permute-start.8 = (bf16[40,5120]{1,0:T(8,128)(2,1)S(1)}, bf16[40,5120]{1,0:T(8,128)(2,1)S(1)}, u32[]{:S(2)}, u32[]{:S(2)}) collective-permute-start(bf16[40,5120]{1,0:T(8,128)(2,1)S(1)} %collective-permute-done.4.refs_1_), channel_id=1, source_target_pairs={{0,2},{1,15},{2,4},{3,1},{4,6},{5,3},{6,8},{7,5},{8,10},{9,7},{10,... | collective-permute-start | bytes 1228808 | tf_op jit(solution)/shard_map/ppermute | solution.py:44
  29.5 9.2 %collective-permute-start.5 = (bf16[40,5120]{1,0:T(8,128)(2,1)S(1)}, bf16[40,5120]{1,0:T(8,128)(2,1)S(1)}, u32[]{:S(2)}, u32[]{:S(2)}) collective-permute-start(bf16[40,5120]{1,0:T(8,128)(2,1)S(1)} %collective-permute-done.3.refs_0_), channel_id=1, source_target_pairs={{0,2},{1,15},{2,4},{3,1},{4,6},{5,3},{6,8},{7,5},{8,10},{9,7},{10,... | collective-permute-start | bytes 1228808 | tf_op jit(solution)/shard_map/ppermute | solution.py:44
  29.5 9.2 %collective-permute-start.10 = (bf16[40,5120]{1,0:T(8,128)(2,1)S(1)}, bf16[40,5120]{1,0:T(8,128)(2,1)S(1)}, u32[]{:S(2)}, u32[]{:S(2)}) collective-permute-start(bf16[40,5120]{1,0:T(8,128)(2,1)S(1)} %collective-permute-done.3.refs_0_), channel_id=1, source_target_pairs={{0,1},{1,0},{2,3},{3,2},{4,5},{5,4},{6,7},{7,6},{8,9},{9,8},{10,11... | collective-permute-start | bytes 1228808 | tf_op jit(solution)/shard_map/ppermute | solution.py:49
  33.9 4.8 %collective-permute-start.11 = (bf16[40,5120]{1,0:T(8,128)(2,1)S(1)}, bf16[40,5120]{1,0:T(8,128)(2,1)S(1)}, u32[]{:S(2)}, u32[]{:S(2)}) collective-permute-start(bf16[40,5120]{1,0:T(8,128)(2,1)S(1)} %collective-permute-done.8.refs_1_), channel_id=1, source_target_pairs={{0,1},{1,0},{2,3},{3,2},{4,5},{5,4},{6,7},{7,6},{8,9},{9,8},{10,11... | collective-permute-start | bytes 1228808 | tf_op jit(solution)/shard_map/ppermute | solution.py:49
  33.9 9.2 %collective-permute-start.9 = (bf16[40,5120]{1,0:T(8,128)(2,1)S(1)}, bf16[40,5120]{1,0:T(8,128)(2,1)S(1)}, u32[]{:S(2)}, u32[]{:S(2)}) collective-permute-start(bf16[40,5120]{1,0:T(8,128)(2,1)S(1)} %collective-permute-done.8.refs_1_), channel_id=1, source_target_pairs={{0,2},{1,15},{2,4},{3,1},{4,6},{5,3},{6,8},{7,5},{8,10},{9,7},{10,... | collective-permute-start | bytes 1228808 | tf_op jit(solution)/shard_map/ppermute | solution.py:44
  38.6 10.6 %collective-permute-start.13 = (bf16[40,5120]{1,0:T(8,128)(2,1)S(1)}, bf16[40,5120]{1,0:T(8,128)(2,1)S(1)}, u32[]{:S(2)}, u32[]{:S(2)}) collective-permute-start(bf16[40,5120]{1,0:T(8,128)(2,1)S(1)} %collective-permute-done.5.refs_0_), channel_id=1, source_target_pairs={{0,1},{1,0},{2,3},{3,2},{4,5},{5,4},{6,7},{7,6},{8,9},{9,8},{10,11... | collective-permute-start | bytes 1228808 | tf_op jit(solution)/shard_map/ppermute | solution.py:49
  38.6 9.2 %collective-permute-start.6 = (bf16[40,5120]{1,0:T(8,128)(2,1)S(1)}, bf16[40,5120]{1,0:T(8,128)(2,1)S(1)}, u32[]{:S(2)}, u32[]{:S(2)}) collective-permute-start(bf16[40,5120]{1,0:T(8,128)(2,1)S(1)} %collective-permute-done.5.refs_0_), channel_id=1, source_target_pairs={{0,2},{1,15},{2,4},{3,1},{4,6},{5,3},{6,8},{7,5},{8,10},{9,7},{10,... | collective-permute-start | bytes 1228808 | tf_op jit(solution)/shard_map/ppermute | solution.py:44
  43.0 6.2 %collective-permute-start.14 = (bf16[40,5120]{1,0:T(8,128)(2,1)S(1)}, bf16[40,5120]{1,0:T(8,128)(2,1)S(1)}, u32[]{:S(2)}, u32[]{:S(2)}) collective-permute-start(bf16[40,5120]{1,0:T(8,128)(2,1)S(1)} %collective-permute-done.9.refs_1_), channel_id=1, source_target_pairs={{0,1},{1,0},{2,3},{3,2},{4,5},{5,4},{6,7},{7,6},{8,9},{9,8},{10,11... | collective-permute-start | bytes 1228808 | tf_op jit(solution)/shard_map/ppermute | solution.py:49
  44.6 9.2 %collective-permute-start.12 = (bf16[40,5120]{1,0:T(8,128)(2,1)S(1)}, bf16[40,5120]{1,0:T(8,128)(2,1)S(1)}, u32[]{:S(2)}, u32[]{:S(2)}) collective-permute-start(bf16[40,5120]{1,0:T(8,128)(2,1)S(1)} %collective-permute-done.9.refs_1_), channel_id=1, source_target_pairs={{0,2},{1,15},{2,4},{3,1},{4,6},{5,3},{6,8},{7,5},{8,10},{9,7},{10,... | collective-permute-start | bytes 1228808 | tf_op jit(solution)/shard_map/ppermute | solution.py:44
  47.8 10.3 %collective-permute-start.7 = (bf16[40,5120]{1,0:T(8,128)(2,1)S(1)}, bf16[40,5120]{1,0:T(8,128)(2,1)S(1)}, u32[]{:S(2)}, u32[]{:S(2)}) collective-permute-start(bf16[40,5120]{1,0:T(8,128)(2,1)S(1)} %collective-permute-done.6.refs_0_), channel_id=1, source_target_pairs={{0,2},{1,15},{2,4},{3,1},{4,6},{5,3},{6,8},{7,5},{8,10},{9,7},{10,... | collective-permute-start | bytes 1228808 | tf_op jit(solution)/shard_map/ppermute | solution.py:44
  47.8 10.3 %collective-permute-start.15 = (bf16[40,5120]{1,0:T(8,128)(2,1)S(1)}, bf16[40,5120]{1,0:T(8,128)(2,1)S(1)}, u32[]{:S(2)}, u32[]{:S(2)}) collective-permute-start(bf16[40,5120]{1,0:T(8,128)(2,1)S(1)} %collective-permute-done.6.refs_0_), channel_id=1, source_target_pairs={{0,1},{1,0},{2,3},{3,2},{4,5},{5,4},{6,7},{7,6},{8,9},{9,8},{10,11... | collective-permute-start | bytes 1228808 | tf_op jit(solution)/shard_map/ppermute | solution.py:49
  66.1 20.4 %collective-permute-start.26 = (bf16[80,5120]{1,0:T(8,128)(2,1)S(1)}, bf16[80,5120]{1,0:T(8,128)(2,1)S(1)}, u32[]{:S(2)}, u32[]{:S(2)}) collective-permute-start(bf16[80,5120]{1,0:T(8,128)(2,1)S(1)} %get-tuple-element.46), channel_id=1, source_target_pairs={{0,1},{1,0},{2,3},{3,2},{4,5},{5,4},{6,7},{7,6},{8,9},{9,8},{10,11... | collective-permute-start | bytes 2457608 | tf_op jit(solution)/shard_map/ppermute | solution.py:49
  66.2 10.9 %collective-permute-start.23 = (bf16[80,5120]{1,0:T(8,128)(2,1)S(1)}, bf16[80,5120]{1,0:T(8,128)(2,1)S(1)}, u32[]{:S(2)}, u32[]{:S(2)}) collective-permute-start(bf16[80,5120]{1,0:T(8,128)(2,1)S(1)} %get-tuple-element.48), channel_id=1, source_target_pairs={{0,1},{1,0},{2,3},{3,2},{4,5},{5,4},{6,7},{7,6},{8,9},{9,8},{10,11... | collective-permute-start | bytes 2457608 | tf_op jit(solution)/shard_map/ppermute | solution.py:49
  67.6 9.2 %collective-permute-start.19 = (bf16[40,5120]{1,0:T(8,128)(2,1)S(1)}, bf16[40,5120]{1,0:T(8,128)(2,1)S(1)}, u32[]{:S(2)}, u32[]{:S(2)}) collective-permute-start(bf16[40,5120]{1,0:T(8,128)(2,1)S(1)} %add_convert_fusion.8), channel_id=1, source_target_pairs={{0,2},{1,15},{2,4},{3,1},{4,6},{5,3},{6,8},{7,5},{8,10},{9,7},{10,... | collective-permute-start | bytes 1228808 | tf_op jit(solution)/shard_map/ppermute | solution.py:44
  71.1 10.1 %collective-permute-start.22 = (bf16[40,5120]{1,0:T(8,128)(2,1)S(1)}, bf16[40,5120]{1,0:T(8,128)(2,1)S(1)}, u32[]{:S(2)}, u32[]{:S(2)}) collective-permute-start(bf16[40,5120]{1,0:T(8,128)(2,1)S(1)} %add_convert_fusion.7), channel_id=1, source_target_pairs={{0,2},{1,15},{2,4},{3,1},{4,6},{5,3},{6,8},{7,5},{8,10},{9,7},{10,... | collective-permute-start | bytes 1228808 | tf_op jit(solution)/shard_map/ppermute | solution.py:44
  76.9 9.2 %collective-permute-start.21 = (bf16[40,5120]{1,0:T(8,128)(2,1)S(1)}, bf16[40,5120]{1,0:T(8,128)(2,1)S(1)}, u32[]{:S(2)}, u32[]{:S(2)}) collective-permute-start(bf16[40,5120]{1,0:T(8,128)(2,1)S(1)} %add_convert_fusion.6), channel_id=1, source_target_pairs={{0,2},{1,15},{2,4},{3,1},{4,6},{5,3},{6,8},{7,5},{8,10},{9,7},{10,... | collective-permute-start | bytes 1228808 | tf_op jit(solution)/shard_map/ppermute | solution.py:44
  81.3 9.2 %collective-permute-start.25 = (bf16[40,5120]{1,0:T(8,128)(2,1)S(1)}, bf16[40,5120]{1,0:T(8,128)(2,1)S(1)}, u32[]{:S(2)}, u32[]{:S(2)}) collective-permute-start(bf16[40,5120]{1,0:T(8,128)(2,1)S(1)} %add_convert_fusion.5), channel_id=1, source_target_pairs={{0,2},{1,15},{2,4},{3,1},{4,6},{5,3},{6,8},{7,5},{8,10},{9,7},{10,... | collective-permute-start | bytes 1228808 | tf_op jit(solution)/shard_map/ppermute | solution.py:44
  86.3 9.2 %collective-permute-start.24 = (bf16[40,5120]{1,0:T(8,128)(2,1)S(1)}, bf16[40,5120]{1,0:T(8,128)(2,1)S(1)}, u32[]{:S(2)}, u32[]{:S(2)}) collective-permute-start(bf16[40,5120]{1,0:T(8,128)(2,1)S(1)} %add_convert_fusion.4), channel_id=1, source_target_pairs={{0,2},{1,15},{2,4},{3,1},{4,6},{5,3},{6,8},{7,5},{8,10},{9,7},{10,... | collective-permute-start | bytes 1228808 | tf_op jit(solution)/shard_map/ppermute | solution.py:44
  90.7 9.2 %collective-permute-start.28 = (bf16[40,5120]{1,0:T(8,128)(2,1)S(1)}, bf16[40,5120]{1,0:T(8,128)(2,1)S(1)}, u32[]{:S(2)}, u32[]{:S(2)}) collective-permute-start(bf16[40,5120]{1,0:T(8,128)(2,1)S(1)} %add_convert_fusion.3), channel_id=1, source_target_pairs={{0,2},{1,15},{2,4},{3,1},{4,6},{5,3},{6,8},{7,5},{8,10},{9,7},{10,... | collective-permute-start | bytes 1228808 | tf_op jit(solution)/shard_map/ppermute | solution.py:44
  95.7 9.5 %collective-permute-start.27 = (bf16[40,5120]{1,0:T(8,128)(2,1)S(1)}, bf16[40,5120]{1,0:T(8,128)(2,1)S(1)}, u32[]{:S(2)}, u32[]{:S(2)}) collective-permute-start(bf16[40,5120]{1,0:T(8,128)(2,1)S(1)} %add_convert_fusion.2), channel_id=1, source_target_pairs={{0,2},{1,15},{2,4},{3,1},{4,6},{5,3},{6,8},{7,5},{8,10},{9,7},{10,... | collective-permute-start | bytes 1228808 | tf_op jit(solution)/shard_map/ppermute | solution.py:44
  100.1 5.1 %collective-permute-start.29 = (bf16[40,5120]{1,0:T(8,128)(2,1)S(1)}, bf16[40,5120]{1,0:T(8,128)(2,1)S(1)}, u32[]{:S(2)}, u32[]{:S(2)}) collective-permute-start(bf16[40,5120]{1,0:T(8,128)(2,1)S(1)} %add_convert_fusion.1), channel_id=1, source_target_pairs={{0,1},{1,0},{2,3},{3,2},{4,5},{5,4},{6,7},{7,6},{8,9},{9,8},{10,11... | collective-permute-start | bytes 1228808 | tf_op jit(solution)/shard_map/ppermute | solution.py:49
  105.5 7.7 %collective-permute-start.32 = (bf16[10,5120]{1,0:T(8,128)(2,1)S(1)}, bf16[10,5120]{1,0:T(8,128)(2,1)S(1)}, u32[]{:S(2)}, u32[]{:S(2)}) collective-permute-start(bf16[10,5120]{1,0:T(8,128)(2,1)S(1)} %get-tuple-element.66), channel_id=1, source_target_pairs={{0,64},{64,128},{128,192},{192,0},{1,65},{65,129},{129,193},{193,1... | collective-permute-start | bytes 307208 | tf_op jit(solution)/shard_map/ppermute | solution.py:38
  108.5 6.9 %collective-permute-start.31 = (bf16[10,5120]{1,0:T(8,128)(2,1)S(1)}, bf16[10,5120]{1,0:T(8,128)(2,1)S(1)}, u32[]{:S(2)}, u32[]{:S(2)}) collective-permute-start(bf16[10,5120]{1,0:T(8,128)(2,1)S(1)} %get-tuple-element.67), channel_id=1, source_target_pairs={{0,128},{64,192},{128,0},{192,64},{1,129},{65,193},{129,1},{193,65... | collective-permute-start | bytes 307208 | tf_op jit(solution)/shard_map/ppermute | solution.py:38
  108.9 8.2 %collective-permute-start.30 = (bf16[10,5120]{1,0:T(8,128)(2,1)S(1)}, bf16[10,5120]{1,0:T(8,128)(2,1)S(1)}, u32[]{:S(2)}, u32[]{:S(2)}) collective-permute-start(bf16[10,5120]{1,0:T(8,128)(2,1)S(1)} %get-tuple-element.68), channel_id=1, source_target_pairs={{0,192},{64,0},{128,64},{192,128},{1,193},{65,1},{129,65},{193,129... | collective-permute-start | bytes 307208 | tf_op jit(solution)/shard_map/ppermute | solution.py:38
  117.3 11.0 %collective-permute-start.35 = (bf16[40,5120]{1,0:T(8,128)(2,1)S(1)}, bf16[40,5120]{1,0:T(8,128)(2,1)S(1)}, u32[]{:S(2)}, u32[]{:S(2)}) collective-permute-start(bf16[40,5120]{1,0:T(8,128)(2,1)S(1)} %pad_maximum_fusion.1.refs_0_), channel_id=1, source_target_pairs={{0,16},{16,32},{32,48},{48,0},{1,17},{17,33},{33,49},{49,1},{2,18}... | collective-permute-start | bytes 1228808 | tf_op jit(solution)/shard_map/ppermute | solution.py:38
  118.9 10.7 %collective-permute-start.33 = (bf16[40,5120]{1,0:T(8,128)(2,1)S(1)}, bf16[40,5120]{1,0:T(8,128)(2,1)S(1)}, u32[]{:S(2)}, u32[]{:S(2)}) collective-permute-start(bf16[40,5120]{1,0:T(8,128)(2,1)S(1)} %pad_maximum_fusion.1.refs_0_), channel_id=1, source_target_pairs={{0,48},{16,0},{32,16},{48,32},{1,49},{17,1},{33,17},{49,33},{2,50}... | collective-permute-start | bytes 1228808 | tf_op jit(solution)/shard_map/ppermute | solution.py:38
  128.2 7.5 %collective-permute-start.36 = (bf16[24,5120]{1,0:T(8,128)(2,1)S(1)}, bf16[24,5120]{1,0:T(8,128)(2,1)S(1)}, u32[]{:S(2)}, u32[]{:S(2)}) collective-permute-start(bf16[24,5120]{1,0:T(8,128)(2,1)S(1)} %slice.59), channel_id=1, source_target_pairs={{0,16},{16,32},{32,48},{48,0},{1,17},{17,33},{33,49},{49,1},{2,18}... | collective-permute-start | bytes 737288 | tf_op jit(solution)/shard_map/ppermute | solution.py:38
  129.6 5.4 %collective-permute-start.34 = (bf16[16,5120]{1,0:T(8,128)(2,1)S(1)}, bf16[16,5120]{1,0:T(8,128)(2,1)S(1)}, u32[]{:S(2)}, u32[]{:S(2)}) collective-permute-start(bf16[16,5120]{1,0:T(8,128)(2,1)S(1)} %slice.58), channel_id=1, source_target_pairs={{0,48},{16,0},{32,16},{48,32},{1,49},{17,1},{33,17},{49,33},{2,50}... | collective-permute-start | bytes 491528 | tf_op jit(solution)/shard_map/ppermute | solution.py:38
  (12 other events, 26.5 us)

commit v2 on v1

--- a/solution.py
+++ b/solution.py
@@ -18,6 +18,10 @@
     return pltpu.with_memory_space_constraint(values, pltpu.VMEM)
 
 
+def in_hbm(values):
+    return pltpu.with_memory_space_constraint(values, pltpu.HBM)
+
+
 def vmem_specs(count):
     return [pl.BlockSpec(memory_space=pltpu.VMEM)] * count
 
@@ -38,23 +42,44 @@
     return lax.ppermute(values, axis, [(i, (i + steps) % size) for i in range(size)])
 
 
-def ring_step(values):
+def ring_step(values, name):
     size = lax.axis_size("expert")
     pairs = [(i, (i + (2 if i % 2 == 0 else -2)) % size) for i in range(size)]
-    return lax.ppermute(values, "expert", pairs)
+    with jax.named_scope(name):
+        return lax.ppermute(values, "expert", pairs)
+
+
+def ring_leave(values, name):
+    size = lax.axis_size("expert")
+    pairs = [(i, (i + (3 if i % 2 == 0 else -3)) % size) for i in range(size)]
+    with jax.named_scope(name):
+        return lax.ppermute(values, "expert", pairs)
 
 
 def swap(values):
     size = lax.axis_size("expert")
-    return lax.ppermute(values, "expert", [(i, i ^ 1) for i in range(size)])
-
-
-def route_kernel(sizes, place, tokens, ids_col, ids_row, gain, router, row_of, *outs):
+    with jax.named_scope("other_core"):
+        return lax.ppermute(values, "expert", [(i, i ^ 1) for i in range(size)])
+
+
+def route_kernel(sizes, place, *refs):
     dp_size, tensor_size, capacity = sizes
-    blocks, normed = outs[:-1], outs[-1]
+    sources, row_of, blocks = refs[:4], refs[4], refs[5 : 5 + dp_size]
+    tokens, ids_row, gain, router, normed, sems = refs[5 + dp_size :]
+    copies = [
+        pltpu.make_async_copy(source, held, sems.at[i])
+        for i, (source, held) in enumerate(zip(sources, (tokens, ids_row, gain, router)))
+    ]
+    for copy in copies:
+        copy.start()
+    for copy in copies:
+        copy.wait()
     count, features = tokens.shape
     step = step_of(features, 512)
     spans = [pl.ds(i, step) for i in range(0, features, step)]
+    down = lax.broadcasted_iota(I32, (count, count), 0)
+    across = lax.broadcasted_iota(I32, (count, count), 1)
+    ids_col = jnp.sum(jnp.where(down == across, ids_row[...], 0), axis=1, keepdims=True)
 
     total = jnp.zeros((count, LANES), F32)
     for i in range(0, features, LANES):
@@ -70,12 +95,10 @@
             part, router[:, cols], (((1,), (1,)), ((), ())), preferred_element_type=F32
         )
     expert = lax.broadcasted_iota(I32, logits.shape, 1)
-    chosen = jnp.sum(jnp.where(ids_col[...] == expert, logits, 0.0), axis=1, keepdims=True)
+    chosen = jnp.sum(jnp.where(ids_col == expert, logits, 0.0), axis=1, keepdims=True)
     gate = 1.0 / (1.0 + jnp.exp(-chosen))
 
-    down = lax.broadcasted_iota(I32, (count, count), 0)
-    across = lax.broadcasted_iota(I32, (count, count), 1)
-    same = ids_col[...] == ids_row[...]
+    same = ids_col == ids_row[...]
     slot_col = jnp.sum(jnp.where(same & (across < down), 1, 0), axis=1, keepdims=True)
     slot_row = jnp.sum(jnp.where(same & (down < across), 1, 0), axis=0, keepdims=True)
 
@@ -88,7 +111,7 @@
         on_dp = jnp.where(on_dp < 0, on_dp + dp_size, on_dp)
         return on_dp, jnp.where(on_tensor < 0, on_tensor + tensor_size, on_tensor)
 
-    on_dp, on_tensor = ahead(ids_col[...])
+    on_dp, on_tensor = ahead(ids_col)
     row_of[...] = (on_tensor * dp_size + on_dp) * capacity + slot_col
     on_dp, on_tensor = ahead(ids_row[...])
     padded = -(-capacity // 16) * 16
@@ -107,7 +130,6 @@
     dp_size, _, capacity = sizes
     operands = (
         tokens,
-        expert_ids,
         expert_ids.reshape(1, count),
         norm_gain.reshape(1, features),
         router_weight.T,
@@ -116,11 +138,16 @@
         functools.partial(route_kernel, sizes),
         out_shape=[pltpu.VMEM((count, 1), I32)]
         + [pltpu.VMEM((capacity, features), BF16)] * dp_size,
-        in_specs=[pl.BlockSpec(memory_space=pltpu.SMEM)] + vmem_specs(len(operands)),
+        in_specs=[pl.BlockSpec(memory_space=pltpu.SMEM)]
+        + [pl.BlockSpec(memory_space=pl.ANY)] * len(operands),
         out_specs=vmem_specs(1 + dp_size),
-        scratch_shapes=[pltpu.VMEM((count, features), BF16)],
+        scratch_shapes=[pltpu.VMEM(x.shape, x.dtype) for x in operands]
+        + [
+            pltpu.VMEM((count, features), BF16),
+            pltpu.SemaphoreType.DMA((len(operands),)),
+        ],
         compiler_params=pltpu.CompilerParams(vmem_limit_bytes=VMEM_LIMIT),
-    )(place, *map(in_vmem, operands))
+    )(place, *map(in_hbm, operands))
 
 
 def load_kernel(*refs):
@@ -142,11 +169,8 @@
         in_specs=[pl.BlockSpec(memory_space=pl.ANY)] * len(arrays),
         out_specs=vmem_specs(len(arrays)),
         scratch_shapes=[pltpu.SemaphoreType.DMA((len(arrays),))],
-        cost_estimate=pl.CostEstimate(
-            flops=0, bytes_accessed=2 * sum(x.size * 2 for x in arrays), transcendentals=0
-        ),
         compiler_params=pltpu.CompilerParams(vmem_limit_bytes=VMEM_LIMIT),
-    )(*arrays)
+    )(*map(in_hbm, arrays))
 
 
 def expert_kernel(groups, *refs):
@@ -189,11 +213,6 @@
         out_specs=vmem_specs(len(groups)),
         scratch_shapes=[pltpu.VMEM((total, 2 * units), F32), pltpu.VMEM((total, units), BF16)],
         compiler_params=pltpu.CompilerParams(vmem_limit_bytes=VMEM_LIMIT),
-        cost_estimate=pl.CostEstimate(
-            flops=6 * total * features * units,
-            bytes_accessed=6 * features * units + 4 * total * features,
-            transcendentals=total * units,
-        ),
     )(*operands)
 
 
@@ -256,29 +275,33 @@
     apply = functools.partial(expert_apply, gate=gate, up=up, down=down)
     other = swap(mine)
     own_part, other_part = apply((1, 1), [mine, other])
-    far, near = after(ring_step(mine), own_part), ring_step(other)
-    parts = []
-    for k in range(1, half):
-        part = apply((2, 1, 1), [far, near, swap(far), swap(near)])
-        far = ring_step(far)
-        if k < half - 1:
-            near = after(ring_step(near), part[0])
-        parts.append(part)
-    last_kept, last_sent = apply((1, 1), [after(far, parts[-1][0]), swap(far)])
-
-    near_sum, far_sum = None, None
+    base = (own_part, swap(other_part))
+    far, near = after(ring_step(mine, "far_rows"), own_part), ring_step(other, "near_rows")
+    near_terms, far_terms = [], []
+    for k in range(1, half - 1):
+        far_out, near_out, near_part, far_part = apply(
+            (1, 1, 1, 1), [far, near, swap(far), swap(near)]
+        )
+        far = after(ring_step(far, "far_rows"), near, *(near_terms + far_terms)[-1:], *base)
+        near = after(ring_step(near, "near_rows"), far_out)
+        near_terms.append((near_part, swap(far_out)))
+        far_terms.append((far_part, swap(near_out)))
+    far_out, near_part = apply((1, 1), [far, swap(far)])
+    far = after(ring_step(far, "far_rows"), near, far_out, *near_terms[-1], *far_terms[-1])
+    near_terms.append((near_part, swap(far_out)))
+    near_out, far_part, last_part, last_out = apply(
+        (1, 1, 1, 1), [near, swap(near), after(far, *near_terms[-1]), swap(far)]
+    )
+    far_terms.append((far_part, swap(near_out)))
+
+    far_sum, near_sum = add(last_part, swap(last_out)), None
     for k in range(half - 1, 0, -1):
-        sent, near_part, far_part = parts[k - 1]
-        theirs = swap(sent)
-        if near_sum is None:
-            near_term = add(near_part, theirs[:rows])
-            far_sum = ring_step(add(last_kept, swap(last_sent)))
-        else:
-            near_term = add(near_sum, near_part, theirs[:rows])
-        near_sum = ring_step(near_term)
-        far_sum = ring_step(add(after(far_sum, near_term), far_part, theirs[rows:]))
-    near_term = swap(add(near_sum, other_part))
-    slot_out = add(after(far_sum, near_term), own_part, near_term)
+        part, theirs = near_terms[k - 1]
+        part = after(part, far_sum)
+        near_sum = add(part, theirs) if near_sum is None else add(near_sum, part, theirs)
+        near_sum = (ring_step if k > 1 else ring_leave)(near_sum, "near_sum")
+        far_sum = add(ring_step(far_sum, "far_sum"), *far_terms[k - 1])
+    slot_out = add(ring_step(far_sum, "far_sum"), near_sum, *base)
 
     returned = [slot_out[:capacity]]
     for j in range(1, dp_size):

time: 138 us -> 133 us (0.964)
  local copies, waits for them, and re-layouts: 10.8 us -> 0.13 us
  Pallas kernels: 22.9 us -> 27.9 us
    unnamed x15 -> x0, local copies, waits for them, and re-layouts: 10.7 us -> none
    ppermute x14 -> x13, waiting for transfers between devices: 52 us -> 48.2 us  [ring_step(): return lax.ppermute(values, 'expert', pairs)]
    pallas_call x1, Pallas kernels: 0.81 us -> 4.45 us  [load(): pl.pallas_call(load_kernel, out_shape=[pltpu.VMEM(x.shape, x.dtype) for x...]
    ppermute x10, waiting for transfers between devices: 18.6 us -> 20.8 us  [shift(): lax.ppermute(values, axis, [(i, (i + steps) % size) for i in range(size)])]
    ppermute x0 -> x1, waiting for transfers between devices: none -> 2.15 us  [ring_leave(): return lax.ppermute(values, 'expert', pairs)]
    pallas_call x1, Pallas kernels: 2.12 us -> 3.5 us  [route(): pl.pallas_call(functools.partial(route_kernel, sizes), out_shape=[pltpu.V...]
    ppermute x13 -> x16, waiting for transfers between devices: 4.11 us -> 2.82 us  [swap(): return lax.ppermute(values, 'expert', [(i, i ^ 1) for i in range(size)])]
    ppermute x13 -> x16, starting transfers between devices: 6.59 us -> 7.75 us  [swap(): return lax.ppermute(values, 'expert', [(i, i ^ 1) for i in range(size)])]
  transfers between devices with their start and end apart: 37 -> 40, of which waited for: 22 -> 23; matrix products, arithmetic and copies ran while one was open for 1% -> 1% of each run, Pallas kernels for 12% -> 14%
where the time goes in v2:
time: 133 us; the launch traced here: 132 us
  waiting for transfers between devices  74 us (56%)
  starting transfers between devices  28 us (21%)
  Pallas kernels  27.9 us (21%)
  other arithmetic  1.59 us (1%)
    ppermute x13, waiting for transfers between devices, ring_step(): return lax.ppermute(values, 'expert', pairs)  48.2 us
    ppermute x10, waiting for transfers between devices, shift(): lax.ppermute(values, axis, [(i, (i + steps) % size) for i in range(size)])  20.8 us
    pallas_call x5, Pallas kernels, expert_apply(): pl.pallas_call(functools.partial(expert_kernel, groups), out_shape=[pltpu...  18.6 us
    ppermute x10, starting transfers between devices, shift(): lax.ppermute(values, axis, [(i, (i + steps) % size) for i in range(size)])  14.5 us
    ppermute x16, starting transfers between devices, swap(): return lax.ppermute(values, 'expert', [(i, i ^ 1) for i in range(size)])  7.75 us
    ppermute x13, starting transfers between devices, ring_step(): return lax.ppermute(values, 'expert', pairs)  5.63 us
    pallas_call x1, Pallas kernels, load(): pl.pallas_call(load_kernel, out_shape=[pltpu.VMEM(x.shape, x.dtype) for x...  4.45 us
    pallas_call x1, Pallas kernels, route(): pl.pallas_call(functools.partial(route_kernel, sizes), out_shape=[pltpu.V...  3.5 us
  transfers between devices with their start and end apart: 40, of which 23 were waited for; matrix products, arithmetic and copies ran while one was open for 1% of the time, Pallas kernels for 14%

profile of v2, /device:TPU:6, one launch (start us, length us, event | category | flops | bytes accessed | tf_op | source)
XLA Modules:
  0.0 132.0 jit_solution(7357211150947209616)
XLA Ops:
  0.1 3.5 %shard_map.73 = (s32[128,1]{1,0:T(8,128)S(1)}, bf16[10,5120]{1,0:T(8,128)(2,1)S(1)}, bf16[10,5120]{1,0:T(8,128)(2,1)S(1)}, bf16[10,5120]{1,0:T(8,128)(2,1)S(1)}, bf16[10,5120]{1,0:T(8,128)(2,1)S(1)}) custom-call(s32[2]{0:T(128)S(1)} %pad_add_fusion.place, bf16[128,5120]{1,0:T(8,128)(2,1)} %refs_0_.1, s32[1,128]{1,0:T(1,128)} %bitcast.13, ...), custom_call_target="tpu_custom_call" | custom-call | tf_op jit(solution)/shard_map/pallas_call | solution.py:137
  4.5 2.4 %collective-permute-start = (bf16[10,5120]{1,0:T(8,128)(2,1)S(1)}, bf16[10,5120]{1,0:T(8,128)(2,1)S(1)}, u32[]{:S(2)}, u32[]{:S(2)}) collective-permute-start(bf16[10,5120]{1,0:T(8,128)(2,1)S(1)} %get-tuple-element.42), channel_id=1, source_target_pairs={{0,64},{64,128},{128,192},{192,0},{1,65},{65,129},{129,193},{193,1... | collective-permute-start | bytes 307208 | tf_op jit(solution)/shard_map/ppermute | solution.py:42
  7.3 4.5 %shard_map.74 = (bf16[5120,384]{1,0:T(8,128)(2,1)S(1)}, bf16[5120,384]{1,0:T(8,128)(2,1)S(1)}, bf16[384,5120]{1,0:T(8,128)(2,1)S(1)}) custom-call(bf16[5120,384]{1,0:T(8,128)(2,1)} %bitcast.8, bf16[5120,384]{1,0:T(8,128)(2,1)} %bitcast.9, bf16[384,5120]{1,0:T(8,128)(2,1)} %bitcast.10), custom_call_target="tpu_custom_call" | custom-call | tf_op jit(solution)/shard_map/pallas_call | solution.py:166
  11.8 2.5 %collective-permute-done.2 = bf16[10,5120]{1,0:T(8,128)(2,1)S(1)} collective-permute-done((bf16[10,5120]{1,0:T(8,128)(2,1)S(1)}, bf16[10,5120]{1,0:T(8,128)(2,1)S(1)}, u32[]{:S(2)}, u32[]{:S(2)}) %collective-permute-start.2) | collective-permute-done | bytes 102432 | tf_op jit(solution)/shard_map/ppermute | solution.py:42
  14.6 2.0 %collective-permute-start.6 = (bf16[40,5120]{1,0:T(8,128)(2,1)S(1)}, bf16[40,5120]{1,0:T(8,128)(2,1)S(1)}, u32[]{:S(2)}, u32[]{:S(2)}) collective-permute-start(bf16[40,5120]{1,0:T(8,128)(2,1)S(1)} %pad_maximum_fusion.refs_0_), channel_id=1, source_target_pairs={{0,2},{1,15},{2,4},{3,1},{4,6},{5,3},{6,8},{7,5},{8,10},{9,7},{10,... | collective-permute-start | bytes 1228808 | tf_op jit(solution)/shard_map/far_rows/ppermute | solution.py:49
  16.6 1.9 %collective-permute-start.4 = (bf16[40,5120]{1,0:T(8,128)(2,1)S(1)}, bf16[40,5120]{1,0:T(8,128)(2,1)S(1)}, u32[]{:S(2)}, u32[]{:S(2)}) collective-permute-start(bf16[40,5120]{1,0:T(8,128)(2,1)S(1)} %collective-permute-done.3.refs_1_), channel_id=1, source_target_pairs={{0,2},{1,15},{2,4},{3,1},{4,6},{5,3},{6,8},{7,5},{8,10},{9,7},{10,... | collective-permute-start | bytes 1228808 | tf_op jit(solution)/shard_map/near_rows/ppermute | solution.py:49
  18.5 3.4 %shard_map.75 = (bf16[40,5120]{1,0:T(8,128)(2,1)S(1)}, bf16[40,5120]{1,0:T(8,128)(2,1)S(1)}) custom-call(bf16[40,5120]{1,0:T(8,128)(2,1)S(1)} %pad_maximum_fusion.refs_0_, bf16[40,5120]{1,0:T(8,128)(2,1)S(1)} %collective-permute-done.3.refs_1_, bf16[5120,384]{1,0:T(8,128)(2,1)S(1)} %get-tuple-element.45.refs_2_.refs_4_, ...), custom_call_target="tpu_custom_call" | custom-call | tf_op jit(solution)/shard_map/pallas_call | solution.py:209
  21.9 4.6 %collective-permute-done.6.refs_0_ = bf16[40,5120]{1,0:T(8,128)(2,1)S(1)} collective-permute-done((bf16[40,5120]{1,0:T(8,128)(2,1)S(1)}, bf16[40,5120]{1,0:T(8,128)(2,1)S(1)}, u32[]{:S(2)}, u32[]{:S(2)}) %collective-permute-start.6) | collective-permute-done | bytes 409632 | tf_op jit(solution)/shard_map/far_rows/ppermute | solution.py:49
  26.5 2.2 %collective-permute-start.11 = (bf16[40,5120]{1,0:T(8,128)(2,1)S(1)}, bf16[40,5120]{1,0:T(8,128)(2,1)S(1)}, u32[]{:S(2)}, u32[]{:S(2)}) collective-permute-start(bf16[40,5120]{1,0:T(8,128)(2,1)S(1)} %get-tuple-element.53), channel_id=1, source_target_pairs={{0,1},{1,0},{2,3},{3,2},{4,5},{5,4},{6,7},{7,6},{8,9},{9,8},{10,11... | collective-permute-start | bytes 1228808 | tf_op jit(solution)/shard_map/other_core/ppermute | solution.py:62
  28.7 2.2 %collective-permute-done.4.refs_1_ = bf16[40,5120]{1,0:T(8,128)(2,1)S(1)} collective-permute-done((bf16[40,5120]{1,0:T(8,128)(2,1)S(1)}, bf16[40,5120]{1,0:T(8,128)(2,1)S(1)}, u32[]{:S(2)}, u32[]{:S(2)}) %collective-permute-start.4) | collective-permute-done | bytes 409632 | tf_op jit(solution)/shard_map/near_rows/ppermute | solution.py:49
  30.9 4.8 %collective-permute-done.10.refs_0_ = bf16[40,5120]{1,0:T(8,128)(2,1)S(1)} collective-permute-done((bf16[40,5120]{1,0:T(8,128)(2,1)S(1)}, bf16[40,5120]{1,0:T(8,128)(2,1)S(1)}, u32[]{:S(2)}, u32[]{:S(2)}) %collective-permute-start.10) | collective-permute-done | bytes 409632 | tf_op jit(solution)/shard_map/far_rows/ppermute | solution.py:49
  35.7 3.9 %shard_map.76 = (bf16[40,5120]{1,0:T(8,128)(2,1)S(1)}, bf16[40,5120]{1,0:T(8,128)(2,1)S(1)}, bf16[40,5120]{1,0:T(8,128)(2,1)S(1)}, bf16[40,5120]{1,0:T(8,128)(2,1)S(1)}) custom-call(bf16[40,5120]{1,0:T(8,128)(2,1)S(1)} %collective-permute-done.6.refs_0_, bf16[40,5120]{1,0:T(8,128)(2,1)S(1)} %collective-permute-done.4.refs_1_, ...), custom_call_target="tpu_custom_call" | custom-call | tf_op jit(solution)/shard_map/pallas_call | solution.py:209
  39.6 1.9 %collective-permute-start.16 = (bf16[40,5120]{1,0:T(8,128)(2,1)S(1)}, bf16[40,5120]{1,0:T(8,128)(2,1)S(1)}, u32[]{:S(2)}, u32[]{:S(2)}) collective-permute-start(bf16[40,5120]{1,0:T(8,128)(2,1)S(1)} %get-tuple-element.58), channel_id=1, source_target_pairs={{0,1},{1,0},{2,3},{3,2},{4,5},{5,4},{6,7},{7,6},{8,9},{9,8},{10,11... | collective-permute-start | bytes 1228808 | tf_op jit(solution)/shard_map/other_core/ppermute | solution.py:62
  42.1 2.8 %collective-permute-done.15.refs_0_ = bf16[40,5120]{1,0:T(8,128)(2,1)S(1)} collective-permute-done((bf16[40,5120]{1,0:T(8,128)(2,1)S(1)}, bf16[40,5120]{1,0:T(8,128)(2,1)S(1)}, u32[]{:S(2)}, u32[]{:S(2)}) %collective-permute-start.15) | collective-permute-done | bytes 409632 | tf_op jit(solution)/shard_map/far_rows/ppermute | solution.py:49
  44.9 4.0 %shard_map.77 = (bf16[40,5120]{1,0:T(8,128)(2,1)S(1)}, bf16[40,5120]{1,0:T(8,128)(2,1)S(1)}, bf16[40,5120]{1,0:T(8,128)(2,1)S(1)}, bf16[40,5120]{1,0:T(8,128)(2,1)S(1)}) custom-call(bf16[40,5120]{1,0:T(8,128)(2,1)S(1)} %collective-permute-done.10.refs_0_, bf16[40,5120]{1,0:T(8,128)(2,1)S(1)} %collective-permute-done.5.refs_1_, ...), custom_call_target="tpu_custom_call" | custom-call | tf_op jit(solution)/shard_map/pallas_call | solution.py:209
  51.2 3.4 %shard_map.78 = (bf16[40,5120]{1,0:T(8,128)(2,1)S(1)}, bf16[40,5120]{1,0:T(8,128)(2,1)S(1)}) custom-call(bf16[40,5120]{1,0:T(8,128)(2,1)S(1)} %collective-permute-done.15.refs_0_, bf16[40,5120]{1,0:T(8,128)(2,1)S(1)} %collective-permute-done.18.refs_1_, bf16[5120,384]{1,0:T(8,128)(2,1)S(1)} %get-tuple-element.45.refs_2_.refs_4_, ...), custom_call_target="tpu_custom_call" | custom-call | tf_op jit(solution)/shard_map/pallas_call | solution.py:209
  57.4 3.9 %shard_map.79 = (bf16[40,5120]{1,0:T(8,128)(2,1)S(1)}, bf16[40,5120]{1,0:T(8,128)(2,1)S(1)}, bf16[40,5120]{1,0:T(8,128)(2,1)S(1)}, bf16[40,5120]{1,0:T(8,128)(2,1)S(1)}) custom-call(bf16[40,5120]{1,0:T(8,128)(2,1)S(1)} %collective-permute-done.9.refs_0_, bf16[40,5120]{1,0:T(8,128)(2,1)S(1)} %collective-permute-done.14.refs_1_, ...), custom_call_target="tpu_custom_call" | custom-call | tf_op jit(solution)/shard_map/pallas_call | solution.py:209
  64.5 8.0 %collective-permute-done.24 = bf16[40,5120]{1,0:T(8,128)(2,1)S(1)} collective-permute-done((bf16[40,5120]{1,0:T(8,128)(2,1)S(1)}, bf16[40,5120]{1,0:T(8,128)(2,1)S(1)}, u32[]{:S(2)}, u32[]{:S(2)}) %collective-permute-start.24) | collective-permute-done | bytes 409632 | tf_op jit(solution)/shard_map/far_sum/ppermute | solution.py:49
  72.7 4.1 %collective-permute-done.29 = bf16[40,5120]{1,0:T(8,128)(2,1)S(1)} collective-permute-done((bf16[40,5120]{1,0:T(8,128)(2,1)S(1)}, bf16[40,5120]{1,0:T(8,128)(2,1)S(1)}, u32[]{:S(2)}, u32[]{:S(2)}) %collective-permute-start.29) | collective-permute-done | bytes 409632 | tf_op jit(solution)/shard_map/near_sum/ppermute | solution.py:49
  77.1 4.8 %collective-permute-done.26 = bf16[40,5120]{1,0:T(8,128)(2,1)S(1)} collective-permute-done((bf16[40,5120]{1,0:T(8,128)(2,1)S(1)}, bf16[40,5120]{1,0:T(8,128)(2,1)S(1)}, u32[]{:S(2)}, u32[]{:S(2)}) %collective-permute-start.26) | collective-permute-done | bytes 409632 | tf_op jit(solution)/shard_map/far_sum/ppermute | solution.py:49
  82.4 3.9 %collective-permute-done.30 = bf16[40,5120]{1,0:T(8,128)(2,1)S(1)} collective-permute-done((bf16[40,5120]{1,0:T(8,128)(2,1)S(1)}, bf16[40,5120]{1,0:T(8,128)(2,1)S(1)}, u32[]{:S(2)}, u32[]{:S(2)}) %collective-permute-start.30) | collective-permute-done | bytes 409632 | tf_op jit(solution)/shard_map/near_sum/ppermute | solution.py:49
  86.5 5.0 %collective-permute-done.27 = bf16[40,5120]{1,0:T(8,128)(2,1)S(1)} collective-permute-done((bf16[40,5120]{1,0:T(8,128)(2,1)S(1)}, bf16[40,5120]{1,0:T(8,128)(2,1)S(1)}, u32[]{:S(2)}, u32[]{:S(2)}) %collective-permute-start.27) | collective-permute-done | bytes 409632 | tf_op jit(solution)/shard_map/far_sum/ppermute | solution.py:49
  91.7 2.1 %collective-permute-done.32 = bf16[40,5120]{1,0:T(8,128)(2,1)S(1)} collective-permute-done((bf16[40,5120]{1,0:T(8,128)(2,1)S(1)}, bf16[40,5120]{1,0:T(8,128)(2,1)S(1)}, u32[]{:S(2)}, u32[]{:S(2)}) %collective-permute-start.32) | collective-permute-done | bytes 409632 | tf_op jit(solution)/shard_map/near_sum/ppermute | solution.py:56
  93.9 7.0 %collective-permute-done.28 = bf16[40,5120]{1,0:T(8,128)(2,1)S(1)} collective-permute-done((bf16[40,5120]{1,0:T(8,128)(2,1)S(1)}, bf16[40,5120]{1,0:T(8,128)(2,1)S(1)}, u32[]{:S(2)}, u32[]{:S(2)}) %collective-permute-start.28) | collective-permute-done | bytes 409632 | tf_op jit(solution)/shard_map/far_sum/ppermute | solution.py:49
  101.2 3.0 %collective-permute-start.35 = (bf16[10,5120]{1,0:T(8,128)(2,1)S(1)}, bf16[10,5120]{1,0:T(8,128)(2,1)S(1)}, u32[]{:S(2)}, u32[]{:S(2)}) collective-permute-start(bf16[10,5120]{1,0:T(8,128)(2,1)S(1)} %get-tuple-element.76), channel_id=1, source_target_pairs={{0,64},{64,128},{128,192},{192,0},{1,65},{65,129},{129,193},{193,1... | collective-permute-start | bytes 307208 | tf_op jit(solution)/shard_map/ppermute | solution.py:42
  105.2 3.7 %collective-permute-done.35 = bf16[10,5120]{1,0:T(8,128)(2,1)S(1)} collective-permute-done((bf16[10,5120]{1,0:T(8,128)(2,1)S(1)}, bf16[10,5120]{1,0:T(8,128)(2,1)S(1)}, u32[]{:S(2)}, u32[]{:S(2)}) %collective-permute-start.35) | collective-permute-done | bytes 102432 | tf_op jit(solution)/shard_map/ppermute | solution.py:42
  108.9 2.3 %collective-permute-done.34 = bf16[10,5120]{1,0:T(8,128)(2,1)S(1)} collective-permute-done((bf16[10,5120]{1,0:T(8,128)(2,1)S(1)}, bf16[10,5120]{1,0:T(8,128)(2,1)S(1)}, u32[]{:S(2)}, u32[]{:S(2)}) %collective-permute-start.34) | collective-permute-done | bytes 102432 | tf_op jit(solution)/shard_map/ppermute | solution.py:42
  112.7 1.7 %collective-permute-start.38 = (bf16[40,5120]{1,0:T(8,128)(2,1)S(1)}, bf16[40,5120]{1,0:T(8,128)(2,1)S(1)}, u32[]{:S(2)}, u32[]{:S(2)}) collective-permute-start(bf16[40,5120]{1,0:T(8,128)(2,1)S(1)} %pad_maximum_fusion.1.refs_0_), channel_id=1, source_target_pairs={{0,16},{16,32},{32,48},{48,0},{1,17},{17,33},{33,49},{49,1},{2,18}... | collective-permute-start | bytes 1228808 | tf_op jit(solution)/shard_map/ppermute | solution.py:42
  116.0 7.0 %collective-permute-done.38.refs_4_ = bf16[40,5120]{1,0:T(8,128)(2,1)S(1)} collective-permute-done((bf16[40,5120]{1,0:T(8,128)(2,1)S(1)}, bf16[40,5120]{1,0:T(8,128)(2,1)S(1)}, u32[]{:S(2)}, u32[]{:S(2)}) %collective-permute-start.38) | collective-permute-done | bytes 409632 | tf_op jit(solution)/shard_map/ppermute | solution.py:42
  123.0 1.7 %collective-permute-start.39 = (bf16[24,5120]{1,0:T(8,128)(2,1)S(1)}, bf16[24,5120]{1,0:T(8,128)(2,1)S(1)}, u32[]{:S(2)}, u32[]{:S(2)}) collective-permute-start(bf16[24,5120]{1,0:T(8,128)(2,1)S(1)} %slice.29), channel_id=1, source_target_pairs={{0,16},{16,32},{32,48},{48,0},{1,17},{17,33},{33,49},{49,1},{2,18}... | collective-permute-start | bytes 737288 | tf_op jit(solution)/shard_map/ppermute | solution.py:42
  124.8 1.7 %collective-permute-start.37 = (bf16[16,5120]{1,0:T(8,128)(2,1)S(1)}, bf16[16,5120]{1,0:T(8,128)(2,1)S(1)}, u32[]{:S(2)}, u32[]{:S(2)}) collective-permute-start(bf16[16,5120]{1,0:T(8,128)(2,1)S(1)} %slice.28), channel_id=1, source_target_pairs={{0,48},{16,0},{32,16},{48,32},{1,49},{17,1},{33,17},{49,33},{2,50}... | collective-permute-start | bytes 491528 | tf_op jit(solution)/shard_map/ppermute | solution.py:42
  126.5 3.7 %collective-permute-done.37.refs_2_ = bf16[16,5120]{1,0:T(8,128)(2,1)S(1)} collective-permute-done((bf16[16,5120]{1,0:T(8,128)(2,1)S(1)}, bf16[16,5120]{1,0:T(8,128)(2,1)S(1)}, u32[]{:S(2)}, u32[]{:S(2)}) %collective-permute-start.37) | collective-permute-done | bytes 163872 | tf_op jit(solution)/shard_map/ppermute | solution.py:42
  (70 shorter events, 18.2 us)
Async XLA Ops:
  3.6 10.7 %collective-permute-start.2 = (bf16[10,5120]{1,0:T(8,128)(2,1)S(1)}, bf16[10,5120]{1,0:T(8,128)(2,1)S(1)}, u32[]{:S(2)}, u32[]{:S(2)}) collective-permute-start(bf16[10,5120]{1,0:T(8,128)(2,1)S(1)} %get-tuple-element.44), channel_id=1, source_target_pairs={{0,192},{64,0},{128,64},{192,128},{1,193},{65,1},{129,65},{193,129... | collective-permute-start | bytes 307208 | tf_op jit(solution)/shard_map/ppermute | solution.py:42
  4.5 9.8 %collective-permute-start = (bf16[10,5120]{1,0:T(8,128)(2,1)S(1)}, bf16[10,5120]{1,0:T(8,128)(2,1)S(1)}, u32[]{:S(2)}, u32[]{:S(2)}) collective-permute-start(bf16[10,5120]{1,0:T(8,128)(2,1)S(1)} %get-tuple-element.42), channel_id=1, source_target_pairs={{0,64},{64,128},{128,192},{192,0},{1,65},{65,129},{129,193},{193,1... | collective-permute-start | bytes 307208 | tf_op jit(solution)/shard_map/ppermute | solution.py:42
  6.9 7.4 %collective-permute-start.1 = (bf16[10,5120]{1,0:T(8,128)(2,1)S(1)}, bf16[10,5120]{1,0:T(8,128)(2,1)S(1)}, u32[]{:S(2)}, u32[]{:S(2)}) collective-permute-start(bf16[10,5120]{1,0:T(8,128)(2,1)S(1)} %get-tuple-element.43), channel_id=1, source_target_pairs={{0,128},{64,192},{128,0},{192,64},{1,129},{65,193},{129,1},{193,65... | collective-permute-start | bytes 307208 | tf_op jit(solution)/shard_map/ppermute | solution.py:42
  14.6 11.9 %collective-permute-start.6 = (bf16[40,5120]{1,0:T(8,128)(2,1)S(1)}, bf16[40,5120]{1,0:T(8,128)(2,1)S(1)}, u32[]{:S(2)}, u32[]{:S(2)}) collective-permute-start(bf16[40,5120]{1,0:T(8,128)(2,1)S(1)} %pad_maximum_fusion.refs_0_), channel_id=1, source_target_pairs={{0,2},{1,15},{2,4},{3,1},{4,6},{5,3},{6,8},{7,5},{8,10},{9,7},{10,... | collective-permute-start | bytes 1228808 | tf_op jit(solution)/shard_map/far_rows/ppermute | solution.py:49
  16.6 14.3 %collective-permute-start.4 = (bf16[40,5120]{1,0:T(8,128)(2,1)S(1)}, bf16[40,5120]{1,0:T(8,128)(2,1)S(1)}, u32[]{:S(2)}, u32[]{:S(2)}) collective-permute-start(bf16[40,5120]{1,0:T(8,128)(2,1)S(1)} %collective-permute-done.3.refs_1_), channel_id=1, source_target_pairs={{0,2},{1,15},{2,4},{3,1},{4,6},{5,3},{6,8},{7,5},{8,10},{9,7},{10,... | collective-permute-start | bytes 1228808 | tf_op jit(solution)/shard_map/near_rows/ppermute | solution.py:49
  26.5 9.2 %collective-permute-start.10 = (bf16[40,5120]{1,0:T(8,128)(2,1)S(1)}, bf16[40,5120]{1,0:T(8,128)(2,1)S(1)}, u32[]{:S(2)}, u32[]{:S(2)}) collective-permute-start(bf16[40,5120]{1,0:T(8,128)(2,1)S(1)} %collective-permute-done.6.refs_0_), channel_id=1, source_target_pairs={{0,2},{1,15},{2,4},{3,1},{4,6},{5,3},{6,8},{7,5},{8,10},{9,7},{10,... | collective-permute-start | bytes 1228808 | tf_op jit(solution)/shard_map/far_rows/ppermute | solution.py:49
  26.5 9.2 %collective-permute-start.11 = (bf16[40,5120]{1,0:T(8,128)(2,1)S(1)}, bf16[40,5120]{1,0:T(8,128)(2,1)S(1)}, u32[]{:S(2)}, u32[]{:S(2)}) collective-permute-start(bf16[40,5120]{1,0:T(8,128)(2,1)S(1)} %get-tuple-element.53), channel_id=1, source_target_pairs={{0,1},{1,0},{2,3},{3,2},{4,5},{5,4},{6,7},{7,6},{8,9},{9,8},{10,11... | collective-permute-start | bytes 1228808 | tf_op jit(solution)/shard_map/other_core/ppermute | solution.py:62
  28.7 6.9 %collective-permute-start.7 = (bf16[40,5120]{1,0:T(8,128)(2,1)S(1)}, bf16[40,5120]{1,0:T(8,128)(2,1)S(1)}, u32[]{:S(2)}, u32[]{:S(2)}) collective-permute-start(bf16[40,5120]{1,0:T(8,128)(2,1)S(1)} %collective-permute-done.6.refs_0_), channel_id=1, source_target_pairs={{0,1},{1,0},{2,3},{3,2},{4,5},{5,4},{6,7},{7,6},{8,9},{9,8},{10,11... | collective-permute-start | bytes 1228808 | tf_op jit(solution)/shard_map/other_core/ppermute | solution.py:62
  30.9 10.8 %collective-permute-start.5 = (bf16[40,5120]{1,0:T(8,128)(2,1)S(1)}, bf16[40,5120]{1,0:T(8,128)(2,1)S(1)}, u32[]{:S(2)}, u32[]{:S(2)}) collective-permute-start(bf16[40,5120]{1,0:T(8,128)(2,1)S(1)} %collective-permute-done.4.refs_1_), channel_id=1, source_target_pairs={{0,2},{1,15},{2,4},{3,1},{4,6},{5,3},{6,8},{7,5},{8,10},{9,7},{10,... | collective-permute-start | bytes 1228808 | tf_op jit(solution)/shard_map/near_rows/ppermute | solution.py:49
  35.7 9.2 %collective-permute-start.15 = (bf16[40,5120]{1,0:T(8,128)(2,1)S(1)}, bf16[40,5120]{1,0:T(8,128)(2,1)S(1)}, u32[]{:S(2)}, u32[]{:S(2)}) collective-permute-start(bf16[40,5120]{1,0:T(8,128)(2,1)S(1)} %collective-permute-done.10.refs_0_), channel_id=1, source_target_pairs={{0,2},{1,15},{2,4},{3,1},{4,6},{5,3},{6,8},{7,5},{8,10},{9,7},{10,... | collective-permute-start | bytes 1228808 | tf_op jit(solution)/shard_map/far_rows/ppermute | solution.py:49
  39.6 5.2 %collective-permute-start.16 = (bf16[40,5120]{1,0:T(8,128)(2,1)S(1)}, bf16[40,5120]{1,0:T(8,128)(2,1)S(1)}, u32[]{:S(2)}, u32[]{:S(2)}) collective-permute-start(bf16[40,5120]{1,0:T(8,128)(2,1)S(1)} %get-tuple-element.58), channel_id=1, source_target_pairs={{0,1},{1,0},{2,3},{3,2},{4,5},{5,4},{6,7},{7,6},{8,9},{9,8},{10,11... | collective-permute-start | bytes 1228808 | tf_op jit(solution)/shard_map/other_core/ppermute | solution.py:62
  42.1 9.2 %collective-permute-start.9 = (bf16[40,5120]{1,0:T(8,128)(2,1)S(1)}, bf16[40,5120]{1,0:T(8,128)(2,1)S(1)}, u32[]{:S(2)}, u32[]{:S(2)}) collective-permute-start(bf16[40,5120]{1,0:T(8,128)(2,1)S(1)} %collective-permute-done.5.refs_1_), channel_id=1, source_target_pairs={{0,2},{1,15},{2,4},{3,1},{4,6},{5,3},{6,8},{7,5},{8,10},{9,7},{10,... | collective-permute-start | bytes 1228808 | tf_op jit(solution)/shard_map/near_rows/ppermute | solution.py:49
  44.8 6.4 %collective-permute-start.18 = (bf16[40,5120]{1,0:T(8,128)(2,1)S(1)}, bf16[40,5120]{1,0:T(8,128)(2,1)S(1)}, u32[]{:S(2)}, u32[]{:S(2)}) collective-permute-start(bf16[40,5120]{1,0:T(8,128)(2,1)S(1)} %collective-permute-done.15.refs_0_), channel_id=1, source_target_pairs={{0,1},{1,0},{2,3},{3,2},{4,5},{5,4},{6,7},{7,6},{8,9},{9,8},{10,11... | collective-permute-start | bytes 1228808 | tf_op jit(solution)/shard_map/other_core/ppermute | solution.py:62
  44.8 10.8 %collective-permute-start.17 = (bf16[40,5120]{1,0:T(8,128)(2,1)S(1)}, bf16[40,5120]{1,0:T(8,128)(2,1)S(1)}, u32[]{:S(2)}, u32[]{:S(2)}) collective-permute-start(bf16[40,5120]{1,0:T(8,128)(2,1)S(1)} %collective-permute-done.15.refs_0_), channel_id=1, source_target_pairs={{0,2},{1,15},{2,4},{3,1},{4,6},{5,3},{6,8},{7,5},{8,10},{9,7},{10,... | collective-permute-start | bytes 1228808 | tf_op jit(solution)/shard_map/far_rows/ppermute | solution.py:49
  48.8 6.8 %collective-permute-start.20 = (bf16[40,5120]{1,0:T(8,128)(2,1)S(1)}, bf16[40,5120]{1,0:T(8,128)(2,1)S(1)}, u32[]{:S(2)}, u32[]{:S(2)}) collective-permute-start(bf16[40,5120]{1,0:T(8,128)(2,1)S(1)} %get-tuple-element.63), channel_id=1, source_target_pairs={{0,1},{1,0},{2,3},{3,2},{4,5},{5,4},{6,7},{7,6},{8,9},{9,8},{10,11... | collective-permute-start | bytes 1228808 | tf_op jit(solution)/shard_map/other_core/ppermute | solution.py:62
  50.3 5.3 %collective-permute-start.19 = (bf16[40,5120]{1,0:T(8,128)(2,1)S(1)}, bf16[40,5120]{1,0:T(8,128)(2,1)S(1)}, u32[]{:S(2)}, u32[]{:S(2)}) collective-permute-start(bf16[40,5120]{1,0:T(8,128)(2,1)S(1)} %get-tuple-element.55), channel_id=1, source_target_pairs={{0,1},{1,0},{2,3},{3,2},{4,5},{5,4},{6,7},{7,6},{8,9},{9,8},{10,11... | collective-permute-start | bytes 1228808 | tf_op jit(solution)/shard_map/other_core/ppermute | solution.py:62
  51.2 5.4 %collective-permute-start.14 = (bf16[40,5120]{1,0:T(8,128)(2,1)S(1)}, bf16[40,5120]{1,0:T(8,128)(2,1)S(1)}, u32[]{:S(2)}, u32[]{:S(2)}) collective-permute-start(bf16[40,5120]{1,0:T(8,128)(2,1)S(1)} %collective-permute-done.9.refs_0_), channel_id=1, source_target_pairs={{0,1},{1,0},{2,3},{3,2},{4,5},{5,4},{6,7},{7,6},{8,9},{9,8},{10,11... | collective-permute-start | bytes 1228808 | tf_op jit(solution)/shard_map/other_core/ppermute | solution.py:62
  61.6 20.8 %collective-permute-start.31 = (bf16[40,5120]{1,0:T(8,128)(2,1)S(1)}, bf16[40,5120]{1,0:T(8,128)(2,1)S(1)}, u32[]{:S(2)}, u32[]{:S(2)}) collective-permute-start(bf16[40,5120]{1,0:T(8,128)(2,1)S(1)} %get-tuple-element.51), channel_id=1, source_target_pairs={{0,1},{1,0},{2,3},{3,2},{4,5},{5,4},{6,7},{7,6},{8,9},{9,8},{10,11... | collective-permute-start | bytes 1228808 | tf_op jit(solution)/shard_map/other_core/ppermute | solution.py:62
  63.2 9.2 %collective-permute-start.24 = (bf16[40,5120]{1,0:T(8,128)(2,1)S(1)}, bf16[40,5120]{1,0:T(8,128)(2,1)S(1)}, u32[]{:S(2)}, u32[]{:S(2)}) collective-permute-start(bf16[40,5120]{1,0:T(8,128)(2,1)S(1)} %add_convert_fusion.7), channel_id=1, source_target_pairs={{0,2},{1,15},{2,4},{3,1},{4,6},{5,3},{6,8},{7,5},{8,10},{9,7},{10,... | collective-permute-start | bytes 1228808 | tf_op jit(solution)/shard_map/far_sum/ppermute | solution.py:49
  63.5 13.4 %collective-permute-start.29 = (bf16[40,5120]{1,0:T(8,128)(2,1)S(1)}, bf16[40,5120]{1,0:T(8,128)(2,1)S(1)}, u32[]{:S(2)}, u32[]{:S(2)}) collective-permute-start(bf16[40,5120]{1,0:T(8,128)(2,1)S(1)} %add_convert_fusion.3), channel_id=1, source_target_pairs={{0,2},{1,15},{2,4},{3,1},{4,6},{5,3},{6,8},{7,5},{8,10},{9,7},{10,... | collective-permute-start | bytes 1228808 | tf_op jit(solution)/shard_map/near_sum/ppermute | solution.py:49
  72.6 9.2 %collective-permute-start.26 = (bf16[40,5120]{1,0:T(8,128)(2,1)S(1)}, bf16[40,5120]{1,0:T(8,128)(2,1)S(1)}, u32[]{:S(2)}, u32[]{:S(2)}) collective-permute-start(bf16[40,5120]{1,0:T(8,128)(2,1)S(1)} %add_convert_fusion.6), channel_id=1, source_target_pairs={{0,2},{1,15},{2,4},{3,1},{4,6},{5,3},{6,8},{7,5},{8,10},{9,7},{10,... | collective-permute-start | bytes 1228808 | tf_op jit(solution)/shard_map/far_sum/ppermute | solution.py:49
  77.0 9.2 %collective-permute-start.30 = (bf16[40,5120]{1,0:T(8,128)(2,1)S(1)}, bf16[40,5120]{1,0:T(8,128)(2,1)S(1)}, u32[]{:S(2)}, u32[]{:S(2)}) collective-permute-start(bf16[40,5120]{1,0:T(8,128)(2,1)S(1)} %add_convert_fusion.2), channel_id=1, source_target_pairs={{0,2},{1,15},{2,4},{3,1},{4,6},{5,3},{6,8},{7,5},{8,10},{9,7},{10,... | collective-permute-start | bytes 1228808 | tf_op jit(solution)/shard_map/near_sum/ppermute | solution.py:49
  82.0 9.5 %collective-permute-start.27 = (bf16[40,5120]{1,0:T(8,128)(2,1)S(1)}, bf16[40,5120]{1,0:T(8,128)(2,1)S(1)}, u32[]{:S(2)}, u32[]{:S(2)}) collective-permute-start(bf16[40,5120]{1,0:T(8,128)(2,1)S(1)} %add_convert_fusion.5), channel_id=1, source_target_pairs={{0,2},{1,15},{2,4},{3,1},{4,6},{5,3},{6,8},{7,5},{8,10},{9,7},{10,... | collective-permute-start | bytes 1228808 | tf_op jit(solution)/shard_map/far_sum/ppermute | solution.py:49
  86.4 7.5 %collective-permute-start.32 = (bf16[40,5120]{1,0:T(8,128)(2,1)S(1)}, bf16[40,5120]{1,0:T(8,128)(2,1)S(1)}, u32[]{:S(2)}, u32[]{:S(2)}) collective-permute-start(bf16[40,5120]{1,0:T(8,128)(2,1)S(1)} %add_convert_fusion.1), channel_id=1, source_target_pairs={{0,3},{1,14},{2,5},{3,0},{4,7},{5,2},{6,9},{7,4},{8,11},{9,6},{10,... | collective-permute-start | bytes 1228808 | tf_op jit(solution)/shard_map/near_sum/ppermute | solution.py:56
  91.6 9.2 %collective-permute-start.28 = (bf16[40,5120]{1,0:T(8,128)(2,1)S(1)}, bf16[40,5120]{1,0:T(8,128)(2,1)S(1)}, u32[]{:S(2)}, u32[]{:S(2)}) collective-permute-start(bf16[40,5120]{1,0:T(8,128)(2,1)S(1)} %add_convert_fusion.4), channel_id=1, source_target_pairs={{0,2},{1,15},{2,4},{3,1},{4,6},{5,3},{6,8},{7,5},{8,10},{9,7},{10,... | collective-permute-start | bytes 1228808 | tf_op jit(solution)/shard_map/far_sum/ppermute | solution.py:49
  101.2 7.7 %collective-permute-start.35 = (bf16[10,5120]{1,0:T(8,128)(2,1)S(1)}, bf16[10,5120]{1,0:T(8,128)(2,1)S(1)}, u32[]{:S(2)}, u32[]{:S(2)}) collective-permute-start(bf16[10,5120]{1,0:T(8,128)(2,1)S(1)} %get-tuple-element.76), channel_id=1, source_target_pairs={{0,64},{64,128},{128,192},{192,0},{1,65},{65,129},{129,193},{193,1... | collective-permute-start | bytes 307208 | tf_op jit(solution)/shard_map/ppermute | solution.py:42
  104.2 6.9 %collective-permute-start.34 = (bf16[10,5120]{1,0:T(8,128)(2,1)S(1)}, bf16[10,5120]{1,0:T(8,128)(2,1)S(1)}, u32[]{:S(2)}, u32[]{:S(2)}) collective-permute-start(bf16[10,5120]{1,0:T(8,128)(2,1)S(1)} %get-tuple-element.77), channel_id=1, source_target_pairs={{0,128},{64,192},{128,0},{192,64},{1,129},{65,193},{129,1},{193,65... | collective-permute-start | bytes 307208 | tf_op jit(solution)/shard_map/ppermute | solution.py:42
  104.2 8.3 %collective-permute-start.33 = (bf16[10,5120]{1,0:T(8,128)(2,1)S(1)}, bf16[10,5120]{1,0:T(8,128)(2,1)S(1)}, u32[]{:S(2)}, u32[]{:S(2)}) collective-permute-start(bf16[10,5120]{1,0:T(8,128)(2,1)S(1)} %get-tuple-element.78), channel_id=1, source_target_pairs={{0,192},{64,0},{128,64},{192,128},{1,193},{65,1},{129,65},{193,129... | collective-permute-start | bytes 307208 | tf_op jit(solution)/shard_map/ppermute | solution.py:42
  112.7 10.3 %collective-permute-start.38 = (bf16[40,5120]{1,0:T(8,128)(2,1)S(1)}, bf16[40,5120]{1,0:T(8,128)(2,1)S(1)}, u32[]{:S(2)}, u32[]{:S(2)}) collective-permute-start(bf16[40,5120]{1,0:T(8,128)(2,1)S(1)} %pad_maximum_fusion.1.refs_0_), channel_id=1, source_target_pairs={{0,16},{16,32},{32,48},{48,0},{1,17},{17,33},{33,49},{49,1},{2,18}... | collective-permute-start | bytes 1228808 | tf_op jit(solution)/shard_map/ppermute | solution.py:42
  114.4 10.4 %collective-permute-start.36 = (bf16[40,5120]{1,0:T(8,128)(2,1)S(1)}, bf16[40,5120]{1,0:T(8,128)(2,1)S(1)}, u32[]{:S(2)}, u32[]{:S(2)}) collective-permute-start(bf16[40,5120]{1,0:T(8,128)(2,1)S(1)} %pad_maximum_fusion.1.refs_0_), channel_id=1, source_target_pairs={{0,48},{16,0},{32,16},{48,32},{1,49},{17,1},{33,17},{49,33},{2,50}... | collective-permute-start | bytes 1228808 | tf_op jit(solution)/shard_map/ppermute | solution.py:42
  123.0 7.5 %collective-permute-start.39 = (bf16[24,5120]{1,0:T(8,128)(2,1)S(1)}, bf16[24,5120]{1,0:T(8,128)(2,1)S(1)}, u32[]{:S(2)}, u32[]{:S(2)}) collective-permute-start(bf16[24,5120]{1,0:T(8,128)(2,1)S(1)} %slice.29), channel_id=1, source_target_pairs={{0,16},{16,32},{32,48},{48,0},{1,17},{17,33},{33,49},{49,1},{2,18}... | collective-permute-start | bytes 737288 | tf_op jit(solution)/shard_map/ppermute | solution.py:42
  124.8 5.4 %collective-permute-start.37 = (bf16[16,5120]{1,0:T(8,128)(2,1)S(1)}, bf16[16,5120]{1,0:T(8,128)(2,1)S(1)}, u32[]{:S(2)}, u32[]{:S(2)}) collective-permute-start(bf16[16,5120]{1,0:T(8,128)(2,1)S(1)} %slice.28), channel_id=1, source_target_pairs={{0,48},{16,0},{32,16},{48,32},{1,49},{17,1},{33,17},{49,33},{2,50}... | collective-permute-start | bytes 491528 | tf_op jit(solution)/shard_map/ppermute | solution.py:42
  (8 other events, 21.5 us)

commit v3 on v2

--- a/solution.py
+++ b/solution.py
@@ -56,6 +56,16 @@
         return lax.ppermute(values, "expert", pairs)
 
 
+def tensor_step(values):
+    size, tensor_size = lax.axis_size("expert"), lax.axis_size("tensor")
+    pairs = [
+        (t * size + i, (t + (1 if i % 2 == 0 else -1)) % tensor_size * size + i)
+        for t in range(tensor_size)
+        for i in range(size)
+    ]
+    return lax.ppermute(values, ("tensor", "expert"), pairs)
+
+
 def swap(values):
     size = lax.axis_size("expert")
     with jax.named_scope("other_core"):
@@ -64,8 +74,8 @@
 
 def route_kernel(sizes, place, *refs):
     dp_size, tensor_size, capacity = sizes
-    sources, row_of, blocks = refs[:4], refs[4], refs[5 : 5 + dp_size]
-    tokens, ids_row, gain, router, normed, sems = refs[5 + dp_size :]
+    sources, row_of, packed = refs[:4], refs[4], refs[5]
+    tokens, ids_row, gain, router, normed, sems = refs[6:]
     copies = [
         pltpu.make_async_copy(source, held, sems.at[i])
         for i, (source, held) in enumerate(zip(sources, (tokens, ids_row, gain, router)))
@@ -107,22 +117,19 @@
         for d in range(1, dp_size):
             dp_of = dp_of + jnp.where(ids >= d * tensor_size, 1, 0)
         on_dp = dp_of - place[0]
-        on_tensor = ids - dp_of * tensor_size - place[1]
+        on_tensor = (ids - dp_of * tensor_size - place[1]) * place[2]
         on_dp = jnp.where(on_dp < 0, on_dp + dp_size, on_dp)
         return on_dp, jnp.where(on_tensor < 0, on_tensor + tensor_size, on_tensor)
 
     on_dp, on_tensor = ahead(ids_col)
     row_of[...] = (on_tensor * dp_size + on_dp) * capacity + slot_col
     on_dp, on_tensor = ahead(ids_row[...])
-    padded = -(-capacity // 16) * 16
-    target = jnp.where(on_tensor == 0, on_dp * padded + slot_row, -1)
-    row = lax.broadcasted_iota(I32, (dp_size * padded, count), 0)
+    target = jnp.where(on_tensor == 0, on_dp * capacity + slot_row, -1)
+    row = lax.broadcasted_iota(I32, (packed.shape[0], count), 0)
     picks = jnp.where(row == target, 1.0, 0.0).astype(BF16)
     for cols in spans:
         routed = (normed[:, cols].astype(F32) * gate).astype(BF16)
-        product = jnp.dot(picks, routed, preferred_element_type=F32)
-        for j, block in enumerate(blocks):
-            block[:, cols] = product[j * padded : j * padded + capacity].astype(BF16)
+        packed[:, cols] = jnp.dot(picks, routed, preferred_element_type=F32).astype(BF16)
 
 
 def route(sizes, place, tokens, expert_ids, norm_gain, router_weight):
@@ -136,11 +143,13 @@
     )
     return pl.pallas_call(
         functools.partial(route_kernel, sizes),
-        out_shape=[pltpu.VMEM((count, 1), I32)]
-        + [pltpu.VMEM((capacity, features), BF16)] * dp_size,
+        out_shape=[
+            pltpu.VMEM((count, 1), I32),
+            pltpu.VMEM((dp_size * capacity, features), BF16),
+        ],
         in_specs=[pl.BlockSpec(memory_space=pltpu.SMEM)]
         + [pl.BlockSpec(memory_space=pl.ANY)] * len(operands),
-        out_specs=vmem_specs(1 + dp_size),
+        out_specs=vmem_specs(2),
         scratch_shapes=[pltpu.VMEM(x.shape, x.dtype) for x in operands]
         + [
             pltpu.VMEM((count, features), BF16),
@@ -178,7 +187,7 @@
     pieces, (gate, up, down), outs = refs[:count], refs[count : count + 3], refs[count + 3 : -2]
     acts, hidden = refs[-2:]
     features, units = gate.shape
-    step = step_of(features, 1024)
+    step = step_of(features, 2560)
     acts[...] = jnp.zeros_like(acts)
 
     @pl.loop(0, features // step)
@@ -249,6 +258,13 @@
     )(*map(in_vmem, (row_of, *pieces)))
 
 
+def exchange(values, direction):
+    size = lax.axis_size("dp")
+    rows = values.shape[0] // size
+    blocks = [values[j * rows : (j + 1) * rows] for j in range(size)]
+    return blocks[:1] + [shift(blocks[j], "dp", direction * j) for j in range(1, size)]
+
+
 def after(values, *earlier):
     return lax.optimization_barrier((values, *earlier))[0]
 
@@ -260,23 +276,23 @@
     half = chips // 2
     capacity = 5 * tokens.shape[0] // (4 * dp_size * tensor_size)
     rows = dp_size * capacity
-    place = jnp.stack([lax.axis_index("dp"), lax.axis_index("tensor")]).astype(I32)
-
-    row_of, *outgoing = route(
+    core = lax.axis_index("expert") % 2
+    place = jnp.stack([lax.axis_index("dp"), lax.axis_index("tensor"), 1 - 2 * core]).astype(I32)
+
+    row_of, packed = route(
         (dp_size, tensor_size, capacity), place, tokens, expert_ids, norm_gain, router_weight
     )
-    arrived = [outgoing[0]]
-    for j in range(1, dp_size):
-        arrived.append(shift(outgoing[j], "dp", j))
+    arrived = exchange(packed, 1)
     gate, up, down = load(w_gate[0], w_up[0], w_down[0])
     arrived[-1] = after(arrived[-1], gate)
     mine = jnp.concatenate(arrived, axis=0)
+    far = ring_step(mine, "far_rows")
 
     apply = functools.partial(expert_apply, gate=gate, up=up, down=down)
     other = swap(mine)
     own_part, other_part = apply((1, 1), [mine, other])
     base = (own_part, swap(other_part))
-    far, near = after(ring_step(mine, "far_rows"), own_part), ring_step(other, "near_rows")
+    far, near = after(far, own_part), ring_step(other, "near_rows")
     near_terms, far_terms = [], []
     for k in range(1, half - 1):
         far_out, near_out, near_part, far_part = apply(
@@ -289,12 +305,12 @@
     far_out, near_part = apply((1, 1), [far, swap(far)])
     far = after(ring_step(far, "far_rows"), near, far_out, *near_terms[-1], *far_terms[-1])
     near_terms.append((near_part, swap(far_out)))
-    near_out, far_part, last_part, last_out = apply(
-        (1, 1, 1, 1), [near, swap(near), after(far, *near_terms[-1]), swap(far)]
-    )
+    last_part, last_out = apply((1, 1), [after(far, *near_terms[-1]), swap(far)])
+    far_sum = add(last_part, swap(last_out))
+    near_out, far_part = apply((1, 1), [after(near, far_sum), swap(near)])
     far_terms.append((far_part, swap(near_out)))
 
-    far_sum, near_sum = add(last_part, swap(last_out)), None
+    near_sum = None
     for k in range(half - 1, 0, -1):
         part, theirs = near_terms[k - 1]
         part = after(part, far_sum)
@@ -303,15 +319,10 @@
         far_sum = add(ring_step(far_sum, "far_sum"), *far_terms[k - 1])
     slot_out = add(ring_step(far_sum, "far_sum"), near_sum, *base)
 
-    returned = [slot_out[:capacity]]
-    for j in range(1, dp_size):
-        returned.append(shift(slot_out[j * capacity : (j + 1) * capacity], "dp", -j))
-    here = jnp.concatenate(returned, axis=0)
-    ahead = shift(here, "tensor", -1)
-    behind = shift(here, "tensor", 1)
-    cut = rows // 16 * 8
-    opposite = [shift(ahead[:cut], "tensor", -1), shift(behind[cut:], "tensor", 1)]
-    return collect(row_of, [here, ahead, *opposite, behind])
+    here = jnp.concatenate(exchange(slot_out, -1), axis=0)
+    far = tensor_step(here)
+    near = swap(tensor_step(swap(here)))
+    return collect(row_of, [here, near, tensor_step(far), far])
 
 
 def solution(mesh):

time: 133 us -> 131 us (0.985)
  Pallas kernels: 27.9 us -> 25.8 us
    ppermute x0 -> x3, waiting for transfers between devices: none -> 14.7 us  [tensor_step(): return lax.ppermute(values, ('tensor', 'expert'), pairs)]
    ppermute x10 -> x6, waiting for transfers between devices: 20.8 us -> 10.3 us  [shift(): lax.ppermute(values, axis, [(i, (i + steps) % size) for i in range(size)])]
    ppermute x10 -> x6, starting transfers between devices: 14.5 us -> 7.78 us  [shift(): lax.ppermute(values, axis, [(i, (i + steps) % size) for i in range(size)])]
    ppermute x13, waiting for transfers between devices: 48.2 us -> 42.6 us  [ring_step(): return lax.ppermute(values, 'expert', pairs)]
    ppermute x16 -> x18, starting transfers between devices: 7.75 us -> 11.7 us  [swap(): return lax.ppermute(values, 'expert', [(i, i ^ 1) for i in range(size)])]
    ppermute x0 -> x3, starting transfers between devices: none -> 3.57 us  [tensor_step(): return lax.ppermute(values, ('tensor', 'expert'), pairs)]
    pallas_call x5 -> x6, Pallas kernels: 18.6 us -> 16.5 us  [expert_apply(): pl.pallas_call(functools.partial(expert_kernel, groups), out_shape=[pltpu...]
    ppermute x16 -> x18, waiting for transfers between devices: 2.82 us -> 4.4 us  [swap(): return lax.ppermute(values, 'expert', [(i, i ^ 1) for i in range(size)])]
  transfers between devices with their start and end apart: 40 -> 41, of which waited for: 23 -> 27; matrix products, arithmetic and copies ran while one was open for 1% -> 1% of each run, Pallas kernels for 14% -> 14%
where the time goes in v3:
time: 131 us
  waiting for transfers between devices  74.4 us (57%)
  starting transfers between devices  28.6 us (22%)
  Pallas kernels  25.8 us (20%)
  other arithmetic  1.59 us (1%)
    ppermute x13, waiting for transfers between devices, ring_step(): return lax.ppermute(values, 'expert', pairs)  42.6 us
    pallas_call x6, Pallas kernels, expert_apply(): pl.pallas_call(functools.partial(expert_kernel, groups), out_shape=[pltpu...  16.5 us
    ppermute x3, waiting for transfers between devices, tensor_step(): return lax.ppermute(values, ('tensor', 'expert'), pairs)  14.7 us
    ppermute x18, starting transfers between devices, swap(): return lax.ppermute(values, 'expert', [(i, i ^ 1) for i in range(size)])  11.7 us
    ppermute x6, waiting for transfers between devices, shift(): lax.ppermute(values, axis, [(i, (i + steps) % size) for i in range(size)])  10.3 us
    ppermute x6, starting transfers between devices, shift(): lax.ppermute(values, axis, [(i, (i + steps) % size) for i in range(size)])  7.78 us
    ppermute x13, starting transfers between devices, ring_step(): return lax.ppermute(values, 'expert', pairs)  5.39 us
    pallas_call x1, Pallas kernels, load(): pl.pallas_call(load_kernel, out_shape=[pltpu.VMEM(x.shape, x.dtype) for x...  4.45 us
  transfers between devices with their start and end apart: 41, of which 27 were waited for; matrix products, arithmetic and copies ran while one was open for 1% of the time, Pallas kernels for 14%

profile of v3, /device:TPU:6, one launch (start us, length us, event | category | flops | bytes accessed | tf_op | source)
XLA Modules:
  0.0 131.0 jit_solution(3085847584026609301)
XLA Ops:
  0.1 3.5 %shard_map.73 = (s32[128,1]{1,0:T(8,128)S(1)}, bf16[40,5120]{1,0:T(8,128)(2,1)S(1)}) custom-call(s32[3]{0:T(128)S(1)} %pad_add_fusion.place, bf16[128,5120]{1,0:T(8,128)(2,1)} %refs_0_.1, s32[1,128]{1,0:T(1,128)} %bitcast.14, f32[1,5120]{1,0:T(1,128)} %bitcast.13, bf16[16,5120]{1,0:T(8,128)(2,1)} %bitcast.12), custom_call_target="tpu_custom_call" | custom-call | tf_op jit(solution)/shard_map/pallas_call | solution.py:144
  4.6 2.8 %collective-permute-start.1 = (bf16[10,5120]{1,0:T(8,128)(2,1)S(1)}, bf16[10,5120]{1,0:T(8,128)(2,1)S(1)}, u32[]{:S(2)}, u32[]{:S(2)}) collective-permute-start(bf16[10,5120]{1,0:T(8,128)(2,1)S(1)} %get-tuple-element.77), channel_id=1, source_target_pairs={{0,128},{64,192},{128,0},{192,64},{1,129},{65,193},{129,1},{193,65... | collective-permute-start | bytes 307208 | tf_op jit(solution)/shard_map/ppermute | solution.py:42
  7.8 4.5 %shard_map.74 = (bf16[5120,384]{1,0:T(8,128)(2,1)S(1)}, bf16[5120,384]{1,0:T(8,128)(2,1)S(1)}, bf16[384,5120]{1,0:T(8,128)(2,1)S(1)}) custom-call(bf16[5120,384]{1,0:T(8,128)(2,1)} %bitcast.9, bf16[5120,384]{1,0:T(8,128)(2,1)} %bitcast.10, bf16[384,5120]{1,0:T(8,128)(2,1)} %bitcast.11), custom_call_target="tpu_custom_call" | custom-call | tf_op jit(solution)/shard_map/pallas_call | solution.py:175
  12.3 2.2 %collective-permute-done.2 = bf16[10,5120]{1,0:T(8,128)(2,1)S(1)} collective-permute-done((bf16[10,5120]{1,0:T(8,128)(2,1)S(1)}, bf16[10,5120]{1,0:T(8,128)(2,1)S(1)}, u32[]{:S(2)}, u32[]{:S(2)}) %collective-permute-start.2) | collective-permute-done | bytes 102432 | tf_op jit(solution)/shard_map/ppermute | solution.py:42
  15.3 2.0 %collective-permute-start.3 = (bf16[40,5120]{1,0:T(8,128)(2,1)S(1)}, bf16[40,5120]{1,0:T(8,128)(2,1)S(1)}, u32[]{:S(2)}, u32[]{:S(2)}) collective-permute-start(bf16[40,5120]{1,0:T(8,128)(2,1)S(1)} %pad_maximum_fusion.refs_0_), channel_id=1, source_target_pairs={{0,2},{1,15},{2,4},{3,1},{4,6},{5,3},{6,8},{7,5},{8,10},{9,7},{10,... | collective-permute-start | bytes 1228808 | tf_op jit(solution)/shard_map/far_rows/ppermute | solution.py:49
  17.3 1.9 %collective-permute-start.6 = (bf16[40,5120]{1,0:T(8,128)(2,1)S(1)}, bf16[40,5120]{1,0:T(8,128)(2,1)S(1)}, u32[]{:S(2)}, u32[]{:S(2)}) collective-permute-start(bf16[40,5120]{1,0:T(8,128)(2,1)S(1)} %collective-permute-done.4.refs_1_), channel_id=1, source_target_pairs={{0,2},{1,15},{2,4},{3,1},{4,6},{5,3},{6,8},{7,5},{8,10},{9,7},{10,... | collective-permute-start | bytes 1228808 | tf_op jit(solution)/shard_map/near_rows/ppermute | solution.py:49
  19.3 2.7 %shard_map.75 = (bf16[40,5120]{1,0:T(8,128)(2,1)S(1)}, bf16[40,5120]{1,0:T(8,128)(2,1)S(1)}) custom-call(bf16[40,5120]{1,0:T(8,128)(2,1)S(1)} %pad_maximum_fusion.refs_0_, bf16[40,5120]{1,0:T(8,128)(2,1)S(1)} %collective-permute-done.4.refs_1_, bf16[5120,384]{1,0:T(8,128)(2,1)S(1)} %get-tuple-element.40.refs_2_.refs_4_, ...), custom_call_target="tpu_custom_call" | custom-call | tf_op jit(solution)/shard_map/pallas_call | solution.py:218
  21.9 3.6 %collective-permute-start.7 = (bf16[40,5120]{1,0:T(8,128)(2,1)S(1)}, bf16[40,5120]{1,0:T(8,128)(2,1)S(1)}, u32[]{:S(2)}, u32[]{:S(2)}) collective-permute-start(bf16[40,5120]{1,0:T(8,128)(2,1)S(1)} %get-tuple-element.46), channel_id=1, source_target_pairs={{0,1},{1,0},{2,3},{3,2},{4,5},{5,4},{6,7},{7,6},{8,9},{9,8},{10,11... | collective-permute-start | bytes 1228808 | tf_op jit(solution)/shard_map/other_core/ppermute | solution.py:72
  25.5 1.7 %collective-permute-done.3.refs_0_ = bf16[40,5120]{1,0:T(8,128)(2,1)S(1)} collective-permute-done((bf16[40,5120]{1,0:T(8,128)(2,1)S(1)}, bf16[40,5120]{1,0:T(8,128)(2,1)S(1)}, u32[]{:S(2)}, u32[]{:S(2)}) %collective-permute-start.3) | collective-permute-done | bytes 409632 | tf_op jit(solution)/shard_map/far_rows/ppermute | solution.py:49
  27.2 2.2 %collective-permute-start.10 = (bf16[40,5120]{1,0:T(8,128)(2,1)S(1)}, bf16[40,5120]{1,0:T(8,128)(2,1)S(1)}, u32[]{:S(2)}, u32[]{:S(2)}) collective-permute-start(bf16[40,5120]{1,0:T(8,128)(2,1)S(1)} %collective-permute-done.3.refs_0_), channel_id=1, source_target_pairs={{0,1},{1,0},{2,3},{3,2},{4,5},{5,4},{6,7},{7,6},{8,9},{9,8},{10,11... | collective-permute-start | bytes 1228808 | tf_op jit(solution)/shard_map/other_core/ppermute | solution.py:72
  29.4 2.2 %collective-permute-done.6.refs_1_ = bf16[40,5120]{1,0:T(8,128)(2,1)S(1)} collective-permute-done((bf16[40,5120]{1,0:T(8,128)(2,1)S(1)}, bf16[40,5120]{1,0:T(8,128)(2,1)S(1)}, u32[]{:S(2)}, u32[]{:S(2)}) %collective-permute-start.6) | collective-permute-done | bytes 409632 | tf_op jit(solution)/shard_map/near_rows/ppermute | solution.py:49
  31.6 4.8 %collective-permute-done.5.refs_0_ = bf16[40,5120]{1,0:T(8,128)(2,1)S(1)} collective-permute-done((bf16[40,5120]{1,0:T(8,128)(2,1)S(1)}, bf16[40,5120]{1,0:T(8,128)(2,1)S(1)}, u32[]{:S(2)}, u32[]{:S(2)}) %collective-permute-start.5) | collective-permute-done | bytes 409632 | tf_op jit(solution)/shard_map/far_rows/ppermute | solution.py:49
  36.4 2.9 %shard_map.76 = (bf16[40,5120]{1,0:T(8,128)(2,1)S(1)}, bf16[40,5120]{1,0:T(8,128)(2,1)S(1)}, bf16[40,5120]{1,0:T(8,128)(2,1)S(1)}, bf16[40,5120]{1,0:T(8,128)(2,1)S(1)}) custom-call(bf16[40,5120]{1,0:T(8,128)(2,1)S(1)} %collective-permute-done.3.refs_0_, bf16[40,5120]{1,0:T(8,128)(2,1)S(1)} %collective-permute-done.6.refs_1_, ...), custom_call_target="tpu_custom_call" | custom-call | tf_op jit(solution)/shard_map/pallas_call | solution.py:218
  39.3 2.1 %collective-permute-start.12 = (bf16[40,5120]{1,0:T(8,128)(2,1)S(1)}, bf16[40,5120]{1,0:T(8,128)(2,1)S(1)}, u32[]{:S(2)}, u32[]{:S(2)}) collective-permute-start(bf16[40,5120]{1,0:T(8,128)(2,1)S(1)} %get-tuple-element.51), channel_id=1, source_target_pairs={{0,1},{1,0},{2,3},{3,2},{4,5},{5,4},{6,7},{7,6},{8,9},{9,8},{10,11... | collective-permute-start | bytes 1228808 | tf_op jit(solution)/shard_map/other_core/ppermute | solution.py:72
  41.9 3.6 %collective-permute-done.8.refs_0_ = bf16[40,5120]{1,0:T(8,128)(2,1)S(1)} collective-permute-done((bf16[40,5120]{1,0:T(8,128)(2,1)S(1)}, bf16[40,5120]{1,0:T(8,128)(2,1)S(1)}, u32[]{:S(2)}, u32[]{:S(2)}) %collective-permute-start.8) | collective-permute-done | bytes 409632 | tf_op jit(solution)/shard_map/far_rows/ppermute | solution.py:49
  47.0 2.9 %shard_map.77 = (bf16[40,5120]{1,0:T(8,128)(2,1)S(1)}, bf16[40,5120]{1,0:T(8,128)(2,1)S(1)}, bf16[40,5120]{1,0:T(8,128)(2,1)S(1)}, bf16[40,5120]{1,0:T(8,128)(2,1)S(1)}) custom-call(bf16[40,5120]{1,0:T(8,128)(2,1)S(1)} %collective-permute-done.5.refs_0_, bf16[40,5120]{1,0:T(8,128)(2,1)S(1)} %collective-permute-done.9.refs_1_, ...), custom_call_target="tpu_custom_call" | custom-call | tf_op jit(solution)/shard_map/pallas_call | solution.py:218
  51.1 2.7 %shard_map.78 = (bf16[40,5120]{1,0:T(8,128)(2,1)S(1)}, bf16[40,5120]{1,0:T(8,128)(2,1)S(1)}) custom-call(bf16[40,5120]{1,0:T(8,128)(2,1)S(1)} %collective-permute-done.8.refs_0_, bf16[40,5120]{1,0:T(8,128)(2,1)S(1)} %collective-permute-done.17.refs_1_, bf16[5120,384]{1,0:T(8,128)(2,1)S(1)} %get-tuple-element.40.refs_2_.refs_4_, ...), custom_call_target="tpu_custom_call" | custom-call | tf_op jit(solution)/shard_map/pallas_call | solution.py:218
  57.2 2.7 %shard_map.79 = (bf16[40,5120]{1,0:T(8,128)(2,1)S(1)}, bf16[40,5120]{1,0:T(8,128)(2,1)S(1)}) custom-call(bf16[40,5120]{1,0:T(8,128)(2,1)S(1)} %collective-permute-done.13.refs_0_, bf16[40,5120]{1,0:T(8,128)(2,1)S(1)} %collective-permute-done.21.refs_1_, bf16[5120,384]{1,0:T(8,128)(2,1)S(1)} %get-tuple-element.40.refs_2_.refs_4_, ...), custom_call_target="tpu_custom_call" | custom-call | tf_op jit(solution)/shard_map/pallas_call | solution.py:218
  62.9 2.7 %shard_map.80 = (bf16[40,5120]{1,0:T(8,128)(2,1)S(1)}, bf16[40,5120]{1,0:T(8,128)(2,1)S(1)}) custom-call(bf16[40,5120]{1,0:T(8,128)(2,1)S(1)} %collective-permute-done.14.refs_0_, bf16[40,5120]{1,0:T(8,128)(2,1)S(1)} %collective-permute-done.24.refs_1_, bf16[5120,384]{1,0:T(8,128)(2,1)S(1)} %get-tuple-element.40.refs_2_.refs_4_, ...), custom_call_target="tpu_custom_call" | custom-call | tf_op jit(solution)/shard_map/pallas_call | solution.py:218
  67.4 3.7 %collective-permute-done.23 = bf16[40,5120]{1,0:T(8,128)(2,1)S(1)} collective-permute-done((bf16[40,5120]{1,0:T(8,128)(2,1)S(1)}, bf16[40,5120]{1,0:T(8,128)(2,1)S(1)}, u32[]{:S(2)}, u32[]{:S(2)}) %collective-permute-start.23) | collective-permute-done | bytes 409632 | tf_op jit(solution)/shard_map/far_sum/ppermute | solution.py:49
  71.3 4.1 %collective-permute-done.29 = bf16[40,5120]{1,0:T(8,128)(2,1)S(1)} collective-permute-done((bf16[40,5120]{1,0:T(8,128)(2,1)S(1)}, bf16[40,5120]{1,0:T(8,128)(2,1)S(1)}, u32[]{:S(2)}, u32[]{:S(2)}) %collective-permute-start.29) | collective-permute-done | bytes 409632 | tf_op jit(solution)/shard_map/near_sum/ppermute | solution.py:49
  75.7 4.8 %collective-permute-done.26 = bf16[40,5120]{1,0:T(8,128)(2,1)S(1)} collective-permute-done((bf16[40,5120]{1,0:T(8,128)(2,1)S(1)}, bf16[40,5120]{1,0:T(8,128)(2,1)S(1)}, u32[]{:S(2)}, u32[]{:S(2)}) %collective-permute-start.26) | collective-permute-done | bytes 409632 | tf_op jit(solution)/shard_map/far_sum/ppermute | solution.py:49
  80.7 4.1 %collective-permute-done.30 = bf16[40,5120]{1,0:T(8,128)(2,1)S(1)} collective-permute-done((bf16[40,5120]{1,0:T(8,128)(2,1)S(1)}, bf16[40,5120]{1,0:T(8,128)(2,1)S(1)}, u32[]{:S(2)}, u32[]{:S(2)}) %collective-permute-start.30) | collective-permute-done | bytes 409632 | tf_op jit(solution)/shard_map/near_sum/ppermute | solution.py:49
  85.1 4.8 %collective-permute-done.27 = bf16[40,5120]{1,0:T(8,128)(2,1)S(1)} collective-permute-done((bf16[40,5120]{1,0:T(8,128)(2,1)S(1)}, bf16[40,5120]{1,0:T(8,128)(2,1)S(1)}, u32[]{:S(2)}, u32[]{:S(2)}) %collective-permute-start.27) | collective-permute-done | bytes 409632 | tf_op jit(solution)/shard_map/far_sum/ppermute | solution.py:49
  90.1 2.4 %collective-permute-done.32 = bf16[40,5120]{1,0:T(8,128)(2,1)S(1)} collective-permute-done((bf16[40,5120]{1,0:T(8,128)(2,1)S(1)}, bf16[40,5120]{1,0:T(8,128)(2,1)S(1)}, u32[]{:S(2)}, u32[]{:S(2)}) %collective-permute-start.32) | collective-permute-done | bytes 409632 | tf_op jit(solution)/shard_map/near_sum/ppermute | solution.py:56
  92.5 6.8 %collective-permute-done.28 = bf16[40,5120]{1,0:T(8,128)(2,1)S(1)} collective-permute-done((bf16[40,5120]{1,0:T(8,128)(2,1)S(1)}, bf16[40,5120]{1,0:T(8,128)(2,1)S(1)}, u32[]{:S(2)}, u32[]{:S(2)}) %collective-permute-start.28) | collective-permute-done | bytes 409632 | tf_op jit(solution)/shard_map/far_sum/ppermute | solution.py:49
  99.6 2.7 %collective-permute-start.35 = (bf16[10,5120]{1,0:T(8,128)(2,1)S(1)}, bf16[10,5120]{1,0:T(8,128)(2,1)S(1)}, u32[]{:S(2)}, u32[]{:S(2)}) collective-permute-start(bf16[10,5120]{1,0:T(8,128)(2,1)S(1)} %get-tuple-element.72), channel_id=1, source_target_pairs={{0,64},{64,128},{128,192},{192,0},{1,65},{65,129},{129,193},{193,1... | collective-permute-start | bytes 307208 | tf_op jit(solution)/shard_map/ppermute | solution.py:42
  103.2 3.9 %collective-permute-done.35 = bf16[10,5120]{1,0:T(8,128)(2,1)S(1)} collective-permute-done((bf16[10,5120]{1,0:T(8,128)(2,1)S(1)}, bf16[10,5120]{1,0:T(8,128)(2,1)S(1)}, u32[]{:S(2)}, u32[]{:S(2)}) %collective-permute-start.35) | collective-permute-done | bytes 102432 | tf_op jit(solution)/shard_map/ppermute | solution.py:42
  107.2 2.1 %collective-permute-done.34 = bf16[10,5120]{1,0:T(8,128)(2,1)S(1)} collective-permute-done((bf16[10,5120]{1,0:T(8,128)(2,1)S(1)}, bf16[10,5120]{1,0:T(8,128)(2,1)S(1)}, u32[]{:S(2)}, u32[]{:S(2)}) %collective-permute-start.34) | collective-permute-done | bytes 102432 | tf_op jit(solution)/shard_map/ppermute | solution.py:42
  114.4 5.9 %collective-permute-done.39.refs_3_ = bf16[40,5120]{1,0:T(8,128)(2,1)S(1)} collective-permute-done((bf16[40,5120]{1,0:T(8,128)(2,1)S(1)}, bf16[40,5120]{1,0:T(8,128)(2,1)S(1)}, u32[]{:S(2)}, u32[]{:S(2)}) %collective-permute-start.39) | collective-permute-done | bytes 409632 | tf_op jit(solution)/shard_map/ppermute | solution.py:66
  120.7 4.0 %collective-permute-done.37 = bf16[40,5120]{1,0:T(8,128)(2,1)S(1)} collective-permute-done((bf16[40,5120]{1,0:T(8,128)(2,1)S(1)}, bf16[40,5120]{1,0:T(8,128)(2,1)S(1)}, u32[]{:S(2)}, u32[]{:S(2)}) %collective-permute-start.37) | collective-permute-done | bytes 409632 | tf_op jit(solution)/shard_map/ppermute | solution.py:66
  124.7 4.8 %collective-permute-done.40.refs_2_ = bf16[40,5120]{1,0:T(8,128)(2,1)S(1)} collective-permute-done((bf16[40,5120]{1,0:T(8,128)(2,1)S(1)}, bf16[40,5120]{1,0:T(8,128)(2,1)S(1)}, u32[]{:S(2)}, u32[]{:S(2)}) %collective-permute-start.40) | collective-permute-done | bytes 409632 | tf_op jit(solution)/shard_map/ppermute | solution.py:66
  (72 shorter events, 23.1 us)
Async XLA Ops:
  3.7 10.7 %collective-permute-start.2 = (bf16[10,5120]{1,0:T(8,128)(2,1)S(1)}, bf16[10,5120]{1,0:T(8,128)(2,1)S(1)}, u32[]{:S(2)}, u32[]{:S(2)}) collective-permute-start(bf16[10,5120]{1,0:T(8,128)(2,1)S(1)} %get-tuple-element.76), channel_id=1, source_target_pairs={{0,192},{64,0},{128,64},{192,128},{1,193},{65,1},{129,65},{193,129... | collective-permute-start | bytes 307208 | tf_op jit(solution)/shard_map/ppermute | solution.py:42
  4.6 9.8 %collective-permute-start.1 = (bf16[10,5120]{1,0:T(8,128)(2,1)S(1)}, bf16[10,5120]{1,0:T(8,128)(2,1)S(1)}, u32[]{:S(2)}, u32[]{:S(2)}) collective-permute-start(bf16[10,5120]{1,0:T(8,128)(2,1)S(1)} %get-tuple-element.77), channel_id=1, source_target_pairs={{0,128},{64,192},{128,0},{192,64},{1,129},{65,193},{129,1},{193,65... | collective-permute-start | bytes 307208 | tf_op jit(solution)/shard_map/ppermute | solution.py:42
  7.5 7.6 %collective-permute-start = (bf16[10,5120]{1,0:T(8,128)(2,1)S(1)}, bf16[10,5120]{1,0:T(8,128)(2,1)S(1)}, u32[]{:S(2)}, u32[]{:S(2)}) collective-permute-start(bf16[10,5120]{1,0:T(8,128)(2,1)S(1)} %get-tuple-element.78), channel_id=1, source_target_pairs={{0,64},{64,128},{128,192},{192,0},{1,65},{65,129},{129,193},{193,1... | collective-permute-start | bytes 307208 | tf_op jit(solution)/shard_map/ppermute | solution.py:42
  15.3 11.9 %collective-permute-start.3 = (bf16[40,5120]{1,0:T(8,128)(2,1)S(1)}, bf16[40,5120]{1,0:T(8,128)(2,1)S(1)}, u32[]{:S(2)}, u32[]{:S(2)}) collective-permute-start(bf16[40,5120]{1,0:T(8,128)(2,1)S(1)} %pad_maximum_fusion.refs_0_), channel_id=1, source_target_pairs={{0,2},{1,15},{2,4},{3,1},{4,6},{5,3},{6,8},{7,5},{8,10},{9,7},{10,... | collective-permute-start | bytes 1228808 | tf_op jit(solution)/shard_map/far_rows/ppermute | solution.py:49
  17.3 14.3 %collective-permute-start.6 = (bf16[40,5120]{1,0:T(8,128)(2,1)S(1)}, bf16[40,5120]{1,0:T(8,128)(2,1)S(1)}, u32[]{:S(2)}, u32[]{:S(2)}) collective-permute-start(bf16[40,5120]{1,0:T(8,128)(2,1)S(1)} %collective-permute-done.4.refs_1_), channel_id=1, source_target_pairs={{0,2},{1,15},{2,4},{3,1},{4,6},{5,3},{6,8},{7,5},{8,10},{9,7},{10,... | collective-permute-start | bytes 1228808 | tf_op jit(solution)/shard_map/near_rows/ppermute | solution.py:49
  21.9 9.7 %collective-permute-start.7 = (bf16[40,5120]{1,0:T(8,128)(2,1)S(1)}, bf16[40,5120]{1,0:T(8,128)(2,1)S(1)}, u32[]{:S(2)}, u32[]{:S(2)}) collective-permute-start(bf16[40,5120]{1,0:T(8,128)(2,1)S(1)} %get-tuple-element.46), channel_id=1, source_target_pairs={{0,1},{1,0},{2,3},{3,2},{4,5},{5,4},{6,7},{7,6},{8,9},{9,8},{10,11... | collective-permute-start | bytes 1228808 | tf_op jit(solution)/shard_map/other_core/ppermute | solution.py:72
  27.2 9.2 %collective-permute-start.5 = (bf16[40,5120]{1,0:T(8,128)(2,1)S(1)}, bf16[40,5120]{1,0:T(8,128)(2,1)S(1)}, u32[]{:S(2)}, u32[]{:S(2)}) collective-permute-start(bf16[40,5120]{1,0:T(8,128)(2,1)S(1)} %collective-permute-done.3.refs_0_), channel_id=1, source_target_pairs={{0,2},{1,15},{2,4},{3,1},{4,6},{5,3},{6,8},{7,5},{8,10},{9,7},{10,... | collective-permute-start | bytes 1228808 | tf_op jit(solution)/shard_map/far_rows/ppermute | solution.py:49
  27.2 9.2 %collective-permute-start.10 = (bf16[40,5120]{1,0:T(8,128)(2,1)S(1)}, bf16[40,5120]{1,0:T(8,128)(2,1)S(1)}, u32[]{:S(2)}, u32[]{:S(2)}) collective-permute-start(bf16[40,5120]{1,0:T(8,128)(2,1)S(1)} %collective-permute-done.3.refs_0_), channel_id=1, source_target_pairs={{0,1},{1,0},{2,3},{3,2},{4,5},{5,4},{6,7},{7,6},{8,9},{9,8},{10,11... | collective-permute-start | bytes 1228808 | tf_op jit(solution)/shard_map/other_core/ppermute | solution.py:72
  31.6 4.8 %collective-permute-start.11 = (bf16[40,5120]{1,0:T(8,128)(2,1)S(1)}, bf16[40,5120]{1,0:T(8,128)(2,1)S(1)}, u32[]{:S(2)}, u32[]{:S(2)}) collective-permute-start(bf16[40,5120]{1,0:T(8,128)(2,1)S(1)} %collective-permute-done.6.refs_1_), channel_id=1, source_target_pairs={{0,1},{1,0},{2,3},{3,2},{4,5},{5,4},{6,7},{7,6},{8,9},{9,8},{10,11... | collective-permute-start | bytes 1228808 | tf_op jit(solution)/shard_map/other_core/ppermute | solution.py:72
  31.6 9.9 %collective-permute-start.9 = (bf16[40,5120]{1,0:T(8,128)(2,1)S(1)}, bf16[40,5120]{1,0:T(8,128)(2,1)S(1)}, u32[]{:S(2)}, u32[]{:S(2)}) collective-permute-start(bf16[40,5120]{1,0:T(8,128)(2,1)S(1)} %collective-permute-done.6.refs_1_), channel_id=1, source_target_pairs={{0,2},{1,15},{2,4},{3,1},{4,6},{5,3},{6,8},{7,5},{8,10},{9,7},{10,... | collective-permute-start | bytes 1228808 | tf_op jit(solution)/shard_map/near_rows/ppermute | solution.py:49
  36.4 9.2 %collective-permute-start.8 = (bf16[40,5120]{1,0:T(8,128)(2,1)S(1)}, bf16[40,5120]{1,0:T(8,128)(2,1)S(1)}, u32[]{:S(2)}, u32[]{:S(2)}) collective-permute-start(bf16[40,5120]{1,0:T(8,128)(2,1)S(1)} %collective-permute-done.5.refs_0_), channel_id=1, source_target_pairs={{0,2},{1,15},{2,4},{3,1},{4,6},{5,3},{6,8},{7,5},{8,10},{9,7},{10,... | collective-permute-start | bytes 1228808 | tf_op jit(solution)/shard_map/far_rows/ppermute | solution.py:49
  39.3 6.2 %collective-permute-start.12 = (bf16[40,5120]{1,0:T(8,128)(2,1)S(1)}, bf16[40,5120]{1,0:T(8,128)(2,1)S(1)}, u32[]{:S(2)}, u32[]{:S(2)}) collective-permute-start(bf16[40,5120]{1,0:T(8,128)(2,1)S(1)} %get-tuple-element.51), channel_id=1, source_target_pairs={{0,1},{1,0},{2,3},{3,2},{4,5},{5,4},{6,7},{7,6},{8,9},{9,8},{10,11... | collective-permute-start | bytes 1228808 | tf_op jit(solution)/shard_map/other_core/ppermute | solution.py:72
  41.4 5.6 %collective-permute-start.15 = (bf16[40,5120]{1,0:T(8,128)(2,1)S(1)}, bf16[40,5120]{1,0:T(8,128)(2,1)S(1)}, u32[]{:S(2)}, u32[]{:S(2)}) collective-permute-start(bf16[40,5120]{1,0:T(8,128)(2,1)S(1)} %collective-permute-done.5.refs_0_), channel_id=1, source_target_pairs={{0,1},{1,0},{2,3},{3,2},{4,5},{5,4},{6,7},{7,6},{8,9},{9,8},{10,11... | collective-permute-start | bytes 1228808 | tf_op jit(solution)/shard_map/other_core/ppermute | solution.py:72
  41.5 5.5 %collective-permute-start.16 = (bf16[40,5120]{1,0:T(8,128)(2,1)S(1)}, bf16[40,5120]{1,0:T(8,128)(2,1)S(1)}, u32[]{:S(2)}, u32[]{:S(2)}) collective-permute-start(bf16[40,5120]{1,0:T(8,128)(2,1)S(1)} %collective-permute-done.9.refs_1_), channel_id=1, source_target_pairs={{0,1},{1,0},{2,3},{3,2},{4,5},{5,4},{6,7},{7,6},{8,9},{9,8},{10,11... | collective-permute-start | bytes 1228808 | tf_op jit(solution)/shard_map/other_core/ppermute | solution.py:72
  41.9 9.2 %collective-permute-start.14 = (bf16[40,5120]{1,0:T(8,128)(2,1)S(1)}, bf16[40,5120]{1,0:T(8,128)(2,1)S(1)}, u32[]{:S(2)}, u32[]{:S(2)}) collective-permute-start(bf16[40,5120]{1,0:T(8,128)(2,1)S(1)} %collective-permute-done.9.refs_1_), channel_id=1, source_target_pairs={{0,2},{1,15},{2,4},{3,1},{4,6},{5,3},{6,8},{7,5},{8,10},{9,7},{10,... | collective-permute-start | bytes 1228808 | tf_op jit(solution)/shard_map/near_rows/ppermute | solution.py:49
  45.5 9.9 %collective-permute-start.13 = (bf16[40,5120]{1,0:T(8,128)(2,1)S(1)}, bf16[40,5120]{1,0:T(8,128)(2,1)S(1)}, u32[]{:S(2)}, u32[]{:S(2)}) collective-permute-start(bf16[40,5120]{1,0:T(8,128)(2,1)S(1)} %collective-permute-done.8.refs_0_), channel_id=1, source_target_pairs={{0,2},{1,15},{2,4},{3,1},{4,6},{5,3},{6,8},{7,5},{8,10},{9,7},{10,... | collective-permute-start | bytes 1228808 | tf_op jit(solution)/shard_map/far_rows/ppermute | solution.py:49
  45.5 5.6 %collective-permute-start.17 = (bf16[40,5120]{1,0:T(8,128)(2,1)S(1)}, bf16[40,5120]{1,0:T(8,128)(2,1)S(1)}, u32[]{:S(2)}, u32[]{:S(2)}) collective-permute-start(bf16[40,5120]{1,0:T(8,128)(2,1)S(1)} %collective-permute-done.8.refs_0_), channel_id=1, source_target_pairs={{0,1},{1,0},{2,3},{3,2},{4,5},{5,4},{6,7},{7,6},{8,9},{9,8},{10,11... | collective-permute-start | bytes 1228808 | tf_op jit(solution)/shard_map/other_core/ppermute | solution.py:72
  50.0 5.5 %collective-permute-start.18 = (bf16[40,5120]{1,0:T(8,128)(2,1)S(1)}, bf16[40,5120]{1,0:T(8,128)(2,1)S(1)}, u32[]{:S(2)}, u32[]{:S(2)}) collective-permute-start(bf16[40,5120]{1,0:T(8,128)(2,1)S(1)} %get-tuple-element.53), channel_id=1, source_target_pairs={{0,1},{1,0},{2,3},{3,2},{4,5},{5,4},{6,7},{7,6},{8,9},{9,8},{10,11... | collective-permute-start | bytes 1228808 | tf_op jit(solution)/shard_map/other_core/ppermute | solution.py:72
  60.1 20.6 %collective-permute-start.31 = (bf16[40,5120]{1,0:T(8,128)(2,1)S(1)}, bf16[40,5120]{1,0:T(8,128)(2,1)S(1)}, u32[]{:S(2)}, u32[]{:S(2)}) collective-permute-start(bf16[40,5120]{1,0:T(8,128)(2,1)S(1)} %get-tuple-element.48), channel_id=1, source_target_pairs={{0,1},{1,0},{2,3},{3,2},{4,5},{5,4},{6,7},{7,6},{8,9},{9,8},{10,11... | collective-permute-start | bytes 1228808 | tf_op jit(solution)/shard_map/other_core/ppermute | solution.py:72
  61.8 9.2 %collective-permute-start.23 = (bf16[40,5120]{1,0:T(8,128)(2,1)S(1)}, bf16[40,5120]{1,0:T(8,128)(2,1)S(1)}, u32[]{:S(2)}, u32[]{:S(2)}) collective-permute-start(bf16[40,5120]{1,0:T(8,128)(2,1)S(1)} %add_convert_fusion.7), channel_id=1, source_target_pairs={{0,2},{1,15},{2,4},{3,1},{4,6},{5,3},{6,8},{7,5},{8,10},{9,7},{10,... | collective-permute-start | bytes 1228808 | tf_op jit(solution)/shard_map/far_sum/ppermute | solution.py:49
  65.9 9.6 %collective-permute-start.29 = (bf16[40,5120]{1,0:T(8,128)(2,1)S(1)}, bf16[40,5120]{1,0:T(8,128)(2,1)S(1)}, u32[]{:S(2)}, u32[]{:S(2)}) collective-permute-start(bf16[40,5120]{1,0:T(8,128)(2,1)S(1)} %add_convert_fusion.3), channel_id=1, source_target_pairs={{0,2},{1,15},{2,4},{3,1},{4,6},{5,3},{6,8},{7,5},{8,10},{9,7},{10,... | collective-permute-start | bytes 1228808 | tf_op jit(solution)/shard_map/near_sum/ppermute | solution.py:49
  71.2 9.2 %collective-permute-start.26 = (bf16[40,5120]{1,0:T(8,128)(2,1)S(1)}, bf16[40,5120]{1,0:T(8,128)(2,1)S(1)}, u32[]{:S(2)}, u32[]{:S(2)}) collective-permute-start(bf16[40,5120]{1,0:T(8,128)(2,1)S(1)} %add_convert_fusion.6), channel_id=1, source_target_pairs={{0,2},{1,15},{2,4},{3,1},{4,6},{5,3},{6,8},{7,5},{8,10},{9,7},{10,... | collective-permute-start | bytes 1228808 | tf_op jit(solution)/shard_map/far_sum/ppermute | solution.py:49
  75.6 9.2 %collective-permute-start.30 = (bf16[40,5120]{1,0:T(8,128)(2,1)S(1)}, bf16[40,5120]{1,0:T(8,128)(2,1)S(1)}, u32[]{:S(2)}, u32[]{:S(2)}) collective-permute-start(bf16[40,5120]{1,0:T(8,128)(2,1)S(1)} %add_convert_fusion.2), channel_id=1, source_target_pairs={{0,2},{1,15},{2,4},{3,1},{4,6},{5,3},{6,8},{7,5},{8,10},{9,7},{10,... | collective-permute-start | bytes 1228808 | tf_op jit(solution)/shard_map/near_sum/ppermute | solution.py:49
  80.6 9.2 %collective-permute-start.27 = (bf16[40,5120]{1,0:T(8,128)(2,1)S(1)}, bf16[40,5120]{1,0:T(8,128)(2,1)S(1)}, u32[]{:S(2)}, u32[]{:S(2)}) collective-permute-start(bf16[40,5120]{1,0:T(8,128)(2,1)S(1)} %add_convert_fusion.5), channel_id=1, source_target_pairs={{0,2},{1,15},{2,4},{3,1},{4,6},{5,3},{6,8},{7,5},{8,10},{9,7},{10,... | collective-permute-start | bytes 1228808 | tf_op jit(solution)/shard_map/far_sum/ppermute | solution.py:49
  85.0 7.5 %collective-permute-start.32 = (bf16[40,5120]{1,0:T(8,128)(2,1)S(1)}, bf16[40,5120]{1,0:T(8,128)(2,1)S(1)}, u32[]{:S(2)}, u32[]{:S(2)}) collective-permute-start(bf16[40,5120]{1,0:T(8,128)(2,1)S(1)} %add_convert_fusion.1), channel_id=1, source_target_pairs={{0,3},{1,14},{2,5},{3,0},{4,7},{5,2},{6,9},{7,4},{8,11},{9,6},{10,... | collective-permute-start | bytes 1228808 | tf_op jit(solution)/shard_map/near_sum/ppermute | solution.py:56
  90.0 9.2 %collective-permute-start.28 = (bf16[40,5120]{1,0:T(8,128)(2,1)S(1)}, bf16[40,5120]{1,0:T(8,128)(2,1)S(1)}, u32[]{:S(2)}, u32[]{:S(2)}) collective-permute-start(bf16[40,5120]{1,0:T(8,128)(2,1)S(1)} %add_convert_fusion.4), channel_id=1, source_target_pairs={{0,2},{1,15},{2,4},{3,1},{4,6},{5,3},{6,8},{7,5},{8,10},{9,7},{10,... | collective-permute-start | bytes 1228808 | tf_op jit(solution)/shard_map/far_sum/ppermute | solution.py:49
  99.6 7.6 %collective-permute-start.35 = (bf16[10,5120]{1,0:T(8,128)(2,1)S(1)}, bf16[10,5120]{1,0:T(8,128)(2,1)S(1)}, u32[]{:S(2)}, u32[]{:S(2)}) collective-permute-start(bf16[10,5120]{1,0:T(8,128)(2,1)S(1)} %get-tuple-element.72), channel_id=1, source_target_pairs={{0,64},{64,128},{128,192},{192,0},{1,65},{65,129},{129,193},{193,1... | collective-permute-start | bytes 307208 | tf_op jit(solution)/shard_map/ppermute | solution.py:42
  102.3 7.0 %collective-permute-start.34 = (bf16[10,5120]{1,0:T(8,128)(2,1)S(1)}, bf16[10,5120]{1,0:T(8,128)(2,1)S(1)}, u32[]{:S(2)}, u32[]{:S(2)}) collective-permute-start(bf16[10,5120]{1,0:T(8,128)(2,1)S(1)} %get-tuple-element.73), channel_id=1, source_target_pairs={{0,128},{64,192},{128,0},{192,64},{1,129},{65,193},{129,1},{193,65... | collective-permute-start | bytes 307208 | tf_op jit(solution)/shard_map/ppermute | solution.py:42
  102.5 8.3 %collective-permute-start.33 = (bf16[10,5120]{1,0:T(8,128)(2,1)S(1)}, bf16[10,5120]{1,0:T(8,128)(2,1)S(1)}, u32[]{:S(2)}, u32[]{:S(2)}) collective-permute-start(bf16[10,5120]{1,0:T(8,128)(2,1)S(1)} %get-tuple-element.74), channel_id=1, source_target_pairs={{0,192},{64,0},{128,64},{192,128},{1,193},{65,1},{129,65},{193,129... | collective-permute-start | bytes 307208 | tf_op jit(solution)/shard_map/ppermute | solution.py:42
  111.1 9.2 %collective-permute-start.39 = (bf16[40,5120]{1,0:T(8,128)(2,1)S(1)}, bf16[40,5120]{1,0:T(8,128)(2,1)S(1)}, u32[]{:S(2)}, u32[]{:S(2)}) collective-permute-start(bf16[40,5120]{1,0:T(8,128)(2,1)S(1)} %pad_maximum_fusion.1.refs_0_), channel_id=1, source_target_pairs={{0,16},{1,49},{2,18},{3,51},{4,20},{5,53},{6,22},{7,55},{8,24},{9,... | collective-permute-start | bytes 1228808 | tf_op jit(solution)/shard_map/ppermute | solution.py:66
  112.8 11.9 %collective-permute-start.37 = (bf16[40,5120]{1,0:T(8,128)(2,1)S(1)}, bf16[40,5120]{1,0:T(8,128)(2,1)S(1)}, u32[]{:S(2)}, u32[]{:S(2)}) collective-permute-start(bf16[40,5120]{1,0:T(8,128)(2,1)S(1)} %collective-permute-done.36), channel_id=1, source_target_pairs={{0,16},{1,49},{2,18},{3,51},{4,20},{5,53},{6,22},{7,55},{8,24},{9,... | collective-permute-start | bytes 1228808 | tf_op jit(solution)/shard_map/ppermute | solution.py:66
  120.3 9.2 %collective-permute-start.40 = (bf16[40,5120]{1,0:T(8,128)(2,1)S(1)}, bf16[40,5120]{1,0:T(8,128)(2,1)S(1)}, u32[]{:S(2)}, u32[]{:S(2)}) collective-permute-start(bf16[40,5120]{1,0:T(8,128)(2,1)S(1)} %collective-permute-done.39.refs_3_), channel_id=1, source_target_pairs={{0,16},{1,49},{2,18},{3,51},{4,20},{5,53},{6,22},{7,55},{8,24},{9,... | collective-permute-start | bytes 1228808 | tf_op jit(solution)/shard_map/ppermute | solution.py:66
  (9 other events, 22.3 us)

commit v4 on v3

--- a/solution.py
+++ b/solution.py
@@ -76,38 +76,26 @@
     dp_size, tensor_size, capacity = sizes
     sources, row_of, packed = refs[:4], refs[4], refs[5]
     tokens, ids_row, gain, router, normed, sems = refs[6:]
+    count, features = tokens.shape
+    rows = packed.shape[0]
+    step = step_of(features, 1280)
+    spans = [pl.ds(i, step) for i in range(0, features, step)]
+    part_size = step_of(features, 1280)
+    part_spans = [pl.ds(i, part_size) for i in range(0, features, part_size)]
     copies = [
         pltpu.make_async_copy(source, held, sems.at[i])
-        for i, (source, held) in enumerate(zip(sources, (tokens, ids_row, gain, router)))
+        for i, (source, held) in enumerate(zip(sources[1:], (ids_row, gain, router)))
+    ] + [
+        pltpu.make_async_copy(sources[0].at[:, cols], tokens.at[:, cols], sems.at[3 + i])
+        for i, cols in enumerate(part_spans)
     ]
     for copy in copies:
         copy.start()
-    for copy in copies:
-        copy.wait()
-    count, features = tokens.shape
-    step = step_of(features, 512)
-    spans = [pl.ds(i, step) for i in range(0, features, step)]
+
+    copies[0].wait()
     down = lax.broadcasted_iota(I32, (count, count), 0)
     across = lax.broadcasted_iota(I32, (count, count), 1)
     ids_col = jnp.sum(jnp.where(down == across, ids_row[...], 0), axis=1, keepdims=True)
-
-    total = jnp.zeros((count, LANES), F32)
-    for i in range(0, features, LANES):
-        part = tokens[:, i : i + LANES].astype(F32)
-        total = total + part * part
-    scale = lax.rsqrt(jnp.sum(total, axis=1, keepdims=True) * (1.0 / features) + 1e-05)
-
-    logits = jnp.zeros((count, router.shape[0]), F32)
-    for cols in spans:
-        part = (tokens[:, cols].astype(F32) * scale * gain[:, cols]).astype(BF16)
-        normed[:, cols] = part
-        logits = logits + lax.dot_general(
-            part, router[:, cols], (((1,), (1,)), ((), ())), preferred_element_type=F32
-        )
-    expert = lax.broadcasted_iota(I32, logits.shape, 1)
-    chosen = jnp.sum(jnp.where(ids_col == expert, logits, 0.0), axis=1, keepdims=True)
-    gate = 1.0 / (1.0 + jnp.exp(-chosen))
-
     same = ids_col == ids_row[...]
     slot_col = jnp.sum(jnp.where(same & (across < down), 1, 0), axis=1, keepdims=True)
     slot_row = jnp.sum(jnp.where(same & (down < across), 1, 0), axis=0, keepdims=True)
@@ -125,11 +113,38 @@
     row_of[...] = (on_tensor * dp_size + on_dp) * capacity + slot_col
     on_dp, on_tensor = ahead(ids_row[...])
     target = jnp.where(on_tensor == 0, on_dp * capacity + slot_row, -1)
-    row = lax.broadcasted_iota(I32, (packed.shape[0], count), 0)
+    row = lax.broadcasted_iota(I32, (rows, count), 0)
     picks = jnp.where(row == target, 1.0, 0.0).astype(BF16)
+
+    total = jnp.zeros((rows, LANES), F32)
+    for cols, copy in zip(part_spans, copies[3:]):
+        copy.wait()
+        part = jnp.dot(picks, tokens[:, cols], preferred_element_type=F32)
+        normed[:, cols] = part.astype(BF16)
+        for i in range(0, part_size, LANES):
+            total = total + part[:, i : i + LANES] * part[:, i : i + LANES]
+    scale = lax.rsqrt(jnp.sum(total, axis=1, keepdims=True) * (1.0 / features) + 1e-05)
+
+    copies[1].wait()
+    copies[2].wait()
+    logits = jnp.zeros((rows, router.shape[0]), F32)
     for cols in spans:
-        routed = (normed[:, cols].astype(F32) * gate).astype(BF16)
-        packed[:, cols] = jnp.dot(picks, routed, preferred_element_type=F32).astype(BF16)
+        part = (normed[:, cols].astype(F32) * scale * gain[:, cols]).astype(BF16)
+        normed[:, cols] = part
+        logits = logits + lax.dot_general(
+            part, router[:, cols], (((1,), (1,)), ((), ())), preferred_element_type=F32
+        )
+    row = lax.broadcasted_iota(I32, logits.shape, 0)
+    dp_of = jnp.zeros_like(row) + place[0]
+    for d in range(1, dp_size):
+        dp_of = dp_of + jnp.where(row >= d * capacity, 1, 0)
+    dp_of = jnp.where(dp_of >= dp_size, dp_of - dp_size, dp_of)
+    expert = lax.broadcasted_iota(I32, logits.shape, 1)
+    mine = expert == dp_of * tensor_size + place[1]
+    chosen = jnp.sum(jnp.where(mine, logits, 0.0), axis=1, keepdims=True)
+    gate = 1.0 / (1.0 + jnp.exp(-chosen))
+    for cols in spans:
+        packed[:, cols] = (normed[:, cols].astype(F32) * gate).astype(BF16)
 
 
 def route(sizes, place, tokens, expert_ids, norm_gain, router_weight):
@@ -152,8 +167,8 @@
         out_specs=vmem_specs(2),
         scratch_shapes=[pltpu.VMEM(x.shape, x.dtype) for x in operands]
         + [
-            pltpu.VMEM((count, features), BF16),
-            pltpu.SemaphoreType.DMA((len(operands),)),
+            pltpu.VMEM((dp_size * capacity, features), BF16),
+            pltpu.SemaphoreType.DMA((3 + features // step_of(features, 1280),)),
         ],
         compiler_params=pltpu.CompilerParams(vmem_limit_bytes=VMEM_LIMIT),
     )(place, *map(in_hbm, operands))

time: 131 us -> 131 us (level)
  no operation moved by 1% of the time
where the time goes in v4:
time: 131 us; the launch traced here: 130 us
  waiting for transfers between devices  74.4 us (57%)
  starting transfers between devices  28.4 us (22%)
  Pallas kernels  25.4 us (19%)
  other arithmetic  1.59 us (1%)
    ppermute x13, waiting for transfers between devices, ring_step(): return lax.ppermute(values, 'expert', pairs)  42.6 us
    pallas_call x6, Pallas kernels, expert_apply(): pl.pallas_call(functools.partial(expert_kernel, groups), out_shape=[pltpu...  16.5 us
    ppermute x3, waiting for transfers between devices, tensor_step(): return lax.ppermute(values, ('tensor', 'expert'), pairs)  14.7 us
    ppermute x18, starting transfers between devices, swap(): return lax.ppermute(values, 'expert', [(i, i ^ 1) for i in range(size)])  11.5 us
    ppermute x6, waiting for transfers between devices, shift(): lax.ppermute(values, axis, [(i, (i + steps) % size) for i in range(size)])  10.3 us
    ppermute x6, starting transfers between devices, shift(): lax.ppermute(values, axis, [(i, (i + steps) % size) for i in range(size)])  7.8 us
    ppermute x13, starting transfers between devices, ring_step(): return lax.ppermute(values, 'expert', pairs)  5.4 us
    pallas_call x1, Pallas kernels, load(): pl.pallas_call(load_kernel, out_shape=[pltpu.VMEM(x.shape, x.dtype) for x...  4.45 us
  transfers between devices with their start and end apart: 41, of which 27 were waited for; matrix products, arithmetic and copies ran while one was open for 1% of the time, Pallas kernels for 14%

profile of v4, /device:TPU:6, one launch (start us, length us, event | category | flops | bytes accessed | tf_op | source)
XLA Modules:
  0.0 130.4 jit_solution(9932260965176869231)
XLA Ops:
  0.1 3.1 %shard_map.73 = (s32[128,1]{1,0:T(8,128)S(1)}, bf16[40,5120]{1,0:T(8,128)(2,1)S(1)}) custom-call(s32[3]{0:T(128)S(1)} %pad_add_fusion.place, bf16[128,5120]{1,0:T(8,128)(2,1)} %refs_0_.1, s32[1,128]{1,0:T(1,128)} %bitcast.14, f32[1,5120]{1,0:T(1,128)} %bitcast.13, bf16[16,5120]{1,0:T(8,128)(2,1)} %bitcast.12), custom_call_target="tpu_custom_call" | custom-call | tf_op jit(solution)/shard_map/pallas_call | solution.py:159
  4.2 2.8 %collective-permute-start.1 = (bf16[10,5120]{1,0:T(8,128)(2,1)S(1)}, bf16[10,5120]{1,0:T(8,128)(2,1)S(1)}, u32[]{:S(2)}, u32[]{:S(2)}) collective-permute-start(bf16[10,5120]{1,0:T(8,128)(2,1)S(1)} %get-tuple-element.77), channel_id=1, source_target_pairs={{0,128},{64,192},{128,0},{192,64},{1,129},{65,193},{129,1},{193,65... | collective-permute-start | bytes 307208 | tf_op jit(solution)/shard_map/ppermute | solution.py:42
  7.4 4.5 %shard_map.74 = (bf16[5120,384]{1,0:T(8,128)(2,1)S(1)}, bf16[5120,384]{1,0:T(8,128)(2,1)S(1)}, bf16[384,5120]{1,0:T(8,128)(2,1)S(1)}) custom-call(bf16[5120,384]{1,0:T(8,128)(2,1)} %bitcast.9, bf16[5120,384]{1,0:T(8,128)(2,1)} %bitcast.10, bf16[384,5120]{1,0:T(8,128)(2,1)} %bitcast.11), custom_call_target="tpu_custom_call" | custom-call | tf_op jit(solution)/shard_map/pallas_call | solution.py:190
  11.9 2.2 %collective-permute-done.2 = bf16[10,5120]{1,0:T(8,128)(2,1)S(1)} collective-permute-done((bf16[10,5120]{1,0:T(8,128)(2,1)S(1)}, bf16[10,5120]{1,0:T(8,128)(2,1)S(1)}, u32[]{:S(2)}, u32[]{:S(2)}) %collective-permute-start.2) | collective-permute-done | bytes 102432 | tf_op jit(solution)/shard_map/ppermute | solution.py:42
  14.9 2.0 %collective-permute-start.3 = (bf16[40,5120]{1,0:T(8,128)(2,1)S(1)}, bf16[40,5120]{1,0:T(8,128)(2,1)S(1)}, u32[]{:S(2)}, u32[]{:S(2)}) collective-permute-start(bf16[40,5120]{1,0:T(8,128)(2,1)S(1)} %pad_maximum_fusion.refs_0_), channel_id=1, source_target_pairs={{0,2},{1,15},{2,4},{3,1},{4,6},{5,3},{6,8},{7,5},{8,10},{9,7},{10,... | collective-permute-start | bytes 1228808 | tf_op jit(solution)/shard_map/far_rows/ppermute | solution.py:49
  16.9 1.9 %collective-permute-start.6 = (bf16[40,5120]{1,0:T(8,128)(2,1)S(1)}, bf16[40,5120]{1,0:T(8,128)(2,1)S(1)}, u32[]{:S(2)}, u32[]{:S(2)}) collective-permute-start(bf16[40,5120]{1,0:T(8,128)(2,1)S(1)} %collective-permute-done.4.refs_1_), channel_id=1, source_target_pairs={{0,2},{1,15},{2,4},{3,1},{4,6},{5,3},{6,8},{7,5},{8,10},{9,7},{10,... | collective-permute-start | bytes 1228808 | tf_op jit(solution)/shard_map/near_rows/ppermute | solution.py:49
  18.9 2.7 %shard_map.75 = (bf16[40,5120]{1,0:T(8,128)(2,1)S(1)}, bf16[40,5120]{1,0:T(8,128)(2,1)S(1)}) custom-call(bf16[40,5120]{1,0:T(8,128)(2,1)S(1)} %pad_maximum_fusion.refs_0_, bf16[40,5120]{1,0:T(8,128)(2,1)S(1)} %collective-permute-done.4.refs_1_, bf16[5120,384]{1,0:T(8,128)(2,1)S(1)} %get-tuple-element.40.refs_2_.refs_4_, ...), custom_call_target="tpu_custom_call" | custom-call | tf_op jit(solution)/shard_map/pallas_call | solution.py:233
  21.5 3.6 %collective-permute-start.7 = (bf16[40,5120]{1,0:T(8,128)(2,1)S(1)}, bf16[40,5120]{1,0:T(8,128)(2,1)S(1)}, u32[]{:S(2)}, u32[]{:S(2)}) collective-permute-start(bf16[40,5120]{1,0:T(8,128)(2,1)S(1)} %get-tuple-element.46), channel_id=1, source_target_pairs={{0,1},{1,0},{2,3},{3,2},{4,5},{5,4},{6,7},{7,6},{8,9},{9,8},{10,11... | collective-permute-start | bytes 1228808 | tf_op jit(solution)/shard_map/other_core/ppermute | solution.py:72
  25.1 1.7 %collective-permute-done.3.refs_0_ = bf16[40,5120]{1,0:T(8,128)(2,1)S(1)} collective-permute-done((bf16[40,5120]{1,0:T(8,128)(2,1)S(1)}, bf16[40,5120]{1,0:T(8,128)(2,1)S(1)}, u32[]{:S(2)}, u32[]{:S(2)}) %collective-permute-start.3) | collective-permute-done | bytes 409632 | tf_op jit(solution)/shard_map/far_rows/ppermute | solution.py:49
  26.8 2.2 %collective-permute-start.10 = (bf16[40,5120]{1,0:T(8,128)(2,1)S(1)}, bf16[40,5120]{1,0:T(8,128)(2,1)S(1)}, u32[]{:S(2)}, u32[]{:S(2)}) collective-permute-start(bf16[40,5120]{1,0:T(8,128)(2,1)S(1)} %collective-permute-done.3.refs_0_), channel_id=1, source_target_pairs={{0,1},{1,0},{2,3},{3,2},{4,5},{5,4},{6,7},{7,6},{8,9},{9,8},{10,11... | collective-permute-start | bytes 1228808 | tf_op jit(solution)/shard_map/other_core/ppermute | solution.py:72
  29.0 2.2 %collective-permute-done.6.refs_1_ = bf16[40,5120]{1,0:T(8,128)(2,1)S(1)} collective-permute-done((bf16[40,5120]{1,0:T(8,128)(2,1)S(1)}, bf16[40,5120]{1,0:T(8,128)(2,1)S(1)}, u32[]{:S(2)}, u32[]{:S(2)}) %collective-permute-start.6) | collective-permute-done | bytes 409632 | tf_op jit(solution)/shard_map/near_rows/ppermute | solution.py:49
  31.2 4.8 %collective-permute-done.5.refs_0_ = bf16[40,5120]{1,0:T(8,128)(2,1)S(1)} collective-permute-done((bf16[40,5120]{1,0:T(8,128)(2,1)S(1)}, bf16[40,5120]{1,0:T(8,128)(2,1)S(1)}, u32[]{:S(2)}, u32[]{:S(2)}) %collective-permute-start.5) | collective-permute-done | bytes 409632 | tf_op jit(solution)/shard_map/far_rows/ppermute | solution.py:49
  36.0 2.9 %shard_map.76 = (bf16[40,5120]{1,0:T(8,128)(2,1)S(1)}, bf16[40,5120]{1,0:T(8,128)(2,1)S(1)}, bf16[40,5120]{1,0:T(8,128)(2,1)S(1)}, bf16[40,5120]{1,0:T(8,128)(2,1)S(1)}) custom-call(bf16[40,5120]{1,0:T(8,128)(2,1)S(1)} %collective-permute-done.3.refs_0_, bf16[40,5120]{1,0:T(8,128)(2,1)S(1)} %collective-permute-done.6.refs_1_, ...), custom_call_target="tpu_custom_call" | custom-call | tf_op jit(solution)/shard_map/pallas_call | solution.py:233
  38.9 1.9 %collective-permute-start.12 = (bf16[40,5120]{1,0:T(8,128)(2,1)S(1)}, bf16[40,5120]{1,0:T(8,128)(2,1)S(1)}, u32[]{:S(2)}, u32[]{:S(2)}) collective-permute-start(bf16[40,5120]{1,0:T(8,128)(2,1)S(1)} %get-tuple-element.51), channel_id=1, source_target_pairs={{0,1},{1,0},{2,3},{3,2},{4,5},{5,4},{6,7},{7,6},{8,9},{9,8},{10,11... | collective-permute-start | bytes 1228808 | tf_op jit(solution)/shard_map/other_core/ppermute | solution.py:72
  41.4 3.8 %collective-permute-done.8.refs_0_ = bf16[40,5120]{1,0:T(8,128)(2,1)S(1)} collective-permute-done((bf16[40,5120]{1,0:T(8,128)(2,1)S(1)}, bf16[40,5120]{1,0:T(8,128)(2,1)S(1)}, u32[]{:S(2)}, u32[]{:S(2)}) %collective-permute-start.8) | collective-permute-done | bytes 409632 | tf_op jit(solution)/shard_map/far_rows/ppermute | solution.py:49
  46.6 2.9 %shard_map.77 = (bf16[40,5120]{1,0:T(8,128)(2,1)S(1)}, bf16[40,5120]{1,0:T(8,128)(2,1)S(1)}, bf16[40,5120]{1,0:T(8,128)(2,1)S(1)}, bf16[40,5120]{1,0:T(8,128)(2,1)S(1)}) custom-call(bf16[40,5120]{1,0:T(8,128)(2,1)S(1)} %collective-permute-done.5.refs_0_, bf16[40,5120]{1,0:T(8,128)(2,1)S(1)} %collective-permute-done.9.refs_1_, ...), custom_call_target="tpu_custom_call" | custom-call | tf_op jit(solution)/shard_map/pallas_call | solution.py:233
  50.5 2.7 %shard_map.78 = (bf16[40,5120]{1,0:T(8,128)(2,1)S(1)}, bf16[40,5120]{1,0:T(8,128)(2,1)S(1)}) custom-call(bf16[40,5120]{1,0:T(8,128)(2,1)S(1)} %collective-permute-done.8.refs_0_, bf16[40,5120]{1,0:T(8,128)(2,1)S(1)} %collective-permute-done.17.refs_1_, bf16[5120,384]{1,0:T(8,128)(2,1)S(1)} %get-tuple-element.40.refs_2_.refs_4_, ...), custom_call_target="tpu_custom_call" | custom-call | tf_op jit(solution)/shard_map/pallas_call | solution.py:233
  56.7 2.7 %shard_map.79 = (bf16[40,5120]{1,0:T(8,128)(2,1)S(1)}, bf16[40,5120]{1,0:T(8,128)(2,1)S(1)}) custom-call(bf16[40,5120]{1,0:T(8,128)(2,1)S(1)} %collective-permute-done.13.refs_0_, bf16[40,5120]{1,0:T(8,128)(2,1)S(1)} %collective-permute-done.21.refs_1_, bf16[5120,384]{1,0:T(8,128)(2,1)S(1)} %get-tuple-element.40.refs_2_.refs_4_, ...), custom_call_target="tpu_custom_call" | custom-call | tf_op jit(solution)/shard_map/pallas_call | solution.py:233
  62.3 2.7 %shard_map.80 = (bf16[40,5120]{1,0:T(8,128)(2,1)S(1)}, bf16[40,5120]{1,0:T(8,128)(2,1)S(1)}) custom-call(bf16[40,5120]{1,0:T(8,128)(2,1)S(1)} %collective-permute-done.14.refs_0_, bf16[40,5120]{1,0:T(8,128)(2,1)S(1)} %collective-permute-done.24.refs_1_, bf16[5120,384]{1,0:T(8,128)(2,1)S(1)} %get-tuple-element.40.refs_2_.refs_4_, ...), custom_call_target="tpu_custom_call" | custom-call | tf_op jit(solution)/shard_map/pallas_call | solution.py:233
  66.8 3.7 %collective-permute-done.23 = bf16[40,5120]{1,0:T(8,128)(2,1)S(1)} collective-permute-done((bf16[40,5120]{1,0:T(8,128)(2,1)S(1)}, bf16[40,5120]{1,0:T(8,128)(2,1)S(1)}, u32[]{:S(2)}, u32[]{:S(2)}) %collective-permute-start.23) | collective-permute-done | bytes 409632 | tf_op jit(solution)/shard_map/far_sum/ppermute | solution.py:49
  70.7 4.1 %collective-permute-done.29 = bf16[40,5120]{1,0:T(8,128)(2,1)S(1)} collective-permute-done((bf16[40,5120]{1,0:T(8,128)(2,1)S(1)}, bf16[40,5120]{1,0:T(8,128)(2,1)S(1)}, u32[]{:S(2)}, u32[]{:S(2)}) %collective-permute-start.29) | collective-permute-done | bytes 409632 | tf_op jit(solution)/shard_map/near_sum/ppermute | solution.py:49
  75.1 4.8 %collective-permute-done.26 = bf16[40,5120]{1,0:T(8,128)(2,1)S(1)} collective-permute-done((bf16[40,5120]{1,0:T(8,128)(2,1)S(1)}, bf16[40,5120]{1,0:T(8,128)(2,1)S(1)}, u32[]{:S(2)}, u32[]{:S(2)}) %collective-permute-start.26) | collective-permute-done | bytes 409632 | tf_op jit(solution)/shard_map/far_sum/ppermute | solution.py:49
  80.1 4.1 %collective-permute-done.30 = bf16[40,5120]{1,0:T(8,128)(2,1)S(1)} collective-permute-done((bf16[40,5120]{1,0:T(8,128)(2,1)S(1)}, bf16[40,5120]{1,0:T(8,128)(2,1)S(1)}, u32[]{:S(2)}, u32[]{:S(2)}) %collective-permute-start.30) | collective-permute-done | bytes 409632 | tf_op jit(solution)/shard_map/near_sum/ppermute | solution.py:49
  84.5 4.8 %collective-permute-done.27 = bf16[40,5120]{1,0:T(8,128)(2,1)S(1)} collective-permute-done((bf16[40,5120]{1,0:T(8,128)(2,1)S(1)}, bf16[40,5120]{1,0:T(8,128)(2,1)S(1)}, u32[]{:S(2)}, u32[]{:S(2)}) %collective-permute-start.27) | collective-permute-done | bytes 409632 | tf_op jit(solution)/shard_map/far_sum/ppermute | solution.py:49
  89.5 2.4 %collective-permute-done.32 = bf16[40,5120]{1,0:T(8,128)(2,1)S(1)} collective-permute-done((bf16[40,5120]{1,0:T(8,128)(2,1)S(1)}, bf16[40,5120]{1,0:T(8,128)(2,1)S(1)}, u32[]{:S(2)}, u32[]{:S(2)}) %collective-permute-start.32) | collective-permute-done | bytes 409632 | tf_op jit(solution)/shard_map/near_sum/ppermute | solution.py:56
  91.9 6.8 %collective-permute-done.28 = bf16[40,5120]{1,0:T(8,128)(2,1)S(1)} collective-permute-done((bf16[40,5120]{1,0:T(8,128)(2,1)S(1)}, bf16[40,5120]{1,0:T(8,128)(2,1)S(1)}, u32[]{:S(2)}, u32[]{:S(2)}) %collective-permute-start.28) | collective-permute-done | bytes 409632 | tf_op jit(solution)/shard_map/far_sum/ppermute | solution.py:49
  99.0 2.7 %collective-permute-start.35 = (bf16[10,5120]{1,0:T(8,128)(2,1)S(1)}, bf16[10,5120]{1,0:T(8,128)(2,1)S(1)}, u32[]{:S(2)}, u32[]{:S(2)}) collective-permute-start(bf16[10,5120]{1,0:T(8,128)(2,1)S(1)} %get-tuple-element.72), channel_id=1, source_target_pairs={{0,64},{64,128},{128,192},{192,0},{1,65},{65,129},{129,193},{193,1... | collective-permute-start | bytes 307208 | tf_op jit(solution)/shard_map/ppermute | solution.py:42
  102.7 3.9 %collective-permute-done.35 = bf16[10,5120]{1,0:T(8,128)(2,1)S(1)} collective-permute-done((bf16[10,5120]{1,0:T(8,128)(2,1)S(1)}, bf16[10,5120]{1,0:T(8,128)(2,1)S(1)}, u32[]{:S(2)}, u32[]{:S(2)}) %collective-permute-start.35) | collective-permute-done | bytes 102432 | tf_op jit(solution)/shard_map/ppermute | solution.py:42
  106.6 2.1 %collective-permute-done.34 = bf16[10,5120]{1,0:T(8,128)(2,1)S(1)} collective-permute-done((bf16[10,5120]{1,0:T(8,128)(2,1)S(1)}, bf16[10,5120]{1,0:T(8,128)(2,1)S(1)}, u32[]{:S(2)}, u32[]{:S(2)}) %collective-permute-start.34) | collective-permute-done | bytes 102432 | tf_op jit(solution)/shard_map/ppermute | solution.py:42
  113.8 5.9 %collective-permute-done.39.refs_3_ = bf16[40,5120]{1,0:T(8,128)(2,1)S(1)} collective-permute-done((bf16[40,5120]{1,0:T(8,128)(2,1)S(1)}, bf16[40,5120]{1,0:T(8,128)(2,1)S(1)}, u32[]{:S(2)}, u32[]{:S(2)}) %collective-permute-start.39) | collective-permute-done | bytes 409632 | tf_op jit(solution)/shard_map/ppermute | solution.py:66
  120.1 4.0 %collective-permute-done.37 = bf16[40,5120]{1,0:T(8,128)(2,1)S(1)} collective-permute-done((bf16[40,5120]{1,0:T(8,128)(2,1)S(1)}, bf16[40,5120]{1,0:T(8,128)(2,1)S(1)}, u32[]{:S(2)}, u32[]{:S(2)}) %collective-permute-start.37) | collective-permute-done | bytes 409632 | tf_op jit(solution)/shard_map/ppermute | solution.py:66
  124.1 4.8 %collective-permute-done.40.refs_2_ = bf16[40,5120]{1,0:T(8,128)(2,1)S(1)} collective-permute-done((bf16[40,5120]{1,0:T(8,128)(2,1)S(1)}, bf16[40,5120]{1,0:T(8,128)(2,1)S(1)}, u32[]{:S(2)}, u32[]{:S(2)}) %collective-permute-start.40) | collective-permute-done | bytes 409632 | tf_op jit(solution)/shard_map/ppermute | solution.py:66
  (72 shorter events, 22.9 us)
Async XLA Ops:
  3.3 10.7 %collective-permute-start.2 = (bf16[10,5120]{1,0:T(8,128)(2,1)S(1)}, bf16[10,5120]{1,0:T(8,128)(2,1)S(1)}, u32[]{:S(2)}, u32[]{:S(2)}) collective-permute-start(bf16[10,5120]{1,0:T(8,128)(2,1)S(1)} %get-tuple-element.76), channel_id=1, source_target_pairs={{0,192},{64,0},{128,64},{192,128},{1,193},{65,1},{129,65},{193,129... | collective-permute-start | bytes 307208 | tf_op jit(solution)/shard_map/ppermute | solution.py:42
  4.2 9.8 %collective-permute-start.1 = (bf16[10,5120]{1,0:T(8,128)(2,1)S(1)}, bf16[10,5120]{1,0:T(8,128)(2,1)S(1)}, u32[]{:S(2)}, u32[]{:S(2)}) collective-permute-start(bf16[10,5120]{1,0:T(8,128)(2,1)S(1)} %get-tuple-element.77), channel_id=1, source_target_pairs={{0,128},{64,192},{128,0},{192,64},{1,129},{65,193},{129,1},{193,65... | collective-permute-start | bytes 307208 | tf_op jit(solution)/shard_map/ppermute | solution.py:42
  7.1 7.6 %collective-permute-start = (bf16[10,5120]{1,0:T(8,128)(2,1)S(1)}, bf16[10,5120]{1,0:T(8,128)(2,1)S(1)}, u32[]{:S(2)}, u32[]{:S(2)}) collective-permute-start(bf16[10,5120]{1,0:T(8,128)(2,1)S(1)} %get-tuple-element.78), channel_id=1, source_target_pairs={{0,64},{64,128},{128,192},{192,0},{1,65},{65,129},{129,193},{193,1... | collective-permute-start | bytes 307208 | tf_op jit(solution)/shard_map/ppermute | solution.py:42
  14.9 11.9 %collective-permute-start.3 = (bf16[40,5120]{1,0:T(8,128)(2,1)S(1)}, bf16[40,5120]{1,0:T(8,128)(2,1)S(1)}, u32[]{:S(2)}, u32[]{:S(2)}) collective-permute-start(bf16[40,5120]{1,0:T(8,128)(2,1)S(1)} %pad_maximum_fusion.refs_0_), channel_id=1, source_target_pairs={{0,2},{1,15},{2,4},{3,1},{4,6},{5,3},{6,8},{7,5},{8,10},{9,7},{10,... | collective-permute-start | bytes 1228808 | tf_op jit(solution)/shard_map/far_rows/ppermute | solution.py:49
  16.9 14.3 %collective-permute-start.6 = (bf16[40,5120]{1,0:T(8,128)(2,1)S(1)}, bf16[40,5120]{1,0:T(8,128)(2,1)S(1)}, u32[]{:S(2)}, u32[]{:S(2)}) collective-permute-start(bf16[40,5120]{1,0:T(8,128)(2,1)S(1)} %collective-permute-done.4.refs_1_), channel_id=1, source_target_pairs={{0,2},{1,15},{2,4},{3,1},{4,6},{5,3},{6,8},{7,5},{8,10},{9,7},{10,... | collective-permute-start | bytes 1228808 | tf_op jit(solution)/shard_map/near_rows/ppermute | solution.py:49
  21.5 9.7 %collective-permute-start.7 = (bf16[40,5120]{1,0:T(8,128)(2,1)S(1)}, bf16[40,5120]{1,0:T(8,128)(2,1)S(1)}, u32[]{:S(2)}, u32[]{:S(2)}) collective-permute-start(bf16[40,5120]{1,0:T(8,128)(2,1)S(1)} %get-tuple-element.46), channel_id=1, source_target_pairs={{0,1},{1,0},{2,3},{3,2},{4,5},{5,4},{6,7},{7,6},{8,9},{9,8},{10,11... | collective-permute-start | bytes 1228808 | tf_op jit(solution)/shard_map/other_core/ppermute | solution.py:72
  26.8 9.2 %collective-permute-start.5 = (bf16[40,5120]{1,0:T(8,128)(2,1)S(1)}, bf16[40,5120]{1,0:T(8,128)(2,1)S(1)}, u32[]{:S(2)}, u32[]{:S(2)}) collective-permute-start(bf16[40,5120]{1,0:T(8,128)(2,1)S(1)} %collective-permute-done.3.refs_0_), channel_id=1, source_target_pairs={{0,2},{1,15},{2,4},{3,1},{4,6},{5,3},{6,8},{7,5},{8,10},{9,7},{10,... | collective-permute-start | bytes 1228808 | tf_op jit(solution)/shard_map/far_rows/ppermute | solution.py:49
  26.8 9.2 %collective-permute-start.10 = (bf16[40,5120]{1,0:T(8,128)(2,1)S(1)}, bf16[40,5120]{1,0:T(8,128)(2,1)S(1)}, u32[]{:S(2)}, u32[]{:S(2)}) collective-permute-start(bf16[40,5120]{1,0:T(8,128)(2,1)S(1)} %collective-permute-done.3.refs_0_), channel_id=1, source_target_pairs={{0,1},{1,0},{2,3},{3,2},{4,5},{5,4},{6,7},{7,6},{8,9},{9,8},{10,11... | collective-permute-start | bytes 1228808 | tf_op jit(solution)/shard_map/other_core/ppermute | solution.py:72
  31.2 4.8 %collective-permute-start.11 = (bf16[40,5120]{1,0:T(8,128)(2,1)S(1)}, bf16[40,5120]{1,0:T(8,128)(2,1)S(1)}, u32[]{:S(2)}, u32[]{:S(2)}) collective-permute-start(bf16[40,5120]{1,0:T(8,128)(2,1)S(1)} %collective-permute-done.6.refs_1_), channel_id=1, source_target_pairs={{0,1},{1,0},{2,3},{3,2},{4,5},{5,4},{6,7},{7,6},{8,9},{9,8},{10,11... | collective-permute-start | bytes 1228808 | tf_op jit(solution)/shard_map/other_core/ppermute | solution.py:72
  31.2 9.9 %collective-permute-start.9 = (bf16[40,5120]{1,0:T(8,128)(2,1)S(1)}, bf16[40,5120]{1,0:T(8,128)(2,1)S(1)}, u32[]{:S(2)}, u32[]{:S(2)}) collective-permute-start(bf16[40,5120]{1,0:T(8,128)(2,1)S(1)} %collective-permute-done.6.refs_1_), channel_id=1, source_target_pairs={{0,2},{1,15},{2,4},{3,1},{4,6},{5,3},{6,8},{7,5},{8,10},{9,7},{10,... | collective-permute-start | bytes 1228808 | tf_op jit(solution)/shard_map/near_rows/ppermute | solution.py:49
  36.0 9.2 %collective-permute-start.8 = (bf16[40,5120]{1,0:T(8,128)(2,1)S(1)}, bf16[40,5120]{1,0:T(8,128)(2,1)S(1)}, u32[]{:S(2)}, u32[]{:S(2)}) collective-permute-start(bf16[40,5120]{1,0:T(8,128)(2,1)S(1)} %collective-permute-done.5.refs_0_), channel_id=1, source_target_pairs={{0,2},{1,15},{2,4},{3,1},{4,6},{5,3},{6,8},{7,5},{8,10},{9,7},{10,... | collective-permute-start | bytes 1228808 | tf_op jit(solution)/shard_map/far_rows/ppermute | solution.py:49
  38.9 6.2 %collective-permute-start.12 = (bf16[40,5120]{1,0:T(8,128)(2,1)S(1)}, bf16[40,5120]{1,0:T(8,128)(2,1)S(1)}, u32[]{:S(2)}, u32[]{:S(2)}) collective-permute-start(bf16[40,5120]{1,0:T(8,128)(2,1)S(1)} %get-tuple-element.51), channel_id=1, source_target_pairs={{0,1},{1,0},{2,3},{3,2},{4,5},{5,4},{6,7},{7,6},{8,9},{9,8},{10,11... | collective-permute-start | bytes 1228808 | tf_op jit(solution)/shard_map/other_core/ppermute | solution.py:72
  40.8 5.8 %collective-permute-start.15 = (bf16[40,5120]{1,0:T(8,128)(2,1)S(1)}, bf16[40,5120]{1,0:T(8,128)(2,1)S(1)}, u32[]{:S(2)}, u32[]{:S(2)}) collective-permute-start(bf16[40,5120]{1,0:T(8,128)(2,1)S(1)} %collective-permute-done.5.refs_0_), channel_id=1, source_target_pairs={{0,1},{1,0},{2,3},{3,2},{4,5},{5,4},{6,7},{7,6},{8,9},{9,8},{10,11... | collective-permute-start | bytes 1228808 | tf_op jit(solution)/shard_map/other_core/ppermute | solution.py:72
  41.1 5.5 %collective-permute-start.16 = (bf16[40,5120]{1,0:T(8,128)(2,1)S(1)}, bf16[40,5120]{1,0:T(8,128)(2,1)S(1)}, u32[]{:S(2)}, u32[]{:S(2)}) collective-permute-start(bf16[40,5120]{1,0:T(8,128)(2,1)S(1)} %collective-permute-done.9.refs_1_), channel_id=1, source_target_pairs={{0,1},{1,0},{2,3},{3,2},{4,5},{5,4},{6,7},{7,6},{8,9},{9,8},{10,11... | collective-permute-start | bytes 1228808 | tf_op jit(solution)/shard_map/other_core/ppermute | solution.py:72
  41.4 9.2 %collective-permute-start.14 = (bf16[40,5120]{1,0:T(8,128)(2,1)S(1)}, bf16[40,5120]{1,0:T(8,128)(2,1)S(1)}, u32[]{:S(2)}, u32[]{:S(2)}) collective-permute-start(bf16[40,5120]{1,0:T(8,128)(2,1)S(1)} %collective-permute-done.9.refs_1_), channel_id=1, source_target_pairs={{0,2},{1,15},{2,4},{3,1},{4,6},{5,3},{6,8},{7,5},{8,10},{9,7},{10,... | collective-permute-start | bytes 1228808 | tf_op jit(solution)/shard_map/near_rows/ppermute | solution.py:49
  45.1 9.8 %collective-permute-start.13 = (bf16[40,5120]{1,0:T(8,128)(2,1)S(1)}, bf16[40,5120]{1,0:T(8,128)(2,1)S(1)}, u32[]{:S(2)}, u32[]{:S(2)}) collective-permute-start(bf16[40,5120]{1,0:T(8,128)(2,1)S(1)} %collective-permute-done.8.refs_0_), channel_id=1, source_target_pairs={{0,2},{1,15},{2,4},{3,1},{4,6},{5,3},{6,8},{7,5},{8,10},{9,7},{10,... | collective-permute-start | bytes 1228808 | tf_op jit(solution)/shard_map/far_rows/ppermute | solution.py:49
  45.1 5.4 %collective-permute-start.17 = (bf16[40,5120]{1,0:T(8,128)(2,1)S(1)}, bf16[40,5120]{1,0:T(8,128)(2,1)S(1)}, u32[]{:S(2)}, u32[]{:S(2)}) collective-permute-start(bf16[40,5120]{1,0:T(8,128)(2,1)S(1)} %collective-permute-done.8.refs_0_), channel_id=1, source_target_pairs={{0,1},{1,0},{2,3},{3,2},{4,5},{5,4},{6,7},{7,6},{8,9},{9,8},{10,11... | collective-permute-start | bytes 1228808 | tf_op jit(solution)/shard_map/other_core/ppermute | solution.py:72
  49.6 5.3 %collective-permute-start.18 = (bf16[40,5120]{1,0:T(8,128)(2,1)S(1)}, bf16[40,5120]{1,0:T(8,128)(2,1)S(1)}, u32[]{:S(2)}, u32[]{:S(2)}) collective-permute-start(bf16[40,5120]{1,0:T(8,128)(2,1)S(1)} %get-tuple-element.53), channel_id=1, source_target_pairs={{0,1},{1,0},{2,3},{3,2},{4,5},{5,4},{6,7},{7,6},{8,9},{9,8},{10,11... | collective-permute-start | bytes 1228808 | tf_op jit(solution)/shard_map/other_core/ppermute | solution.py:72
  59.5 20.6 %collective-permute-start.31 = (bf16[40,5120]{1,0:T(8,128)(2,1)S(1)}, bf16[40,5120]{1,0:T(8,128)(2,1)S(1)}, u32[]{:S(2)}, u32[]{:S(2)}) collective-permute-start(bf16[40,5120]{1,0:T(8,128)(2,1)S(1)} %get-tuple-element.48), channel_id=1, source_target_pairs={{0,1},{1,0},{2,3},{3,2},{4,5},{5,4},{6,7},{7,6},{8,9},{9,8},{10,11... | collective-permute-start | bytes 1228808 | tf_op jit(solution)/shard_map/other_core/ppermute | solution.py:72
  61.2 9.2 %collective-permute-start.23 = (bf16[40,5120]{1,0:T(8,128)(2,1)S(1)}, bf16[40,5120]{1,0:T(8,128)(2,1)S(1)}, u32[]{:S(2)}, u32[]{:S(2)}) collective-permute-start(bf16[40,5120]{1,0:T(8,128)(2,1)S(1)} %add_convert_fusion.7), channel_id=1, source_target_pairs={{0,2},{1,15},{2,4},{3,1},{4,6},{5,3},{6,8},{7,5},{8,10},{9,7},{10,... | collective-permute-start | bytes 1228808 | tf_op jit(solution)/shard_map/far_sum/ppermute | solution.py:49
  65.3 9.6 %collective-permute-start.29 = (bf16[40,5120]{1,0:T(8,128)(2,1)S(1)}, bf16[40,5120]{1,0:T(8,128)(2,1)S(1)}, u32[]{:S(2)}, u32[]{:S(2)}) collective-permute-start(bf16[40,5120]{1,0:T(8,128)(2,1)S(1)} %add_convert_fusion.3), channel_id=1, source_target_pairs={{0,2},{1,15},{2,4},{3,1},{4,6},{5,3},{6,8},{7,5},{8,10},{9,7},{10,... | collective-permute-start | bytes 1228808 | tf_op jit(solution)/shard_map/near_sum/ppermute | solution.py:49
  70.6 9.2 %collective-permute-start.26 = (bf16[40,5120]{1,0:T(8,128)(2,1)S(1)}, bf16[40,5120]{1,0:T(8,128)(2,1)S(1)}, u32[]{:S(2)}, u32[]{:S(2)}) collective-permute-start(bf16[40,5120]{1,0:T(8,128)(2,1)S(1)} %add_convert_fusion.6), channel_id=1, source_target_pairs={{0,2},{1,15},{2,4},{3,1},{4,6},{5,3},{6,8},{7,5},{8,10},{9,7},{10,... | collective-permute-start | bytes 1228808 | tf_op jit(solution)/shard_map/far_sum/ppermute | solution.py:49
  75.0 9.2 %collective-permute-start.30 = (bf16[40,5120]{1,0:T(8,128)(2,1)S(1)}, bf16[40,5120]{1,0:T(8,128)(2,1)S(1)}, u32[]{:S(2)}, u32[]{:S(2)}) collective-permute-start(bf16[40,5120]{1,0:T(8,128)(2,1)S(1)} %add_convert_fusion.2), channel_id=1, source_target_pairs={{0,2},{1,15},{2,4},{3,1},{4,6},{5,3},{6,8},{7,5},{8,10},{9,7},{10,... | collective-permute-start | bytes 1228808 | tf_op jit(solution)/shard_map/near_sum/ppermute | solution.py:49
  80.0 9.2 %collective-permute-start.27 = (bf16[40,5120]{1,0:T(8,128)(2,1)S(1)}, bf16[40,5120]{1,0:T(8,128)(2,1)S(1)}, u32[]{:S(2)}, u32[]{:S(2)}) collective-permute-start(bf16[40,5120]{1,0:T(8,128)(2,1)S(1)} %add_convert_fusion.5), channel_id=1, source_target_pairs={{0,2},{1,15},{2,4},{3,1},{4,6},{5,3},{6,8},{7,5},{8,10},{9,7},{10,... | collective-permute-start | bytes 1228808 | tf_op jit(solution)/shard_map/far_sum/ppermute | solution.py:49
  84.4 7.5 %collective-permute-start.32 = (bf16[40,5120]{1,0:T(8,128)(2,1)S(1)}, bf16[40,5120]{1,0:T(8,128)(2,1)S(1)}, u32[]{:S(2)}, u32[]{:S(2)}) collective-permute-start(bf16[40,5120]{1,0:T(8,128)(2,1)S(1)} %add_convert_fusion.1), channel_id=1, source_target_pairs={{0,3},{1,14},{2,5},{3,0},{4,7},{5,2},{6,9},{7,4},{8,11},{9,6},{10,... | collective-permute-start | bytes 1228808 | tf_op jit(solution)/shard_map/near_sum/ppermute | solution.py:56
  89.4 9.2 %collective-permute-start.28 = (bf16[40,5120]{1,0:T(8,128)(2,1)S(1)}, bf16[40,5120]{1,0:T(8,128)(2,1)S(1)}, u32[]{:S(2)}, u32[]{:S(2)}) collective-permute-start(bf16[40,5120]{1,0:T(8,128)(2,1)S(1)} %add_convert_fusion.4), channel_id=1, source_target_pairs={{0,2},{1,15},{2,4},{3,1},{4,6},{5,3},{6,8},{7,5},{8,10},{9,7},{10,... | collective-permute-start | bytes 1228808 | tf_op jit(solution)/shard_map/far_sum/ppermute | solution.py:49
  99.0 7.6 %collective-permute-start.35 = (bf16[10,5120]{1,0:T(8,128)(2,1)S(1)}, bf16[10,5120]{1,0:T(8,128)(2,1)S(1)}, u32[]{:S(2)}, u32[]{:S(2)}) collective-permute-start(bf16[10,5120]{1,0:T(8,128)(2,1)S(1)} %get-tuple-element.72), channel_id=1, source_target_pairs={{0,64},{64,128},{128,192},{192,0},{1,65},{65,129},{129,193},{193,1... | collective-permute-start | bytes 307208 | tf_op jit(solution)/shard_map/ppermute | solution.py:42
  101.7 7.0 %collective-permute-start.34 = (bf16[10,5120]{1,0:T(8,128)(2,1)S(1)}, bf16[10,5120]{1,0:T(8,128)(2,1)S(1)}, u32[]{:S(2)}, u32[]{:S(2)}) collective-permute-start(bf16[10,5120]{1,0:T(8,128)(2,1)S(1)} %get-tuple-element.73), channel_id=1, source_target_pairs={{0,128},{64,192},{128,0},{192,64},{1,129},{65,193},{129,1},{193,65... | collective-permute-start | bytes 307208 | tf_op jit(solution)/shard_map/ppermute | solution.py:42
  101.9 8.3 %collective-permute-start.33 = (bf16[10,5120]{1,0:T(8,128)(2,1)S(1)}, bf16[10,5120]{1,0:T(8,128)(2,1)S(1)}, u32[]{:S(2)}, u32[]{:S(2)}) collective-permute-start(bf16[10,5120]{1,0:T(8,128)(2,1)S(1)} %get-tuple-element.74), channel_id=1, source_target_pairs={{0,192},{64,0},{128,64},{192,128},{1,193},{65,1},{129,65},{193,129... | collective-permute-start | bytes 307208 | tf_op jit(solution)/shard_map/ppermute | solution.py:42
  110.5 9.2 %collective-permute-start.39 = (bf16[40,5120]{1,0:T(8,128)(2,1)S(1)}, bf16[40,5120]{1,0:T(8,128)(2,1)S(1)}, u32[]{:S(2)}, u32[]{:S(2)}) collective-permute-start(bf16[40,5120]{1,0:T(8,128)(2,1)S(1)} %pad_maximum_fusion.1.refs_0_), channel_id=1, source_target_pairs={{0,16},{1,49},{2,18},{3,51},{4,20},{5,53},{6,22},{7,55},{8,24},{9,... | collective-permute-start | bytes 1228808 | tf_op jit(solution)/shard_map/ppermute | solution.py:66
  112.2 11.9 %collective-permute-start.37 = (bf16[40,5120]{1,0:T(8,128)(2,1)S(1)}, bf16[40,5120]{1,0:T(8,128)(2,1)S(1)}, u32[]{:S(2)}, u32[]{:S(2)}) collective-permute-start(bf16[40,5120]{1,0:T(8,128)(2,1)S(1)} %collective-permute-done.36), channel_id=1, source_target_pairs={{0,16},{1,49},{2,18},{3,51},{4,20},{5,53},{6,22},{7,55},{8,24},{9,... | collective-permute-start | bytes 1228808 | tf_op jit(solution)/shard_map/ppermute | solution.py:66
  119.7 9.2 %collective-permute-start.40 = (bf16[40,5120]{1,0:T(8,128)(2,1)S(1)}, bf16[40,5120]{1,0:T(8,128)(2,1)S(1)}, u32[]{:S(2)}, u32[]{:S(2)}) collective-permute-start(bf16[40,5120]{1,0:T(8,128)(2,1)S(1)} %collective-permute-done.39.refs_3_), channel_id=1, source_target_pairs={{0,16},{1,49},{2,18},{3,51},{4,20},{5,53},{6,22},{7,55},{8,24},{9,... | collective-permute-start | bytes 1228808 | tf_op jit(solution)/shard_map/ppermute | solution.py:66
  (9 other events, 22.1 us)

commit v5 on v4

--- a/solution.py
+++ b/solution.py
@@ -328,7 +328,7 @@
     near_sum = None
     for k in range(half - 1, 0, -1):
         part, theirs = near_terms[k - 1]
-        part = after(part, far_sum)
+        part = after(part, far_sum) if near_sum is not None else after(part, far_part)
         near_sum = add(part, theirs) if near_sum is None else add(near_sum, part, theirs)
         near_sum = (ring_step if k > 1 else ring_leave)(near_sum, "near_sum")
         far_sum = add(ring_step(far_sum, "far_sum"), *far_terms[k - 1])

time: 131 us -> 131 us (level)
  no operation moved by 1% of the time
where the time goes in v5:
time: 131 us; the launch traced here: 130 us
  waiting for transfers between devices  74.4 us (57%)
  starting transfers between devices  28.4 us (22%)
  Pallas kernels  25.4 us (19%)
  other arithmetic  1.59 us (1%)
    ppermute x13, waiting for transfers between devices, ring_step(): return lax.ppermute(values, 'expert', pairs)  42.6 us
    pallas_call x6, Pallas kernels, expert_apply(): pl.pallas_call(functools.partial(expert_kernel, groups), out_shape=[pltpu...  16.5 us
    ppermute x3, waiting for transfers between devices, tensor_step(): return lax.ppermute(values, ('tensor', 'expert'), pairs)  14.7 us
    ppermute x18, starting transfers between devices, swap(): return lax.ppermute(values, 'expert', [(i, i ^ 1) for i in range(size)])  11.5 us
    ppermute x6, waiting for transfers between devices, shift(): lax.ppermute(values, axis, [(i, (i + steps) % size) for i in range(size)])  10.3 us
    ppermute x6, starting transfers between devices, shift(): lax.ppermute(values, axis, [(i, (i + steps) % size) for i in range(size)])  7.8 us
    ppermute x13, starting transfers between devices, ring_step(): return lax.ppermute(values, 'expert', pairs)  5.4 us
    pallas_call x1, Pallas kernels, load(): pl.pallas_call(load_kernel, out_shape=[pltpu.VMEM(x.shape, x.dtype) for x...  4.45 us
  transfers between devices with their start and end apart: 41, of which 27 were waited for; matrix products, arithmetic and copies ran while one was open for 1% of the time, Pallas kernels for 14%

profile of v5, /device:TPU:6, one launch (start us, length us, event | category | flops | bytes accessed | tf_op | source)
XLA Modules:
  0.0 130.4 jit_solution(9932260965176869231)
XLA Ops:
  0.1 3.1 %shard_map.73 = (s32[128,1]{1,0:T(8,128)S(1)}, bf16[40,5120]{1,0:T(8,128)(2,1)S(1)}) custom-call(s32[3]{0:T(128)S(1)} %pad_add_fusion.place, bf16[128,5120]{1,0:T(8,128)(2,1)} %refs_0_.1, s32[1,128]{1,0:T(1,128)} %bitcast.14, f32[1,5120]{1,0:T(1,128)} %bitcast.13, bf16[16,5120]{1,0:T(8,128)(2,1)} %bitcast.12), custom_call_target="tpu_custom_call" | custom-call | tf_op jit(solution)/shard_map/pallas_call | solution.py:159
  4.2 2.8 %collective-permute-start.1 = (bf16[10,5120]{1,0:T(8,128)(2,1)S(1)}, bf16[10,5120]{1,0:T(8,128)(2,1)S(1)}, u32[]{:S(2)}, u32[]{:S(2)}) collective-permute-start(bf16[10,5120]{1,0:T(8,128)(2,1)S(1)} %get-tuple-element.77), channel_id=1, source_target_pairs={{0,128},{64,192},{128,0},{192,64},{1,129},{65,193},{129,1},{193,65... | collective-permute-start | bytes 307208 | tf_op jit(solution)/shard_map/ppermute | solution.py:42
  7.4 4.5 %shard_map.74 = (bf16[5120,384]{1,0:T(8,128)(2,1)S(1)}, bf16[5120,384]{1,0:T(8,128)(2,1)S(1)}, bf16[384,5120]{1,0:T(8,128)(2,1)S(1)}) custom-call(bf16[5120,384]{1,0:T(8,128)(2,1)} %bitcast.9, bf16[5120,384]{1,0:T(8,128)(2,1)} %bitcast.10, bf16[384,5120]{1,0:T(8,128)(2,1)} %bitcast.11), custom_call_target="tpu_custom_call" | custom-call | tf_op jit(solution)/shard_map/pallas_call | solution.py:190
  11.9 2.2 %collective-permute-done.2 = bf16[10,5120]{1,0:T(8,128)(2,1)S(1)} collective-permute-done((bf16[10,5120]{1,0:T(8,128)(2,1)S(1)}, bf16[10,5120]{1,0:T(8,128)(2,1)S(1)}, u32[]{:S(2)}, u32[]{:S(2)}) %collective-permute-start.2) | collective-permute-done | bytes 102432 | tf_op jit(solution)/shard_map/ppermute | solution.py:42
  14.9 2.0 %collective-permute-start.3 = (bf16[40,5120]{1,0:T(8,128)(2,1)S(1)}, bf16[40,5120]{1,0:T(8,128)(2,1)S(1)}, u32[]{:S(2)}, u32[]{:S(2)}) collective-permute-start(bf16[40,5120]{1,0:T(8,128)(2,1)S(1)} %pad_maximum_fusion.refs_0_), channel_id=1, source_target_pairs={{0,2},{1,15},{2,4},{3,1},{4,6},{5,3},{6,8},{7,5},{8,10},{9,7},{10,... | collective-permute-start | bytes 1228808 | tf_op jit(solution)/shard_map/far_rows/ppermute | solution.py:49
  16.9 1.9 %collective-permute-start.6 = (bf16[40,5120]{1,0:T(8,128)(2,1)S(1)}, bf16[40,5120]{1,0:T(8,128)(2,1)S(1)}, u32[]{:S(2)}, u32[]{:S(2)}) collective-permute-start(bf16[40,5120]{1,0:T(8,128)(2,1)S(1)} %collective-permute-done.4.refs_1_), channel_id=1, source_target_pairs={{0,2},{1,15},{2,4},{3,1},{4,6},{5,3},{6,8},{7,5},{8,10},{9,7},{10,... | collective-permute-start | bytes 1228808 | tf_op jit(solution)/shard_map/near_rows/ppermute | solution.py:49
  18.9 2.7 %shard_map.75 = (bf16[40,5120]{1,0:T(8,128)(2,1)S(1)}, bf16[40,5120]{1,0:T(8,128)(2,1)S(1)}) custom-call(bf16[40,5120]{1,0:T(8,128)(2,1)S(1)} %pad_maximum_fusion.refs_0_, bf16[40,5120]{1,0:T(8,128)(2,1)S(1)} %collective-permute-done.4.refs_1_, bf16[5120,384]{1,0:T(8,128)(2,1)S(1)} %get-tuple-element.40.refs_2_.refs_4_, ...), custom_call_target="tpu_custom_call" | custom-call | tf_op jit(solution)/shard_map/pallas_call | solution.py:233
  21.5 3.6 %collective-permute-start.7 = (bf16[40,5120]{1,0:T(8,128)(2,1)S(1)}, bf16[40,5120]{1,0:T(8,128)(2,1)S(1)}, u32[]{:S(2)}, u32[]{:S(2)}) collective-permute-start(bf16[40,5120]{1,0:T(8,128)(2,1)S(1)} %get-tuple-element.46), channel_id=1, source_target_pairs={{0,1},{1,0},{2,3},{3,2},{4,5},{5,4},{6,7},{7,6},{8,9},{9,8},{10,11... | collective-permute-start | bytes 1228808 | tf_op jit(solution)/shard_map/other_core/ppermute | solution.py:72
  25.1 1.7 %collective-permute-done.3.refs_0_ = bf16[40,5120]{1,0:T(8,128)(2,1)S(1)} collective-permute-done((bf16[40,5120]{1,0:T(8,128)(2,1)S(1)}, bf16[40,5120]{1,0:T(8,128)(2,1)S(1)}, u32[]{:S(2)}, u32[]{:S(2)}) %collective-permute-start.3) | collective-permute-done | bytes 409632 | tf_op jit(solution)/shard_map/far_rows/ppermute | solution.py:49
  26.8 2.2 %collective-permute-start.10 = (bf16[40,5120]{1,0:T(8,128)(2,1)S(1)}, bf16[40,5120]{1,0:T(8,128)(2,1)S(1)}, u32[]{:S(2)}, u32[]{:S(2)}) collective-permute-start(bf16[40,5120]{1,0:T(8,128)(2,1)S(1)} %collective-permute-done.3.refs_0_), channel_id=1, source_target_pairs={{0,1},{1,0},{2,3},{3,2},{4,5},{5,4},{6,7},{7,6},{8,9},{9,8},{10,11... | collective-permute-start | bytes 1228808 | tf_op jit(solution)/shard_map/other_core/ppermute | solution.py:72
  29.0 2.2 %collective-permute-done.6.refs_1_ = bf16[40,5120]{1,0:T(8,128)(2,1)S(1)} collective-permute-done((bf16[40,5120]{1,0:T(8,128)(2,1)S(1)}, bf16[40,5120]{1,0:T(8,128)(2,1)S(1)}, u32[]{:S(2)}, u32[]{:S(2)}) %collective-permute-start.6) | collective-permute-done | bytes 409632 | tf_op jit(solution)/shard_map/near_rows/ppermute | solution.py:49
  31.2 4.8 %collective-permute-done.5.refs_0_ = bf16[40,5120]{1,0:T(8,128)(2,1)S(1)} collective-permute-done((bf16[40,5120]{1,0:T(8,128)(2,1)S(1)}, bf16[40,5120]{1,0:T(8,128)(2,1)S(1)}, u32[]{:S(2)}, u32[]{:S(2)}) %collective-permute-start.5) | collective-permute-done | bytes 409632 | tf_op jit(solution)/shard_map/far_rows/ppermute | solution.py:49
  36.0 2.9 %shard_map.76 = (bf16[40,5120]{1,0:T(8,128)(2,1)S(1)}, bf16[40,5120]{1,0:T(8,128)(2,1)S(1)}, bf16[40,5120]{1,0:T(8,128)(2,1)S(1)}, bf16[40,5120]{1,0:T(8,128)(2,1)S(1)}) custom-call(bf16[40,5120]{1,0:T(8,128)(2,1)S(1)} %collective-permute-done.3.refs_0_, bf16[40,5120]{1,0:T(8,128)(2,1)S(1)} %collective-permute-done.6.refs_1_, ...), custom_call_target="tpu_custom_call" | custom-call | tf_op jit(solution)/shard_map/pallas_call | solution.py:233
  38.9 1.9 %collective-permute-start.12 = (bf16[40,5120]{1,0:T(8,128)(2,1)S(1)}, bf16[40,5120]{1,0:T(8,128)(2,1)S(1)}, u32[]{:S(2)}, u32[]{:S(2)}) collective-permute-start(bf16[40,5120]{1,0:T(8,128)(2,1)S(1)} %get-tuple-element.51), channel_id=1, source_target_pairs={{0,1},{1,0},{2,3},{3,2},{4,5},{5,4},{6,7},{7,6},{8,9},{9,8},{10,11... | collective-permute-start | bytes 1228808 | tf_op jit(solution)/shard_map/other_core/ppermute | solution.py:72
  41.4 3.8 %collective-permute-done.8.refs_0_ = bf16[40,5120]{1,0:T(8,128)(2,1)S(1)} collective-permute-done((bf16[40,5120]{1,0:T(8,128)(2,1)S(1)}, bf16[40,5120]{1,0:T(8,128)(2,1)S(1)}, u32[]{:S(2)}, u32[]{:S(2)}) %collective-permute-start.8) | collective-permute-done | bytes 409632 | tf_op jit(solution)/shard_map/far_rows/ppermute | solution.py:49
  46.6 2.9 %shard_map.77 = (bf16[40,5120]{1,0:T(8,128)(2,1)S(1)}, bf16[40,5120]{1,0:T(8,128)(2,1)S(1)}, bf16[40,5120]{1,0:T(8,128)(2,1)S(1)}, bf16[40,5120]{1,0:T(8,128)(2,1)S(1)}) custom-call(bf16[40,5120]{1,0:T(8,128)(2,1)S(1)} %collective-permute-done.5.refs_0_, bf16[40,5120]{1,0:T(8,128)(2,1)S(1)} %collective-permute-done.9.refs_1_, ...), custom_call_target="tpu_custom_call" | custom-call | tf_op jit(solution)/shard_map/pallas_call | solution.py:233
  50.5 2.7 %shard_map.78 = (bf16[40,5120]{1,0:T(8,128)(2,1)S(1)}, bf16[40,5120]{1,0:T(8,128)(2,1)S(1)}) custom-call(bf16[40,5120]{1,0:T(8,128)(2,1)S(1)} %collective-permute-done.8.refs_0_, bf16[40,5120]{1,0:T(8,128)(2,1)S(1)} %collective-permute-done.17.refs_1_, bf16[5120,384]{1,0:T(8,128)(2,1)S(1)} %get-tuple-element.40.refs_2_.refs_4_, ...), custom_call_target="tpu_custom_call" | custom-call | tf_op jit(solution)/shard_map/pallas_call | solution.py:233
  56.7 2.7 %shard_map.79 = (bf16[40,5120]{1,0:T(8,128)(2,1)S(1)}, bf16[40,5120]{1,0:T(8,128)(2,1)S(1)}) custom-call(bf16[40,5120]{1,0:T(8,128)(2,1)S(1)} %collective-permute-done.13.refs_0_, bf16[40,5120]{1,0:T(8,128)(2,1)S(1)} %collective-permute-done.21.refs_1_, bf16[5120,384]{1,0:T(8,128)(2,1)S(1)} %get-tuple-element.40.refs_2_.refs_4_, ...), custom_call_target="tpu_custom_call" | custom-call | tf_op jit(solution)/shard_map/pallas_call | solution.py:233
  62.3 2.7 %shard_map.80 = (bf16[40,5120]{1,0:T(8,128)(2,1)S(1)}, bf16[40,5120]{1,0:T(8,128)(2,1)S(1)}) custom-call(bf16[40,5120]{1,0:T(8,128)(2,1)S(1)} %collective-permute-done.14.refs_0_, bf16[40,5120]{1,0:T(8,128)(2,1)S(1)} %collective-permute-done.24.refs_1_, bf16[5120,384]{1,0:T(8,128)(2,1)S(1)} %get-tuple-element.40.refs_2_.refs_4_, ...), custom_call_target="tpu_custom_call" | custom-call | tf_op jit(solution)/shard_map/pallas_call | solution.py:233
  66.8 3.7 %collective-permute-done.23 = bf16[40,5120]{1,0:T(8,128)(2,1)S(1)} collective-permute-done((bf16[40,5120]{1,0:T(8,128)(2,1)S(1)}, bf16[40,5120]{1,0:T(8,128)(2,1)S(1)}, u32[]{:S(2)}, u32[]{:S(2)}) %collective-permute-start.23) | collective-permute-done | bytes 409632 | tf_op jit(solution)/shard_map/far_sum/ppermute | solution.py:49
  70.7 4.1 %collective-permute-done.29 = bf16[40,5120]{1,0:T(8,128)(2,1)S(1)} collective-permute-done((bf16[40,5120]{1,0:T(8,128)(2,1)S(1)}, bf16[40,5120]{1,0:T(8,128)(2,1)S(1)}, u32[]{:S(2)}, u32[]{:S(2)}) %collective-permute-start.29) | collective-permute-done | bytes 409632 | tf_op jit(solution)/shard_map/near_sum/ppermute | solution.py:49
  75.1 4.8 %collective-permute-done.26 = bf16[40,5120]{1,0:T(8,128)(2,1)S(1)} collective-permute-done((bf16[40,5120]{1,0:T(8,128)(2,1)S(1)}, bf16[40,5120]{1,0:T(8,128)(2,1)S(1)}, u32[]{:S(2)}, u32[]{:S(2)}) %collective-permute-start.26) | collective-permute-done | bytes 409632 | tf_op jit(solution)/shard_map/far_sum/ppermute | solution.py:49
  80.1 4.1 %collective-permute-done.30 = bf16[40,5120]{1,0:T(8,128)(2,1)S(1)} collective-permute-done((bf16[40,5120]{1,0:T(8,128)(2,1)S(1)}, bf16[40,5120]{1,0:T(8,128)(2,1)S(1)}, u32[]{:S(2)}, u32[]{:S(2)}) %collective-permute-start.30) | collective-permute-done | bytes 409632 | tf_op jit(solution)/shard_map/near_sum/ppermute | solution.py:49
  84.5 4.8 %collective-permute-done.27 = bf16[40,5120]{1,0:T(8,128)(2,1)S(1)} collective-permute-done((bf16[40,5120]{1,0:T(8,128)(2,1)S(1)}, bf16[40,5120]{1,0:T(8,128)(2,1)S(1)}, u32[]{:S(2)}, u32[]{:S(2)}) %collective-permute-start.27) | collective-permute-done | bytes 409632 | tf_op jit(solution)/shard_map/far_sum/ppermute | solution.py:49
  89.5 2.4 %collective-permute-done.32 = bf16[40,5120]{1,0:T(8,128)(2,1)S(1)} collective-permute-done((bf16[40,5120]{1,0:T(8,128)(2,1)S(1)}, bf16[40,5120]{1,0:T(8,128)(2,1)S(1)}, u32[]{:S(2)}, u32[]{:S(2)}) %collective-permute-start.32) | collective-permute-done | bytes 409632 | tf_op jit(solution)/shard_map/near_sum/ppermute | solution.py:56
  91.9 6.8 %collective-permute-done.28 = bf16[40,5120]{1,0:T(8,128)(2,1)S(1)} collective-permute-done((bf16[40,5120]{1,0:T(8,128)(2,1)S(1)}, bf16[40,5120]{1,0:T(8,128)(2,1)S(1)}, u32[]{:S(2)}, u32[]{:S(2)}) %collective-permute-start.28) | collective-permute-done | bytes 409632 | tf_op jit(solution)/shard_map/far_sum/ppermute | solution.py:49
  99.0 2.7 %collective-permute-start.35 = (bf16[10,5120]{1,0:T(8,128)(2,1)S(1)}, bf16[10,5120]{1,0:T(8,128)(2,1)S(1)}, u32[]{:S(2)}, u32[]{:S(2)}) collective-permute-start(bf16[10,5120]{1,0:T(8,128)(2,1)S(1)} %get-tuple-element.72), channel_id=1, source_target_pairs={{0,64},{64,128},{128,192},{192,0},{1,65},{65,129},{129,193},{193,1... | collective-permute-start | bytes 307208 | tf_op jit(solution)/shard_map/ppermute | solution.py:42
  102.7 3.9 %collective-permute-done.35 = bf16[10,5120]{1,0:T(8,128)(2,1)S(1)} collective-permute-done((bf16[10,5120]{1,0:T(8,128)(2,1)S(1)}, bf16[10,5120]{1,0:T(8,128)(2,1)S(1)}, u32[]{:S(2)}, u32[]{:S(2)}) %collective-permute-start.35) | collective-permute-done | bytes 102432 | tf_op jit(solution)/shard_map/ppermute | solution.py:42
  106.6 2.1 %collective-permute-done.34 = bf16[10,5120]{1,0:T(8,128)(2,1)S(1)} collective-permute-done((bf16[10,5120]{1,0:T(8,128)(2,1)S(1)}, bf16[10,5120]{1,0:T(8,128)(2,1)S(1)}, u32[]{:S(2)}, u32[]{:S(2)}) %collective-permute-start.34) | collective-permute-done | bytes 102432 | tf_op jit(solution)/shard_map/ppermute | solution.py:42
  113.8 5.9 %collective-permute-done.39.refs_3_ = bf16[40,5120]{1,0:T(8,128)(2,1)S(1)} collective-permute-done((bf16[40,5120]{1,0:T(8,128)(2,1)S(1)}, bf16[40,5120]{1,0:T(8,128)(2,1)S(1)}, u32[]{:S(2)}, u32[]{:S(2)}) %collective-permute-start.39) | collective-permute-done | bytes 409632 | tf_op jit(solution)/shard_map/ppermute | solution.py:66
  120.1 4.0 %collective-permute-done.37 = bf16[40,5120]{1,0:T(8,128)(2,1)S(1)} collective-permute-done((bf16[40,5120]{1,0:T(8,128)(2,1)S(1)}, bf16[40,5120]{1,0:T(8,128)(2,1)S(1)}, u32[]{:S(2)}, u32[]{:S(2)}) %collective-permute-start.37) | collective-permute-done | bytes 409632 | tf_op jit(solution)/shard_map/ppermute | solution.py:66
  124.1 4.8 %collective-permute-done.40.refs_2_ = bf16[40,5120]{1,0:T(8,128)(2,1)S(1)} collective-permute-done((bf16[40,5120]{1,0:T(8,128)(2,1)S(1)}, bf16[40,5120]{1,0:T(8,128)(2,1)S(1)}, u32[]{:S(2)}, u32[]{:S(2)}) %collective-permute-start.40) | collective-permute-done | bytes 409632 | tf_op jit(solution)/shard_map/ppermute | solution.py:66
  (72 shorter events, 22.9 us)
Async XLA Ops:
  3.3 10.7 %collective-permute-start.2 = (bf16[10,5120]{1,0:T(8,128)(2,1)S(1)}, bf16[10,5120]{1,0:T(8,128)(2,1)S(1)}, u32[]{:S(2)}, u32[]{:S(2)}) collective-permute-start(bf16[10,5120]{1,0:T(8,128)(2,1)S(1)} %get-tuple-element.76), channel_id=1, source_target_pairs={{0,192},{64,0},{128,64},{192,128},{1,193},{65,1},{129,65},{193,129... | collective-permute-start | bytes 307208 | tf_op jit(solution)/shard_map/ppermute | solution.py:42
  4.2 9.8 %collective-permute-start.1 = (bf16[10,5120]{1,0:T(8,128)(2,1)S(1)}, bf16[10,5120]{1,0:T(8,128)(2,1)S(1)}, u32[]{:S(2)}, u32[]{:S(2)}) collective-permute-start(bf16[10,5120]{1,0:T(8,128)(2,1)S(1)} %get-tuple-element.77), channel_id=1, source_target_pairs={{0,128},{64,192},{128,0},{192,64},{1,129},{65,193},{129,1},{193,65... | collective-permute-start | bytes 307208 | tf_op jit(solution)/shard_map/ppermute | solution.py:42
  7.1 7.6 %collective-permute-start = (bf16[10,5120]{1,0:T(8,128)(2,1)S(1)}, bf16[10,5120]{1,0:T(8,128)(2,1)S(1)}, u32[]{:S(2)}, u32[]{:S(2)}) collective-permute-start(bf16[10,5120]{1,0:T(8,128)(2,1)S(1)} %get-tuple-element.78), channel_id=1, source_target_pairs={{0,64},{64,128},{128,192},{192,0},{1,65},{65,129},{129,193},{193,1... | collective-permute-start | bytes 307208 | tf_op jit(solution)/shard_map/ppermute | solution.py:42
  14.9 11.9 %collective-permute-start.3 = (bf16[40,5120]{1,0:T(8,128)(2,1)S(1)}, bf16[40,5120]{1,0:T(8,128)(2,1)S(1)}, u32[]{:S(2)}, u32[]{:S(2)}) collective-permute-start(bf16[40,5120]{1,0:T(8,128)(2,1)S(1)} %pad_maximum_fusion.refs_0_), channel_id=1, source_target_pairs={{0,2},{1,15},{2,4},{3,1},{4,6},{5,3},{6,8},{7,5},{8,10},{9,7},{10,... | collective-permute-start | bytes 1228808 | tf_op jit(solution)/shard_map/far_rows/ppermute | solution.py:49
  16.9 14.3 %collective-permute-start.6 = (bf16[40,5120]{1,0:T(8,128)(2,1)S(1)}, bf16[40,5120]{1,0:T(8,128)(2,1)S(1)}, u32[]{:S(2)}, u32[]{:S(2)}) collective-permute-start(bf16[40,5120]{1,0:T(8,128)(2,1)S(1)} %collective-permute-done.4.refs_1_), channel_id=1, source_target_pairs={{0,2},{1,15},{2,4},{3,1},{4,6},{5,3},{6,8},{7,5},{8,10},{9,7},{10,... | collective-permute-start | bytes 1228808 | tf_op jit(solution)/shard_map/near_rows/ppermute | solution.py:49
  21.5 9.7 %collective-permute-start.7 = (bf16[40,5120]{1,0:T(8,128)(2,1)S(1)}, bf16[40,5120]{1,0:T(8,128)(2,1)S(1)}, u32[]{:S(2)}, u32[]{:S(2)}) collective-permute-start(bf16[40,5120]{1,0:T(8,128)(2,1)S(1)} %get-tuple-element.46), channel_id=1, source_target_pairs={{0,1},{1,0},{2,3},{3,2},{4,5},{5,4},{6,7},{7,6},{8,9},{9,8},{10,11... | collective-permute-start | bytes 1228808 | tf_op jit(solution)/shard_map/other_core/ppermute | solution.py:72
  26.8 9.2 %collective-permute-start.5 = (bf16[40,5120]{1,0:T(8,128)(2,1)S(1)}, bf16[40,5120]{1,0:T(8,128)(2,1)S(1)}, u32[]{:S(2)}, u32[]{:S(2)}) collective-permute-start(bf16[40,5120]{1,0:T(8,128)(2,1)S(1)} %collective-permute-done.3.refs_0_), channel_id=1, source_target_pairs={{0,2},{1,15},{2,4},{3,1},{4,6},{5,3},{6,8},{7,5},{8,10},{9,7},{10,... | collective-permute-start | bytes 1228808 | tf_op jit(solution)/shard_map/far_rows/ppermute | solution.py:49
  26.8 9.2 %collective-permute-start.10 = (bf16[40,5120]{1,0:T(8,128)(2,1)S(1)}, bf16[40,5120]{1,0:T(8,128)(2,1)S(1)}, u32[]{:S(2)}, u32[]{:S(2)}) collective-permute-start(bf16[40,5120]{1,0:T(8,128)(2,1)S(1)} %collective-permute-done.3.refs_0_), channel_id=1, source_target_pairs={{0,1},{1,0},{2,3},{3,2},{4,5},{5,4},{6,7},{7,6},{8,9},{9,8},{10,11... | collective-permute-start | bytes 1228808 | tf_op jit(solution)/shard_map/other_core/ppermute | solution.py:72
  31.2 4.8 %collective-permute-start.11 = (bf16[40,5120]{1,0:T(8,128)(2,1)S(1)}, bf16[40,5120]{1,0:T(8,128)(2,1)S(1)}, u32[]{:S(2)}, u32[]{:S(2)}) collective-permute-start(bf16[40,5120]{1,0:T(8,128)(2,1)S(1)} %collective-permute-done.6.refs_1_), channel_id=1, source_target_pairs={{0,1},{1,0},{2,3},{3,2},{4,5},{5,4},{6,7},{7,6},{8,9},{9,8},{10,11... | collective-permute-start | bytes 1228808 | tf_op jit(solution)/shard_map/other_core/ppermute | solution.py:72
  31.2 9.9 %collective-permute-start.9 = (bf16[40,5120]{1,0:T(8,128)(2,1)S(1)}, bf16[40,5120]{1,0:T(8,128)(2,1)S(1)}, u32[]{:S(2)}, u32[]{:S(2)}) collective-permute-start(bf16[40,5120]{1,0:T(8,128)(2,1)S(1)} %collective-permute-done.6.refs_1_), channel_id=1, source_target_pairs={{0,2},{1,15},{2,4},{3,1},{4,6},{5,3},{6,8},{7,5},{8,10},{9,7},{10,... | collective-permute-start | bytes 1228808 | tf_op jit(solution)/shard_map/near_rows/ppermute | solution.py:49
  36.0 9.2 %collective-permute-start.8 = (bf16[40,5120]{1,0:T(8,128)(2,1)S(1)}, bf16[40,5120]{1,0:T(8,128)(2,1)S(1)}, u32[]{:S(2)}, u32[]{:S(2)}) collective-permute-start(bf16[40,5120]{1,0:T(8,128)(2,1)S(1)} %collective-permute-done.5.refs_0_), channel_id=1, source_target_pairs={{0,2},{1,15},{2,4},{3,1},{4,6},{5,3},{6,8},{7,5},{8,10},{9,7},{10,... | collective-permute-start | bytes 1228808 | tf_op jit(solution)/shard_map/far_rows/ppermute | solution.py:49
  38.9 6.2 %collective-permute-start.12 = (bf16[40,5120]{1,0:T(8,128)(2,1)S(1)}, bf16[40,5120]{1,0:T(8,128)(2,1)S(1)}, u32[]{:S(2)}, u32[]{:S(2)}) collective-permute-start(bf16[40,5120]{1,0:T(8,128)(2,1)S(1)} %get-tuple-element.51), channel_id=1, source_target_pairs={{0,1},{1,0},{2,3},{3,2},{4,5},{5,4},{6,7},{7,6},{8,9},{9,8},{10,11... | collective-permute-start | bytes 1228808 | tf_op jit(solution)/shard_map/other_core/ppermute | solution.py:72
  40.8 5.8 %collective-permute-start.15 = (bf16[40,5120]{1,0:T(8,128)(2,1)S(1)}, bf16[40,5120]{1,0:T(8,128)(2,1)S(1)}, u32[]{:S(2)}, u32[]{:S(2)}) collective-permute-start(bf16[40,5120]{1,0:T(8,128)(2,1)S(1)} %collective-permute-done.5.refs_0_), channel_id=1, source_target_pairs={{0,1},{1,0},{2,3},{3,2},{4,5},{5,4},{6,7},{7,6},{8,9},{9,8},{10,11... | collective-permute-start | bytes 1228808 | tf_op jit(solution)/shard_map/other_core/ppermute | solution.py:72
  41.1 5.5 %collective-permute-start.16 = (bf16[40,5120]{1,0:T(8,128)(2,1)S(1)}, bf16[40,5120]{1,0:T(8,128)(2,1)S(1)}, u32[]{:S(2)}, u32[]{:S(2)}) collective-permute-start(bf16[40,5120]{1,0:T(8,128)(2,1)S(1)} %collective-permute-done.9.refs_1_), channel_id=1, source_target_pairs={{0,1},{1,0},{2,3},{3,2},{4,5},{5,4},{6,7},{7,6},{8,9},{9,8},{10,11... | collective-permute-start | bytes 1228808 | tf_op jit(solution)/shard_map/other_core/ppermute | solution.py:72
  41.4 9.2 %collective-permute-start.14 = (bf16[40,5120]{1,0:T(8,128)(2,1)S(1)}, bf16[40,5120]{1,0:T(8,128)(2,1)S(1)}, u32[]{:S(2)}, u32[]{:S(2)}) collective-permute-start(bf16[40,5120]{1,0:T(8,128)(2,1)S(1)} %collective-permute-done.9.refs_1_), channel_id=1, source_target_pairs={{0,2},{1,15},{2,4},{3,1},{4,6},{5,3},{6,8},{7,5},{8,10},{9,7},{10,... | collective-permute-start | bytes 1228808 | tf_op jit(solution)/shard_map/near_rows/ppermute | solution.py:49
  45.1 9.8 %collective-permute-start.13 = (bf16[40,5120]{1,0:T(8,128)(2,1)S(1)}, bf16[40,5120]{1,0:T(8,128)(2,1)S(1)}, u32[]{:S(2)}, u32[]{:S(2)}) collective-permute-start(bf16[40,5120]{1,0:T(8,128)(2,1)S(1)} %collective-permute-done.8.refs_0_), channel_id=1, source_target_pairs={{0,2},{1,15},{2,4},{3,1},{4,6},{5,3},{6,8},{7,5},{8,10},{9,7},{10,... | collective-permute-start | bytes 1228808 | tf_op jit(solution)/shard_map/far_rows/ppermute | solution.py:49
  45.1 5.4 %collective-permute-start.17 = (bf16[40,5120]{1,0:T(8,128)(2,1)S(1)}, bf16[40,5120]{1,0:T(8,128)(2,1)S(1)}, u32[]{:S(2)}, u32[]{:S(2)}) collective-permute-start(bf16[40,5120]{1,0:T(8,128)(2,1)S(1)} %collective-permute-done.8.refs_0_), channel_id=1, source_target_pairs={{0,1},{1,0},{2,3},{3,2},{4,5},{5,4},{6,7},{7,6},{8,9},{9,8},{10,11... | collective-permute-start | bytes 1228808 | tf_op jit(solution)/shard_map/other_core/ppermute | solution.py:72
  49.6 5.3 %collective-permute-start.18 = (bf16[40,5120]{1,0:T(8,128)(2,1)S(1)}, bf16[40,5120]{1,0:T(8,128)(2,1)S(1)}, u32[]{:S(2)}, u32[]{:S(2)}) collective-permute-start(bf16[40,5120]{1,0:T(8,128)(2,1)S(1)} %get-tuple-element.53), channel_id=1, source_target_pairs={{0,1},{1,0},{2,3},{3,2},{4,5},{5,4},{6,7},{7,6},{8,9},{9,8},{10,11... | collective-permute-start | bytes 1228808 | tf_op jit(solution)/shard_map/other_core/ppermute | solution.py:72
  59.5 20.6 %collective-permute-start.31 = (bf16[40,5120]{1,0:T(8,128)(2,1)S(1)}, bf16[40,5120]{1,0:T(8,128)(2,1)S(1)}, u32[]{:S(2)}, u32[]{:S(2)}) collective-permute-start(bf16[40,5120]{1,0:T(8,128)(2,1)S(1)} %get-tuple-element.48), channel_id=1, source_target_pairs={{0,1},{1,0},{2,3},{3,2},{4,5},{5,4},{6,7},{7,6},{8,9},{9,8},{10,11... | collective-permute-start | bytes 1228808 | tf_op jit(solution)/shard_map/other_core/ppermute | solution.py:72
  61.2 9.2 %collective-permute-start.23 = (bf16[40,5120]{1,0:T(8,128)(2,1)S(1)}, bf16[40,5120]{1,0:T(8,128)(2,1)S(1)}, u32[]{:S(2)}, u32[]{:S(2)}) collective-permute-start(bf16[40,5120]{1,0:T(8,128)(2,1)S(1)} %add_convert_fusion.7), channel_id=1, source_target_pairs={{0,2},{1,15},{2,4},{3,1},{4,6},{5,3},{6,8},{7,5},{8,10},{9,7},{10,... | collective-permute-start | bytes 1228808 | tf_op jit(solution)/shard_map/far_sum/ppermute | solution.py:49
  65.3 9.6 %collective-permute-start.29 = (bf16[40,5120]{1,0:T(8,128)(2,1)S(1)}, bf16[40,5120]{1,0:T(8,128)(2,1)S(1)}, u32[]{:S(2)}, u32[]{:S(2)}) collective-permute-start(bf16[40,5120]{1,0:T(8,128)(2,1)S(1)} %add_convert_fusion.3), channel_id=1, source_target_pairs={{0,2},{1,15},{2,4},{3,1},{4,6},{5,3},{6,8},{7,5},{8,10},{9,7},{10,... | collective-permute-start | bytes 1228808 | tf_op jit(solution)/shard_map/near_sum/ppermute | solution.py:49
  70.6 9.2 %collective-permute-start.26 = (bf16[40,5120]{1,0:T(8,128)(2,1)S(1)}, bf16[40,5120]{1,0:T(8,128)(2,1)S(1)}, u32[]{:S(2)}, u32[]{:S(2)}) collective-permute-start(bf16[40,5120]{1,0:T(8,128)(2,1)S(1)} %add_convert_fusion.6), channel_id=1, source_target_pairs={{0,2},{1,15},{2,4},{3,1},{4,6},{5,3},{6,8},{7,5},{8,10},{9,7},{10,... | collective-permute-start | bytes 1228808 | tf_op jit(solution)/shard_map/far_sum/ppermute | solution.py:49
  75.0 9.2 %collective-permute-start.30 = (bf16[40,5120]{1,0:T(8,128)(2,1)S(1)}, bf16[40,5120]{1,0:T(8,128)(2,1)S(1)}, u32[]{:S(2)}, u32[]{:S(2)}) collective-permute-start(bf16[40,5120]{1,0:T(8,128)(2,1)S(1)} %add_convert_fusion.2), channel_id=1, source_target_pairs={{0,2},{1,15},{2,4},{3,1},{4,6},{5,3},{6,8},{7,5},{8,10},{9,7},{10,... | collective-permute-start | bytes 1228808 | tf_op jit(solution)/shard_map/near_sum/ppermute | solution.py:49
  80.0 9.2 %collective-permute-start.27 = (bf16[40,5120]{1,0:T(8,128)(2,1)S(1)}, bf16[40,5120]{1,0:T(8,128)(2,1)S(1)}, u32[]{:S(2)}, u32[]{:S(2)}) collective-permute-start(bf16[40,5120]{1,0:T(8,128)(2,1)S(1)} %add_convert_fusion.5), channel_id=1, source_target_pairs={{0,2},{1,15},{2,4},{3,1},{4,6},{5,3},{6,8},{7,5},{8,10},{9,7},{10,... | collective-permute-start | bytes 1228808 | tf_op jit(solution)/shard_map/far_sum/ppermute | solution.py:49
  84.4 7.5 %collective-permute-start.32 = (bf16[40,5120]{1,0:T(8,128)(2,1)S(1)}, bf16[40,5120]{1,0:T(8,128)(2,1)S(1)}, u32[]{:S(2)}, u32[]{:S(2)}) collective-permute-start(bf16[40,5120]{1,0:T(8,128)(2,1)S(1)} %add_convert_fusion.1), channel_id=1, source_target_pairs={{0,3},{1,14},{2,5},{3,0},{4,7},{5,2},{6,9},{7,4},{8,11},{9,6},{10,... | collective-permute-start | bytes 1228808 | tf_op jit(solution)/shard_map/near_sum/ppermute | solution.py:56
  89.4 9.2 %collective-permute-start.28 = (bf16[40,5120]{1,0:T(8,128)(2,1)S(1)}, bf16[40,5120]{1,0:T(8,128)(2,1)S(1)}, u32[]{:S(2)}, u32[]{:S(2)}) collective-permute-start(bf16[40,5120]{1,0:T(8,128)(2,1)S(1)} %add_convert_fusion.4), channel_id=1, source_target_pairs={{0,2},{1,15},{2,4},{3,1},{4,6},{5,3},{6,8},{7,5},{8,10},{9,7},{10,... | collective-permute-start | bytes 1228808 | tf_op jit(solution)/shard_map/far_sum/ppermute | solution.py:49
  99.0 7.6 %collective-permute-start.35 = (bf16[10,5120]{1,0:T(8,128)(2,1)S(1)}, bf16[10,5120]{1,0:T(8,128)(2,1)S(1)}, u32[]{:S(2)}, u32[]{:S(2)}) collective-permute-start(bf16[10,5120]{1,0:T(8,128)(2,1)S(1)} %get-tuple-element.72), channel_id=1, source_target_pairs={{0,64},{64,128},{128,192},{192,0},{1,65},{65,129},{129,193},{193,1... | collective-permute-start | bytes 307208 | tf_op jit(solution)/shard_map/ppermute | solution.py:42
  101.7 7.0 %collective-permute-start.34 = (bf16[10,5120]{1,0:T(8,128)(2,1)S(1)}, bf16[10,5120]{1,0:T(8,128)(2,1)S(1)}, u32[]{:S(2)}, u32[]{:S(2)}) collective-permute-start(bf16[10,5120]{1,0:T(8,128)(2,1)S(1)} %get-tuple-element.73), channel_id=1, source_target_pairs={{0,128},{64,192},{128,0},{192,64},{1,129},{65,193},{129,1},{193,65... | collective-permute-start | bytes 307208 | tf_op jit(solution)/shard_map/ppermute | solution.py:42
  101.9 8.3 %collective-permute-start.33 = (bf16[10,5120]{1,0:T(8,128)(2,1)S(1)}, bf16[10,5120]{1,0:T(8,128)(2,1)S(1)}, u32[]{:S(2)}, u32[]{:S(2)}) collective-permute-start(bf16[10,5120]{1,0:T(8,128)(2,1)S(1)} %get-tuple-element.74), channel_id=1, source_target_pairs={{0,192},{64,0},{128,64},{192,128},{1,193},{65,1},{129,65},{193,129... | collective-permute-start | bytes 307208 | tf_op jit(solution)/shard_map/ppermute | solution.py:42
  110.5 9.2 %collective-permute-start.39 = (bf16[40,5120]{1,0:T(8,128)(2,1)S(1)}, bf16[40,5120]{1,0:T(8,128)(2,1)S(1)}, u32[]{:S(2)}, u32[]{:S(2)}) collective-permute-start(bf16[40,5120]{1,0:T(8,128)(2,1)S(1)} %pad_maximum_fusion.1.refs_0_), channel_id=1, source_target_pairs={{0,16},{1,49},{2,18},{3,51},{4,20},{5,53},{6,22},{7,55},{8,24},{9,... | collective-permute-start | bytes 1228808 | tf_op jit(solution)/shard_map/ppermute | solution.py:66
  112.2 11.9 %collective-permute-start.37 = (bf16[40,5120]{1,0:T(8,128)(2,1)S(1)}, bf16[40,5120]{1,0:T(8,128)(2,1)S(1)}, u32[]{:S(2)}, u32[]{:S(2)}) collective-permute-start(bf16[40,5120]{1,0:T(8,128)(2,1)S(1)} %collective-permute-done.36), channel_id=1, source_target_pairs={{0,16},{1,49},{2,18},{3,51},{4,20},{5,53},{6,22},{7,55},{8,24},{9,... | collective-permute-start | bytes 1228808 | tf_op jit(solution)/shard_map/ppermute | solution.py:66
  119.7 9.2 %collective-permute-start.40 = (bf16[40,5120]{1,0:T(8,128)(2,1)S(1)}, bf16[40,5120]{1,0:T(8,128)(2,1)S(1)}, u32[]{:S(2)}, u32[]{:S(2)}) collective-permute-start(bf16[40,5120]{1,0:T(8,128)(2,1)S(1)} %collective-permute-done.39.refs_3_), channel_id=1, source_target_pairs={{0,16},{1,49},{2,18},{3,51},{4,20},{5,53},{6,22},{7,55},{8,24},{9,... | collective-permute-start | bytes 1228808 | tf_op jit(solution)/shard_map/ppermute | solution.py:66
  (9 other events, 22.1 us)
